TPU v7x, 32 devices: a whole 2x2x4 slice. The times are simulated.
32 devices in a mesh: node: 4 (over z), local: 4 (over y, x), cuts: 2 (over core).
Axes of the slice: x: 2, y: 2, z: 4, core: 2. Of those that a mesh axis runs over, the one named last changes fastest.
Arguments:
- tokens: bfloat16 [384, 3584], P('node', 'cuts'), may hold values from -6 to 6
- expert_ids: int32 [384, 8], P('node'), may hold values from 0 to 7, as said below
- affinity: float32 [384, 8], P('node'), may hold values from 0.1 to 1
- w_gate: bfloat16 [16, 3584, 512], P(('node', 'local'), 'cuts'), may hold values from -0.09375 to 0.09375
- w_up: bfloat16 [16, 3584, 512], P(('node', 'local'), 'cuts'), may hold values from -0.09375 to 0.09375
- w_down: bfloat16 [16, 512, 3584], P(('node', 'local'), None, 'cuts'), may hold values from -0.1875 to 0.1875
Outputs:
- moe_out: bfloat16 [384, 3584], P(('node', 'local'), 'cuts')
Inputs may be any that keep to these rules, and one draw needn't show every extreme that they name: `expert_ids`: each row names both experts 2m and 2m + 1 of each of 4 different nodes m, in some order.
All inputs are finite; a program needn't handle non-finite values.
Results may differ from a plain program's by a relative error of at most 0.009.
Values may be sent and summed in bfloat16 or wider, within the bound.
No kernel may reach another device: no remote copies, remote signals or barrier semaphores. Data moves between devices by JAX's collectives and lax.ppermute only.
A program may use at most 64 MiB of HBM per device.

v0:
```python
import jax
import jax.numpy as jnp
from jax import lax
from jax.sharding import PartitionSpec as P


def on_device(tokens, expert_ids, affinity, w_gate, w_up, w_down):
    node_count = lax.axis_size("node")
    local_count = lax.axis_size("local")
    group_size = local_count // 2
    expert_count = 2 * node_count
    tok_count, top_count = expert_ids.shape
    capacity = (5 * tok_count * top_count + 4 * expert_count - 1) // (4 * expert_count)
    half_width = tokens.shape[1]
    my_local = lax.axis_index("local")
    pair_index = my_local // group_size
    node_range = jnp.arange(node_count, dtype=jnp.int32)
    chosen_node = jnp.any(
        (expert_ids // 2)[:, :, None] == node_range[None, None, :], axis=1
    ).astype(jnp.float32)
    tok_range = jnp.arange(tok_count, dtype=jnp.int32)
    earlier = (tok_range[None, :] < tok_range[:, None]).astype(jnp.float32)
    node_rank = jnp.dot(earlier, chosen_node, precision=lax.Precision.HIGHEST)
    slot_range = jnp.arange(capacity, dtype=jnp.float32)
    dispatch = chosen_node[:, :, None] * (
        node_rank[:, :, None] == slot_range[None, None, :]
    ).astype(jnp.float32)
    outgoing = jnp.einsum(
        "tmc,td->mcd", dispatch.astype(jnp.bfloat16), tokens, preferred_element_type=jnp.float32
    ).astype(jnp.bfloat16)
    affinity_sum = jnp.sum(affinity, axis=1, keepdims=True)
    route_share = (2.5 * affinity / affinity_sum).astype(jnp.bfloat16).astype(jnp.float32)
    pair_range = jnp.arange(2, dtype=jnp.int32)
    expert_grid = 2 * node_range[:, None] + pair_range[None, :]
    own_route = expert_ids[:, :, None, None] == expert_grid[None, None, :, :]
    pair_weight = jnp.sum(jnp.where(own_route, route_share[:, :, None, None], 0.0), axis=1)
    slot_weight = jnp.einsum(
        "tmc,tmp->mcp", dispatch, pair_weight, precision=lax.Precision.HIGHEST
    ).astype(jnp.bfloat16)
    arrived, arrived_weight = (
        lax.all_to_all(outgoing, "node", split_axis=0, concat_axis=0, tiled=True),
        lax.all_to_all(slot_weight, "node", split_axis=0, concat_axis=0, tiled=True),
    )
    expert_rows = arrived.reshape(node_count * capacity, half_width)
    gate_part = jnp.dot(expert_rows, w_gate[0], preferred_element_type=jnp.float32)
    up_part = jnp.dot(expert_rows, w_up[0], preferred_element_type=jnp.float32)
    gate_full, up_full = lax.psum((gate_part, up_part), "cuts")
    hidden = (jax.nn.silu(gate_full) * up_full).astype(jnp.bfloat16)
    slice_out = jnp.dot(hidden, w_down[0], preferred_element_type=jnp.float32)
    pick = (pair_range == pair_index).astype(jnp.float32)
    slot_scale = jnp.sum(arrived_weight.astype(jnp.float32) * pick[None, None, :], axis=2).reshape(
        node_count * capacity
    )
    weighted = (slice_out * slot_scale[:, None]).reshape(node_count, capacity, half_width)
    grouped = lax.psum_scatter(weighted, "local", scatter_dimension=2, tiled=True)
    returned = lax.all_to_all(grouped, "node", split_axis=0, concat_axis=0, tiled=True)
    partial_value = jnp.einsum("tmc,mcd->td", dispatch, returned, precision=lax.Precision.HIGHEST)
    summed = lax.all_to_all(partial_value, "local", split_axis=0, concat_axis=1, tiled=True)
    return summed.astype(jnp.bfloat16)


def solution(mesh):
    return jax.shard_map(
        on_device,
        mesh=mesh,
        in_specs=(
            P("node", "cuts"),
            P("node", None),
            P("node", None),
            P(("node", "local"), "cuts", None),
            P(("node", "local"), "cuts", None),
            P(("node", "local"), None, "cuts"),
        ),
        out_specs=P(("node", "local"), "cuts"),
        check_vma=False,
    )
```

profile of v0, /device:TPU:0, one launch (start us, length us, event | category | flops | bytes accessed | tf_op | source)
XLA Modules:
  0.0 183.0 jit_solution(11079640018803634916)
XLA Ops:
  6.5 0.0 copy-start
  6.5 0.0 all-reduce.3.cloned.1.call-start
  6.5 0.8 add_select_fusion
  7.4 0.1 fusion.19
  7.5 1.7 convolution_convert_fusion
  9.3 0.0 copy-start.3
  9.3 46.4 %all_to_all.28 = bf16[4,120,1792]{2,1,0:T(8,128)(2,1)S(1)} all-to-all(bf16[4,120,1792]{2,1,0:T(8,128)(2,1)S(1)} %convolution_convert_fusion), channel_id=1, replica_groups=mesh['node'=4,'local'=4,'cuts'=2] {'node'}, dimensions={0} | all-to-all | bytes 3440640 | tf_op jit(solution)/shard_map/all_to_all | solution.py:41
  55.7 0.0 copy-done.3
  55.7 2.0 %fusion.1 = f32[480,512]{1,0:T(8,128)} fusion(bf16[480,1792]{1,0:T(8,128)(2,1)S(1)} %bitcast.26, bf16[1,1792,512]{2,1,0:T(8,128)(2,1)S(1)} %copy-done.3), kind=kOutput, calls=%fused_computation.3 | convolution fusion | flops 880803840 | bytes 4538368 | tf_op jit(solution)/shard_map/dot_general | solution.py:46
  57.7 0.0 copy-done.4
  57.7 2.0 %fusion.3 = f32[480,512]{1,0:T(8,128)} fusion(bf16[480,1792]{1,0:T(8,128)(2,1)S(1)} %bitcast.27, bf16[1,1792,512]{2,1,0:T(8,128)(2,1)S(1)} %copy-done.4), kind=kOutput, calls=%fused_computation.5 | convolution fusion | flops 880803840 | bytes 4538368 | tf_op jit(solution)/shard_map/dot_general | solution.py:45
  59.7 0.0 all-reduce.3.cloned.1.call-update
  59.7 0.7 copy-done.2
  60.4 0.1 iota_add_fusion
  60.5 0.1 select_reduce_fusion
  60.6 1.0 convolution_convert_fusion.1
  61.6 3.2 %all-to-all-start.1 = ((bf16[4,120,2]{1,2,0:T(2,128)(2,1)}), bf16[4,120,2]{1,2,0:T(2,128)(2,1)S(1)}, u32[]{:S(2)}, u32[]{:S(2)}) async-start(bf16[4,120,2]{1,2,0:T(2,128)(2,1)} %convolution_convert_fusion.1), calls=%async_computation.1 | async-start | bytes 4096 | tf_op jit(solution)/shard_map/all_to_all | solution.py:42
  64.8 0.0 reduce-scatter.2.cloned.1.call-start
  64.9 5.4 %all-to-all-done.1 = bf16[4,120,2]{1,2,0:T(2,128)(2,1)S(1)} async-done(((bf16[4,120,2]{1,2,0:T(2,128)(2,1)}), bf16[4,120,2]{1,2,0:T(2,128)(2,1)S(1)}, u32[]{:S(2)}, u32[]{:S(2)}) %all-to-all-start.1) | async-done | bytes 1952 | tf_op jit(solution)/shard_map/all_to_all | solution.py:42
  70.3 0.1 multiply_reduce_fusion
  70.3 0.1 mul.56
  70.4 9.7 %all-reduce.3.cloned.1.call-done = (f32[480,512]{1,0:T(8,128)}, f32[480,512]{1,0:T(8,128)}) async-done(((f32[480,512]{1,0:T(8,128)}, f32[480,512]{1,0:T(8,128)}), (f32[480,512]{1,0:T(8,128)}, f32[480,512]{1,0:T(8,128)})) %all-reduce.3.cloned.1.call-update) | async-done | bytes 1966096 | tf_op jit(solution)/shard_map/psum | solution.py:47
  80.1 0.0 copy-done
  80.1 4.5 %convolution_multiply_fusion = f32[480,1792]{1,0:T(8,128)} fusion(bf16[1,512,1792]{2,1,0:T(8,128)(2,1)S(1)} %copy-done, f32[480]{0:T(512)S(1)} %mul.56, f32[480,512]{1,0:T(8,128)} %get-tuple-element.5, f32[480,512]{1,0:T(8,128)} %get-tuple-element.6), kind=kOutput, calls=%fused_computation | convolution fusion | flops 883138560 | bytes 7243648 | tf_op jit(solution)/shard_map/dot_general | solution.py:49
  84.6 5.0 %copy.12 = f32[4,120,1792]{1,2,0:T(8,128)} copy(f32[4,120,1792]{2,1,0:T(8,128)} %bitcast.25) | data formatting | bytes 6881280 | tf_op jit(solution)/shard_map/reshape | solution.py:54
  89.7 0.0 reduce-scatter.2.cloned.1.call-update
  89.7 49.7 %reduce-scatter.2.cloned.1.call-done = f32[4,120,448]{1,2,0:T(8,128)} async-done(((f32[4,120,1792]{1,2,0:T(8,128)}), f32[4,120,448]{1,2,0:T(8,128)}) %reduce-scatter.2.cloned.1.call-update) | async-done | bytes 860176 | tf_op jit(solution)/shard_map/reduce_scatter | solution.py:55
  139.4 27.5 %all_to_all.29 = f32[4,120,448]{1,2,0:T(8,128)S(1)} all-to-all(f32[4,120,448]{1,2,0:T(8,128)} %reduce-scatter.2.cloned.1.call-done), channel_id=1, replica_groups=mesh['node'=4,'local'=4,'cuts'=2] {'node'}, dimensions={0} | all-to-all | bytes 1720320 | tf_op jit(solution)/shard_map/all_to_all | solution.py:56
  166.9 1.0 fusion.7
  167.8 7.5 %all_to_all.30 = bf16[4,24,448]{2,1,0:T(8,128)(2,1)S(1)} all-to-all(bf16[4,24,448]{2,1,0:T(8,128)(2,1)S(1)} %bitcast.29), channel_id=1, replica_groups=mesh['node'=4,'local'=4,'cuts'=2] {'local'}, dimensions={0} | all-to-all | bytes 172032 | tf_op jit(solution)/shard_map/all_to_all | solution.py:58
  175.3 0.1 copy.13
  175.3 0.8 convert_element_type.57
  (10 shorter events, 0.1 us)
Async XLA Ops:
  6.5 73.6 %copy-start = (bf16[1,512,1792]{2,1,0:T(8,128)(2,1)S(1)}, bf16[1,512,1792]{2,1,0:T(8,128)(2,1)}, u32[]{:S(2)}) copy-start(bf16[1,512,1792]{2,1,0:T(8,128)(2,1)} %param.11) | copy-start | bytes 5505028
  6.5 73.6 %all-reduce.3.cloned.1.call-start = ((), (), s32[]{:S(2)}) async-start(), calls=%async_computation.6 | async-start | bytes 3932160 | tf_op jit(solution)/shard_map/psum | solution.py:47
  9.3 46.4 %copy-start.3 = (bf16[1,1792,512]{2,1,0:T(8,128)(2,1)S(1)}, bf16[1,1792,512]{2,1,0:T(8,128)(2,1)}, u32[]{:S(2)}) copy-start(bf16[1,1792,512]{2,1,0:T(8,128)(2,1)} %param.10) | copy-start | bytes 5505028
  55.7 2.0 %copy-start.4 = (bf16[1,1792,512]{2,1,0:T(8,128)(2,1)S(1)}, bf16[1,1792,512]{2,1,0:T(8,128)(2,1)}, u32[]{:S(2)}) copy-start(bf16[1,1792,512]{2,1,0:T(8,128)(2,1)} %param.9) | copy-start | bytes 5505028
  59.7 0.7 copy-start.2
  59.7 0.8 copy-start.1
  61.6 8.7 %all-to-all-start.1 = ((bf16[4,120,2]{1,2,0:T(2,128)(2,1)}), bf16[4,120,2]{1,2,0:T(2,128)(2,1)S(1)}, u32[]{:S(2)}, u32[]{:S(2)}) async-start(bf16[4,120,2]{1,2,0:T(2,128)(2,1)} %convolution_convert_fusion.1), calls=%async_computation.1 | async-start | bytes 4096 | tf_op jit(solution)/shard_map/all_to_all | solution.py:42
  64.8 74.5 %reduce-scatter.2.cloned.1.call-start = ((), (), s32[]{:S(2)}) async-start(), calls=%async_computation.5 | async-start | bytes 4587520 | tf_op jit(solution)/shard_map/reduce_scatter | solution.py:55
Sparse Core Ops, SparseCore 0:
  59.8 20.2 all-reduce.2
  89.8 49.5 reduce-scatter.1
where the time goes:
time: 183 us
  blocking collectives  81.3 us (44%)
  waiting for transfers between devices  64.8 us (35%)
  between operations  13.5 us (7%)
  matrix products  12.3 us (7%)
  local copies, waits for them, and re-layouts  6.63 us (4%)
  starting transfers between devices  3.27 us (2%)
    reduce_scatter x1, waiting for transfers between devices, on_device(): lax.psum_scatter(weighted, 'local', scatter_dimension=2, tiled=True)  49.7 us
    all_to_all x1, blocking collectives, on_device(): lax.all_to_all(outgoing, 'node', split_axis=0, concat_axis=0, tiled=True)  46.4 us
    all_to_all x1, blocking collectives, on_device(): lax.all_to_all(grouped, 'node', split_axis=0, concat_axis=0, tiled=True)  27.5 us
    psum x1, waiting for transfers between devices, on_device(): gate_full, up_full = lax.psum((gate_part, up_part), 'cuts')  9.72 us
    all_to_all x1, blocking collectives, on_device(): lax.all_to_all(partial_value, 'local', split_axis=0, concat_axis=1, tiled...  7.45 us
    all_to_all x1, waiting for transfers between devices, on_device(): lax.all_to_all(slot_weight, 'node', split_axis=0, concat_axis=0, tiled=True)  5.36 us
    reshape x1, local copies, waits for them, and re-layouts, on_device(): (slice_out * slot_scale[:, None]).reshape(node_count, capacity, half_width)  5.05 us
    dot_general x1, matrix products, on_device(): slice_out = jnp.dot(hidden, w_down[0], preferred_element_type=jnp.float32)  4.47 us
  transfers between devices with their start and end apart: 3, of which 3 were waited for; matrix products, arithmetic and copies ran while one was open for 1% of the time, Pallas kernels for 0%

commit v1 on v0

--- a/solution.py
+++ b/solution.py
@@ -3,8 +3,76 @@
 from jax import lax
 from jax.sharding import PartitionSpec as P
 
+GROUPS = ((0,), (1, 2, 3))
 
-def on_device(tokens, expert_ids, affinity, w_gate, w_up, w_down):
+
+def swap(value, axis, bits):
+    size = lax.axis_size(axis)
+    return lax.ppermute(value, axis, [(i, i ^ bits) for i in range(size)])
+
+
+def route_shares(affinity):
+    affinity_sum = jnp.sum(affinity, axis=1, keepdims=True)
+    return (2.5 * affinity / affinity_sum).astype(jnp.bfloat16).astype(jnp.float32)
+
+
+def dense_on_device(tokens, expert_ids, affinity, w_gate, w_up, w_down):
+    node_count = lax.axis_size("node")
+    local_count = lax.axis_size("local")
+    group_size = local_count // 2
+    expert_count = 2 * node_count
+    tok_count, _ = expert_ids.shape
+    rows = tok_count // local_count
+    my_node = lax.axis_index("node")
+    my_local = lax.axis_index("local")
+    share = route_shares(affinity)
+    expert_range = jnp.arange(expert_count, dtype=jnp.int32)
+    hit = expert_ids[:, :, None] == expert_range[None, None, :]
+    weight = jnp.sum(jnp.where(hit, share[:, :, None], 0.0), axis=1).astype(jnp.bfloat16)
+    all_weight = lax.all_gather(weight, "node")
+    mine = (expert_range == 2 * my_node + my_local // group_size).astype(jnp.float32)
+    own_weight = jnp.sum(all_weight.astype(jnp.float32) * mine, axis=-1)
+    own_weight = own_weight.reshape(node_count, local_count, rows)
+
+    def quarter(index):
+        return lax.dynamic_slice_in_dim(tokens, index * rows, rows, 0)
+
+    own = [quarter(my_local ^ j) for j in range(local_count)]
+    arrived = {k: swap(own[0], "node", k) for k in range(1, node_count)}
+    results = {}
+    for group in GROUPS:
+        if group == (0,):
+            parts = [own]
+        else:
+            joined = jnp.concatenate([arrived[k] for k in group], axis=0)
+            others = [swap(joined, "local", j) for j in range(1, local_count)]
+            parts = [[joined] + others]
+        blocks = parts[0]
+        x = jnp.concatenate(blocks, axis=0)
+        gate = jnp.dot(x, w_gate[0], preferred_element_type=jnp.float32)
+        up = jnp.dot(x, w_up[0], preferred_element_type=jnp.float32)
+        both = jnp.concatenate([gate, up], axis=1)
+        both = both + swap(both.astype(jnp.bfloat16), "cuts", 1).astype(jnp.float32)
+        gate, up = both[:, : gate.shape[1]], both[:, gate.shape[1] :]
+        hidden = (jax.nn.silu(gate) * up).astype(jnp.bfloat16)
+        out = jnp.dot(hidden, w_down[0], preferred_element_type=jnp.float32)
+        scale = jnp.concatenate(
+            [own_weight[my_node ^ k, my_local ^ j] for j in range(local_count) for k in group]
+        )
+        out = (out * scale[:, None]).astype(jnp.bfloat16)
+        step = len(group) * rows
+        total = out[:step].astype(jnp.float32)
+        for j in range(1, local_count):
+            total = total + swap(out[j * step : (j + 1) * step], "local", j).astype(jnp.float32)
+        for i, k in enumerate(group):
+            results[k] = total[i * rows : (i + 1) * rows]
+    final = results[0]
+    for k in range(1, node_count):
+        final = final + swap(results[k].astype(jnp.bfloat16), "node", k).astype(jnp.float32)
+    return final.astype(jnp.bfloat16)
+
+
+def slots_on_device(tokens, expert_ids, affinity, w_gate, w_up, w_down):
     node_count = lax.axis_size("node")
     local_count = lax.axis_size("local")
     group_size = local_count // 2
@@ -28,8 +96,7 @@
     outgoing = jnp.einsum(
         "tmc,td->mcd", dispatch.astype(jnp.bfloat16), tokens, preferred_element_type=jnp.float32
     ).astype(jnp.bfloat16)
-    affinity_sum = jnp.sum(affinity, axis=1, keepdims=True)
-    route_share = (2.5 * affinity / affinity_sum).astype(jnp.bfloat16).astype(jnp.float32)
+    route_share = route_shares(affinity)
     pair_range = jnp.arange(2, dtype=jnp.int32)
     expert_grid = 2 * node_range[:, None] + pair_range[None, :]
     own_route = expert_ids[:, :, None, None] == expert_grid[None, None, :, :]
@@ -59,6 +126,18 @@
     return summed.astype(jnp.bfloat16)
 
 
+def on_device(tokens, expert_ids, affinity, w_gate, w_up, w_down):
+    node_count = lax.axis_size("node")
+    local_count = lax.axis_size("local")
+    tok_count, top_count = expert_ids.shape
+    expert_count = 2 * node_count
+    capacity = (5 * tok_count * top_count + 4 * expert_count - 1) // (4 * expert_count)
+    powers = all(size & (size - 1) == 0 for size in (node_count, local_count))
+    everywhere = node_count == top_count // 2 and capacity >= tok_count
+    chosen = dense_on_device if everywhere and powers and tok_count % local_count == 0 else slots_on_device
+    return chosen(tokens, expert_ids, affinity, w_gate, w_up, w_down)
+
+
 def solution(mesh):
     return jax.shard_map(
         on_device,

time: 183 us -> 71.4 us (0.39)
  blocking collectives: 81.3 us -> 11.9 us
  waiting for transfers between devices: 64.8 us -> 24.1 us
  starting transfers between devices: 3.27 us -> 21 us
  between operations: 13.5 us -> 0.21 us
  matrix products: 12.3 us -> 6.92 us
    all_to_all x3 -> x0, blocking collectives: 81.3 us -> none  [the longest x1 46.4 us: on_device(): lax.all_to_all(outgoing, 'node', split_axis=0, concat_axis=0, tiled=True)]
    reduce_scatter x1 -> x0, waiting for transfers between devices: 49.7 us -> none  [on_device(): lax.psum_scatter(weighted, 'local', scatter_dimension=2, tiled=True)]
    ppermute x0 -> x17, waiting for transfers between devices: none -> 24.1 us  [swap(): return lax.ppermute(value, axis, [(i, i ^ bits) for i in range(size)])]
    ppermute x0 -> x17, starting transfers between devices: none -> 21 us  [swap(): return lax.ppermute(value, axis, [(i, i ^ bits) for i in range(size)])]
    all_gather x0 -> x1, blocking collectives: none -> 11.9 us  [dense_on_device(): all_weight = lax.all_gather(weight, 'node')]
    psum x1 -> x0, waiting for transfers between devices: 9.72 us -> none  [on_device(): gate_full, up_full = lax.psum((gate_part, up_part), 'cuts')]
    dot_general x7 -> x6, matrix products: 12.3 us -> 6.92 us  [the longest x2 3.07 us: dense_on_device(): up = jnp.dot(x, w_up[0], preferred_element_type=jnp.float32)]
    all_to_all x1 -> x0, waiting for transfers between devices: 5.36 us -> none  [on_device(): lax.all_to_all(slot_weight, 'node', split_axis=0, concat_axis=0, tiled=True)]
  transfers between devices with their start and end apart: 3 -> 17, of which waited for: 3 -> 8; matrix products, arithmetic and copies ran while one was open for 1% -> 15% of each run, Pallas kernels for 0% -> 0%
where the time goes in v1:
time: 71.4 us; the launch traced here: 71.2 us
  waiting for transfers between devices  24.1 us (34%)
  starting transfers between devices  21 us (29%)
  blocking collectives  11.9 us (17%)
  matrix products  6.92 us (10%)
  local copies, waits for them, and re-layouts  5.67 us (8%)
  other arithmetic  1.36 us (2%)
    ppermute x17, waiting for transfers between devices, swap(): return lax.ppermute(value, axis, [(i, i ^ bits) for i in range(size)])  24.1 us
    ppermute x17, starting transfers between devices, swap(): return lax.ppermute(value, axis, [(i, i ^ bits) for i in range(size)])  21 us
    all_gather x1, blocking collectives, dense_on_device(): all_weight = lax.all_gather(weight, 'node')  11.9 us
    dot_general x2, matrix products, dense_on_device(): up = jnp.dot(x, w_up[0], preferred_element_type=jnp.float32)  3.07 us
    unnamed x16, local copies, waits for them, and re-layouts  2.85 us
    dot_general x2, matrix products, dense_on_device(): gate = jnp.dot(x, w_gate[0], preferred_element_type=jnp.float32)  2.61 us
  transfers between devices with their start and end apart: 17, of which 8 were waited for; matrix products, arithmetic and copies ran while one was open for 15% of the time, Pallas kernels for 0%

profile of v1, /device:TPU:0, one launch (start us, length us, event | category | flops | bytes accessed | tf_op | source)
XLA Modules:
  0.0 71.2 jit_solution(1976424067221022738)
XLA Ops:
  0.0 1.2 %constant_dynamic-slice_fusion.18 = (bf16[24,1792]{1,0:T(8,128)(2,1)S(1)}, bf16[24,1792]{1,0:T(8,128)(2,1)S(1)}, bf16[24,1792]{1,0:T(8,128)(2,1)S(1)}, bf16[24,1792]{1,0:T(8,128)(2,1)S(1)}) fusion(bf16[96,1792]{1,0:T(8,128)(2,1)} %param.6, s32[]{:T(128)S(6)} %select_n.34, s32[]{:T(128)S(6)} %select_n.33, s32[]{:T(128)S(6)} %select_n.36, s32[]{:T(128)S(6)} %select_n.35), kind=kLoop, calls=%fused_computation.60 | loop fusion | bytes 688144 | tf_op jit(solution)/shard_map/dynamic_slice | solution.py:38
  1.2 3.1 %collective-permute-start.4 = (bf16[24,1792]{1,0:T(8,128)(2,1)S(1)}, bf16[24,1792]{1,0:T(8,128)(2,1)S(1)}, u32[]{:S(2)}, u32[]{:S(2)}) collective-permute-start(bf16[24,1792]{1,0:T(8,128)(2,1)S(1)} %get-tuple-element.12), channel_id=1, source_target_pairs={{0,8},{8,0},{16,24},{24,16},{1,9},{9,1},{17,25},{25,17},{2,10},{10... | collective-permute-start | bytes 258056 | tf_op jit(solution)/shard_map/ppermute | solution.py:11
  4.3 2.6 %collective-permute-start.5 = (bf16[24,1792]{1,0:T(8,128)(2,1)S(1)}, bf16[24,1792]{1,0:T(8,128)(2,1)S(1)}, u32[]{:S(2)}, u32[]{:S(2)}) collective-permute-start(bf16[24,1792]{1,0:T(8,128)(2,1)S(1)} %get-tuple-element.12), channel_id=1, source_target_pairs={{0,16},{8,24},{16,0},{24,8},{1,17},{9,25},{17,1},{25,9},{2,18},{10... | collective-permute-start | bytes 258056 | tf_op jit(solution)/shard_map/ppermute | solution.py:11
  6.9 1.9 %fusion.10 = f32[96,512]{1,0:T(8,128)S(1)} fusion(bf16[1,1792,512]{2,1,0:T(8,128)(2,1)} %param.9, bf16[24,1792]{1,0:T(8,128)(2,1)S(1)} %get-tuple-element.13, bf16[24,1792]{1,0:T(8,128)(2,1)S(1)} %get-tuple-element.14, bf16[24,1792]{1,0:T(8,128)(2,1)S(1)} %get-tuple-element.11, bf16[24,1792]{1,0:T(8,128)(2,1)S(1)} %get-tuple-element.12), kind=kOutput, calls=%fused_computation.12 | convolution fusion | flops 177537024 | bytes 2375680 | tf_op jit(solution)/shard_map/dot_general | solution.py:52
  9.6 0.6 constant_dynamic-update-slice_fusion.2
  10.2 3.6 %collective-permute-done.5 = bf16[24,1792]{1,0:T(8,128)(2,1)S(1)} collective-permute-done((bf16[24,1792]{1,0:T(8,128)(2,1)S(1)}, bf16[24,1792]{1,0:T(8,128)(2,1)S(1)}, u32[]{:S(2)}, u32[]{:S(2)}) %collective-permute-start.5) | collective-permute-done | bytes 86048 | tf_op jit(solution)/shard_map/ppermute | solution.py:11
  13.8 0.6 constant_dynamic-update-slice_fusion.1
  14.4 0.6 constant_dynamic-update-slice_fusion
  15.1 1.5 %collective-permute-start.7 = (bf16[72,1792]{1,0:T(8,128)(2,1)S(1)}, bf16[72,1792]{1,0:T(8,128)(2,1)S(1)}, u32[]{:S(2)}, u32[]{:S(2)}) collective-permute-start(bf16[72,1792]{1,0:T(8,128)(2,1)S(1)} %get-tuple-element.18), channel_id=1, source_target_pairs={{0,2},{2,0},{4,6},{6,4},{1,3},{3,1},{5,7},{7,5},{8,10},{10,8},{12,... | collective-permute-start | bytes 774152 | tf_op jit(solution)/shard_map/ppermute | solution.py:11
  16.6 11.9 %all-gather.1 = bf16[4,96,8]{1,2,0:T(8,128)(2,1)S(1)} all-gather(bf16[1,96,8]{1,2,0:T(8,128)(2,1)S(1)} %bitcast.52), channel_id=2, replica_groups=mesh['node'=4,'local'=4,'cuts'=2] {'node'}, dimensions={0}, use_global_device_ids=true | all-gather | bytes 7680 | tf_op jit(solution)/shard_map/all_gather | solution.py:32
  28.6 1.5 %collective-permute-start.8 = (bf16[72,1792]{1,0:T(8,128)(2,1)S(1)}, bf16[72,1792]{1,0:T(8,128)(2,1)S(1)}, u32[]{:S(2)}, u32[]{:S(2)}) collective-permute-start(bf16[72,1792]{1,0:T(8,128)(2,1)S(1)} %get-tuple-element.18), channel_id=1, source_target_pairs={{0,4},{2,6},{4,0},{6,2},{1,5},{3,7},{5,1},{7,3},{8,12},{10,14},{12... | collective-permute-start | bytes 774152 | tf_op jit(solution)/shard_map/ppermute | solution.py:11
  30.8 0.7 %constant_dynamic-update-slice_fusion.5 = bf16[288,1792]{1,0:T(8,128)(2,1)} fusion(bf16[288,1792]{1,0:T(8,128)(2,1)} %get-tuple-element.19, bf16[72,1792]{1,0:T(8,128)(2,1)S(1)} %collective-permute-done.7), kind=kLoop, calls=%fused_computation.36 | loop fusion | bytes 516096
  31.5 6.3 %collective-permute-done.8 = bf16[72,1792]{1,0:T(8,128)(2,1)S(1)} collective-permute-done((bf16[72,1792]{1,0:T(8,128)(2,1)S(1)}, bf16[72,1792]{1,0:T(8,128)(2,1)S(1)}, u32[]{:S(2)}, u32[]{:S(2)}) %collective-permute-start.8) | collective-permute-done | bytes 258080 | tf_op jit(solution)/shard_map/ppermute | solution.py:11
  37.8 0.7 %constant_dynamic-update-slice_fusion.4 = bf16[288,1792]{1,0:T(8,128)(2,1)} fusion(bf16[288,1792]{1,0:T(8,128)(2,1)} %constant_dynamic-update-slice_fusion.5, bf16[72,1792]{1,0:T(8,128)(2,1)S(1)} %collective-permute-done.8), kind=kLoop, calls=%fused_computation.35 | loop fusion | bytes 516096
  38.6 0.7 constant_dynamic-update-slice_fusion.3
  39.3 2.6 %fusion.4 = f32[288,512]{1,0:T(8,128)S(1)} fusion(bf16[288,1792]{1,0:T(8,128)(2,1)} %constant_dynamic-update-slice_fusion.3, bf16[1,1792,512]{2,1,0:T(8,128)(2,1)} %param.10), kind=kOutput, calls=%fused_computation.6 | convolution fusion | flops 528482304 | bytes 3457024 | tf_op jit(solution)/shard_map/dot_general | solution.py:53
  41.9 0.7 fusion.8
  43.4 1.4 %collective-permute-done.10 = bf16[288,1024]{1,0:T(8,128)(2,1)S(1)} collective-permute-done((bf16[288,1024]{1,0:T(8,128)(2,1)S(1)}, bf16[288,1024]{1,0:T(8,128)(2,1)S(1)}, u32[]{:S(2)}, u32[]{:S(2)}) %collective-permute-start.10) | collective-permute-done | bytes 589856 | tf_op jit(solution)/shard_map/ppermute | solution.py:11
  45.0 0.8 %fusion = bf16[288,1792]{1,0:T(8,128)(2,1)S(1)} fusion(bf16[1,512,1792]{2,1,0:T(8,128)(2,1)S(1)} %copy-done, f32[288]{0:T(512)S(1)} %concatenate.28, f32[288,1024]{1,0:T(8,128)S(1)} %convert_add_fusion), kind=kOutput, calls=%fused_computation.1 | convolution fusion | flops 530399232 | bytes 4048000 | tf_op jit(solution)/shard_map/dot_general | solution.py:58
  46.4 1.5 %collective-permute-start.12 = (bf16[72,1792]{1,0:T(8,128)(2,1)S(1)}, bf16[72,1792]{1,0:T(8,128)(2,1)S(1)}, u32[]{:S(2)}, u32[]{:S(2)}) collective-permute-start(bf16[72,1792]{1,0:T(8,128)(2,1)S(1)} %get-tuple-element.7), channel_id=1, source_target_pairs={{0,4},{2,6},{4,0},{6,2},{1,5},{3,7},{5,1},{7,3},{8,12},{10,14},{12... | collective-permute-start | bytes 774152 | tf_op jit(solution)/shard_map/ppermute | solution.py:11
  47.9 1.4 %collective-permute-start.13 = (bf16[72,1792]{1,0:T(8,128)(2,1)S(1)}, bf16[72,1792]{1,0:T(8,128)(2,1)S(1)}, u32[]{:S(2)}, u32[]{:S(2)}) collective-permute-start(bf16[72,1792]{1,0:T(8,128)(2,1)S(1)} %get-tuple-element.6), channel_id=1, source_target_pairs={{0,6},{2,4},{4,2},{6,0},{1,7},{3,5},{5,3},{7,1},{8,14},{10,12},{12... | collective-permute-start | bytes 774152 | tf_op jit(solution)/shard_map/ppermute | solution.py:11
  49.4 0.6 collective-permute-start.1
  50.0 1.5 %collective-permute-start.2 = (bf16[24,1792]{1,0:T(8,128)(2,1)S(1)}, bf16[24,1792]{1,0:T(8,128)(2,1)S(1)}, u32[]{:S(2)}, u32[]{:S(2)}) collective-permute-start(bf16[24,1792]{1,0:T(8,128)(2,1)S(1)} %get-tuple-element.10), channel_id=1, source_target_pairs={{0,4},{2,6},{4,0},{6,2},{1,5},{3,7},{5,1},{7,3},{8,12},{10,14},{12... | collective-permute-start | bytes 258056 | tf_op jit(solution)/shard_map/ppermute | solution.py:11
  51.5 3.4 %collective-permute-done.11 = bf16[72,1792]{1,0:T(8,128)(2,1)S(1)} collective-permute-done((bf16[72,1792]{1,0:T(8,128)(2,1)S(1)}, bf16[72,1792]{1,0:T(8,128)(2,1)S(1)}, u32[]{:S(2)}, u32[]{:S(2)}) %collective-permute-start.11) | collective-permute-done | bytes 258080 | tf_op jit(solution)/shard_map/ppermute | solution.py:11
  55.0 1.5 %collective-permute-start.3 = (bf16[24,1792]{1,0:T(8,128)(2,1)S(1)}, bf16[24,1792]{1,0:T(8,128)(2,1)S(1)}, u32[]{:S(2)}, u32[]{:S(2)}) collective-permute-start(bf16[24,1792]{1,0:T(8,128)(2,1)S(1)} %get-tuple-element.9), channel_id=1, source_target_pairs={{0,6},{2,4},{4,2},{6,0},{1,7},{3,5},{5,3},{7,1},{8,14},{10,12},{12... | collective-permute-start | bytes 258056 | tf_op jit(solution)/shard_map/ppermute | solution.py:11
  56.4 3.8 %collective-permute-done.12 = bf16[72,1792]{1,0:T(8,128)(2,1)S(1)} collective-permute-done((bf16[72,1792]{1,0:T(8,128)(2,1)S(1)}, bf16[72,1792]{1,0:T(8,128)(2,1)S(1)}, u32[]{:S(2)}, u32[]{:S(2)}) %collective-permute-start.12) | collective-permute-done | bytes 258080 | tf_op jit(solution)/shard_map/ppermute | solution.py:11
  60.2 1.3 %collective-permute-done.13 = bf16[72,1792]{1,0:T(8,128)(2,1)S(1)} collective-permute-done((bf16[72,1792]{1,0:T(8,128)(2,1)S(1)}, bf16[72,1792]{1,0:T(8,128)(2,1)S(1)}, u32[]{:S(2)}, u32[]{:S(2)}) %collective-permute-start.13) | collective-permute-done | bytes 258080 | tf_op jit(solution)/shard_map/ppermute | solution.py:11
  61.7 0.6 collective-permute-start.14
  62.3 1.2 %collective-permute-start.15 = (bf16[24,1792]{1,0:T(8,128)(2,1)S(1)}, bf16[24,1792]{1,0:T(8,128)(2,1)S(1)}, u32[]{:S(2)}, u32[]{:S(2)}) collective-permute-start(bf16[24,1792]{1,0:T(8,128)(2,1)S(1)} %get-tuple-element.17), channel_id=1, source_target_pairs={{0,16},{8,24},{16,0},{24,8},{1,17},{9,25},{17,1},{25,9},{2,18},{10... | collective-permute-start | bytes 258056 | tf_op jit(solution)/shard_map/ppermute | solution.py:11
  63.5 2.6 %collective-permute-start.16 = (bf16[24,1792]{1,0:T(8,128)(2,1)S(1)}, bf16[24,1792]{1,0:T(8,128)(2,1)S(1)}, u32[]{:S(2)}, u32[]{:S(2)}) collective-permute-start(bf16[24,1792]{1,0:T(8,128)(2,1)S(1)} %get-tuple-element.16), channel_id=1, source_target_pairs={{0,24},{8,16},{16,8},{24,0},{1,25},{9,17},{17,9},{25,1},{2,26},{10... | collective-permute-start | bytes 258056 | tf_op jit(solution)/shard_map/ppermute | solution.py:11
  66.2 4.2 %collective-permute-done.15 = bf16[24,1792]{1,0:T(8,128)(2,1)S(1)} collective-permute-done((bf16[24,1792]{1,0:T(8,128)(2,1)S(1)}, bf16[24,1792]{1,0:T(8,128)(2,1)S(1)}, u32[]{:S(2)}, u32[]{:S(2)}) %collective-permute-start.15) | collective-permute-done | bytes 86048 | tf_op jit(solution)/shard_map/ppermute | solution.py:11
  70.4 0.7 %add_convert_fusion.1 = bf16[24,1792]{1,0:T(8,128)(2,1)} fusion(bf16[24,1792]{1,0:T(8,128)(2,1)S(1)} %collective-permute-done.16, bf16[24,1792]{1,0:T(8,128)(2,1)S(1)} %collective-permute-done.15, bf16[24,1792]{1,0:T(8,128)(2,1)S(1)} %collective-permute-done.14, bf16[24,1792]{1,0:T(8,128)(2,1)S(1)} %collective-permute-done.3, ...), kind=kLoop, calls=%fused_computation.27 | loop fusion | flops 602112 | bytes 688128 | tf_op jit(solution)/shard_map/convert_element_type | solution.py:72
  (46 shorter events, 3.3 us)
Async XLA Ops:
  0.0 42.9 %copy-start = (bf16[1,512,1792]{2,1,0:T(8,128)(2,1)S(1)}, bf16[1,512,1792]{2,1,0:T(8,128)(2,1)}, u32[]{:S(2)}) copy-start(bf16[1,512,1792]{2,1,0:T(8,128)(2,1)} %param.11) | copy-start | bytes 5505028
  0.0 8.8 %copy-start.4 = (bf16[1,1792,512]{2,1,0:T(8,128)(2,1)S(1)}, bf16[1,1792,512]{2,1,0:T(8,128)(2,1)}, u32[]{:S(2)}) copy-start(bf16[1,1792,512]{2,1,0:T(8,128)(2,1)} %param.10) | copy-start | bytes 5505028
  1.2 8.4 %collective-permute-start.4 = (bf16[24,1792]{1,0:T(8,128)(2,1)S(1)}, bf16[24,1792]{1,0:T(8,128)(2,1)S(1)}, u32[]{:S(2)}, u32[]{:S(2)}) collective-permute-start(bf16[24,1792]{1,0:T(8,128)(2,1)S(1)} %get-tuple-element.12), channel_id=1, source_target_pairs={{0,8},{8,0},{16,24},{24,16},{1,9},{9,1},{17,25},{25,17},{2,10},{10... | collective-permute-start | bytes 258056 | tf_op jit(solution)/shard_map/ppermute | solution.py:11
  4.3 9.5 %collective-permute-start.5 = (bf16[24,1792]{1,0:T(8,128)(2,1)S(1)}, bf16[24,1792]{1,0:T(8,128)(2,1)S(1)}, u32[]{:S(2)}, u32[]{:S(2)}) collective-permute-start(bf16[24,1792]{1,0:T(8,128)(2,1)S(1)} %get-tuple-element.12), channel_id=1, source_target_pairs={{0,16},{8,24},{16,0},{24,8},{1,17},{9,25},{17,1},{25,9},{2,18},{10... | collective-permute-start | bytes 258056 | tf_op jit(solution)/shard_map/ppermute | solution.py:11
  6.9 7.5 %collective-permute-start.6 = (bf16[24,1792]{1,0:T(8,128)(2,1)S(1)}, bf16[24,1792]{1,0:T(8,128)(2,1)S(1)}, u32[]{:S(2)}, u32[]{:S(2)}) collective-permute-start(bf16[24,1792]{1,0:T(8,128)(2,1)S(1)} %get-tuple-element.12), channel_id=1, source_target_pairs={{0,24},{8,16},{16,8},{24,0},{1,25},{9,17},{17,9},{25,1},{2,26},{10... | collective-permute-start | bytes 258056 | tf_op jit(solution)/shard_map/ppermute | solution.py:11
  8.8 0.7 copy-start.1
  8.8 0.7 %copy-start.3 = (s32[96,8]{0,1:T(8,128)S(1)}, s32[96,8]{0,1:T(8,128)}, u32[]{:S(2)}) copy-start(s32[96,8]{0,1:T(8,128)} %param.7) | copy-start | bytes 9220
  9.3 33.6 %collective-permute-start = (bf16[96,1024]{1,0:T(8,128)(2,1)S(1)}, bf16[96,1024]{1,0:T(8,128)(2,1)S(1)}, u32[]{:S(2)}, u32[]{:S(2)}) collective-permute-start(bf16[96,1024]{1,0:T(8,128)(2,1)S(1)} %fusion.14), channel_id=1, source_target_pairs={{0,1},{1,0},{2,3},{3,2},{4,5},{5,4},{6,7},{7,6},{8,9},{9,8},{10,11... | collective-permute-start | bytes 589832 | tf_op jit(solution)/shard_map/ppermute | solution.py:11
  15.1 15.7 %collective-permute-start.7 = (bf16[72,1792]{1,0:T(8,128)(2,1)S(1)}, bf16[72,1792]{1,0:T(8,128)(2,1)S(1)}, u32[]{:S(2)}, u32[]{:S(2)}) collective-permute-start(bf16[72,1792]{1,0:T(8,128)(2,1)S(1)} %get-tuple-element.18), channel_id=1, source_target_pairs={{0,2},{2,0},{4,6},{6,4},{1,3},{3,1},{5,7},{7,5},{8,10},{10,8},{12,... | collective-permute-start | bytes 774152 | tf_op jit(solution)/shard_map/ppermute | solution.py:11
  28.6 9.2 %collective-permute-start.8 = (bf16[72,1792]{1,0:T(8,128)(2,1)S(1)}, bf16[72,1792]{1,0:T(8,128)(2,1)S(1)}, u32[]{:S(2)}, u32[]{:S(2)}) collective-permute-start(bf16[72,1792]{1,0:T(8,128)(2,1)S(1)} %get-tuple-element.18), channel_id=1, source_target_pairs={{0,4},{2,6},{4,0},{6,2},{1,5},{3,7},{5,1},{7,3},{8,12},{10,14},{12... | collective-permute-start | bytes 774152 | tf_op jit(solution)/shard_map/ppermute | solution.py:11
  30.2 8.3 %collective-permute-start.9 = (bf16[72,1792]{1,0:T(8,128)(2,1)S(1)}, bf16[72,1792]{1,0:T(8,128)(2,1)S(1)}, u32[]{:S(2)}, u32[]{:S(2)}) collective-permute-start(bf16[72,1792]{1,0:T(8,128)(2,1)S(1)} %get-tuple-element.18), channel_id=1, source_target_pairs={{0,6},{2,4},{4,2},{6,0},{1,7},{3,5},{5,3},{7,1},{8,14},{10,12},{12... | collective-permute-start | bytes 774152 | tf_op jit(solution)/shard_map/ppermute | solution.py:11
  39.3 2.7 %copy-start.2 = (bf16[288,1792]{1,0:T(8,128)(2,1)S(1)}, bf16[288,1792]{1,0:T(8,128)(2,1)}, u32[]{:S(2)}) copy-start(bf16[288,1792]{1,0:T(8,128)(2,1)} %constant_dynamic-update-slice_fusion.3) | copy-start | bytes 3096580
  39.3 2.7 %copy-start.5 = (bf16[1,1792,512]{2,1,0:T(8,128)(2,1)S(1)}, bf16[1,1792,512]{2,1,0:T(8,128)(2,1)}, u32[]{:S(2)}) copy-start(bf16[1,1792,512]{2,1,0:T(8,128)(2,1)} %param.9) | copy-start | bytes 5505028
  42.7 2.1 %collective-permute-start.10 = (bf16[288,1024]{1,0:T(8,128)(2,1)S(1)}, bf16[288,1024]{1,0:T(8,128)(2,1)S(1)}, u32[]{:S(2)}, u32[]{:S(2)}) collective-permute-start(bf16[288,1024]{1,0:T(8,128)(2,1)S(1)} %fusion.12), channel_id=1, source_target_pairs={{0,1},{1,0},{2,3},{3,2},{4,5},{5,4},{6,7},{7,6},{8,9},{9,8},{10,11... | collective-permute-start | bytes 1769480 | tf_op jit(solution)/shard_map/ppermute | solution.py:11
  45.8 9.1 %collective-permute-start.11 = (bf16[72,1792]{1,0:T(8,128)(2,1)S(1)}, bf16[72,1792]{1,0:T(8,128)(2,1)S(1)}, u32[]{:S(2)}, u32[]{:S(2)}) collective-permute-start(bf16[72,1792]{1,0:T(8,128)(2,1)S(1)} %get-tuple-element.5), channel_id=1, source_target_pairs={{0,2},{2,0},{4,6},{6,4},{1,3},{3,1},{5,7},{7,5},{8,10},{10,8},{12,... | collective-permute-start | bytes 774152 | tf_op jit(solution)/shard_map/ppermute | solution.py:11
  46.4 13.8 %collective-permute-start.12 = (bf16[72,1792]{1,0:T(8,128)(2,1)S(1)}, bf16[72,1792]{1,0:T(8,128)(2,1)S(1)}, u32[]{:S(2)}, u32[]{:S(2)}) collective-permute-start(bf16[72,1792]{1,0:T(8,128)(2,1)S(1)} %get-tuple-element.7), channel_id=1, source_target_pairs={{0,4},{2,6},{4,0},{6,2},{1,5},{3,7},{5,1},{7,3},{8,12},{10,14},{12... | collective-permute-start | bytes 774152 | tf_op jit(solution)/shard_map/ppermute | solution.py:11
  47.9 13.5 %collective-permute-start.13 = (bf16[72,1792]{1,0:T(8,128)(2,1)S(1)}, bf16[72,1792]{1,0:T(8,128)(2,1)S(1)}, u32[]{:S(2)}, u32[]{:S(2)}) collective-permute-start(bf16[72,1792]{1,0:T(8,128)(2,1)S(1)} %get-tuple-element.6), channel_id=1, source_target_pairs={{0,6},{2,4},{4,2},{6,0},{1,7},{3,5},{5,3},{7,1},{8,14},{10,12},{12... | collective-permute-start | bytes 774152 | tf_op jit(solution)/shard_map/ppermute | solution.py:11
  49.4 14.1 %collective-permute-start.1 = (bf16[24,1792]{1,0:T(8,128)(2,1)S(1)}, bf16[24,1792]{1,0:T(8,128)(2,1)S(1)}, u32[]{:S(2)}, u32[]{:S(2)}) collective-permute-start(bf16[24,1792]{1,0:T(8,128)(2,1)S(1)} %get-tuple-element.8), channel_id=1, source_target_pairs={{0,2},{2,0},{4,6},{6,4},{1,3},{3,1},{5,7},{7,5},{8,10},{10,8},{12,... | collective-permute-start | bytes 258056 | tf_op jit(solution)/shard_map/ppermute | solution.py:11
  50.0 16.1 %collective-permute-start.2 = (bf16[24,1792]{1,0:T(8,128)(2,1)S(1)}, bf16[24,1792]{1,0:T(8,128)(2,1)S(1)}, u32[]{:S(2)}, u32[]{:S(2)}) collective-permute-start(bf16[24,1792]{1,0:T(8,128)(2,1)S(1)} %get-tuple-element.10), channel_id=1, source_target_pairs={{0,4},{2,6},{4,0},{6,2},{1,5},{3,7},{5,1},{7,3},{8,12},{10,14},{12... | collective-permute-start | bytes 258056 | tf_op jit(solution)/shard_map/ppermute | solution.py:11
  55.0 11.2 %collective-permute-start.3 = (bf16[24,1792]{1,0:T(8,128)(2,1)S(1)}, bf16[24,1792]{1,0:T(8,128)(2,1)S(1)}, u32[]{:S(2)}, u32[]{:S(2)}) collective-permute-start(bf16[24,1792]{1,0:T(8,128)(2,1)S(1)} %get-tuple-element.9), channel_id=1, source_target_pairs={{0,6},{2,4},{4,2},{6,0},{1,7},{3,5},{5,3},{7,1},{8,14},{10,12},{12... | collective-permute-start | bytes 258056 | tf_op jit(solution)/shard_map/ppermute | solution.py:11
  61.7 4.6 %collective-permute-start.14 = (bf16[24,1792]{1,0:T(8,128)(2,1)S(1)}, bf16[24,1792]{1,0:T(8,128)(2,1)S(1)}, u32[]{:S(2)}, u32[]{:S(2)}) collective-permute-start(bf16[24,1792]{1,0:T(8,128)(2,1)S(1)} %get-tuple-element.15), channel_id=1, source_target_pairs={{0,8},{8,0},{16,24},{24,16},{1,9},{9,1},{17,25},{25,17},{2,10},{10... | collective-permute-start | bytes 258056 | tf_op jit(solution)/shard_map/ppermute | solution.py:11
  62.3 8.2 %collective-permute-start.15 = (bf16[24,1792]{1,0:T(8,128)(2,1)S(1)}, bf16[24,1792]{1,0:T(8,128)(2,1)S(1)}, u32[]{:S(2)}, u32[]{:S(2)}) collective-permute-start(bf16[24,1792]{1,0:T(8,128)(2,1)S(1)} %get-tuple-element.17), channel_id=1, source_target_pairs={{0,16},{8,24},{16,0},{24,8},{1,17},{9,25},{17,1},{25,9},{2,18},{10... | collective-permute-start | bytes 258056 | tf_op jit(solution)/shard_map/ppermute | solution.py:11
  63.5 6.9 %collective-permute-start.16 = (bf16[24,1792]{1,0:T(8,128)(2,1)S(1)}, bf16[24,1792]{1,0:T(8,128)(2,1)S(1)}, u32[]{:S(2)}, u32[]{:S(2)}) collective-permute-start(bf16[24,1792]{1,0:T(8,128)(2,1)S(1)} %get-tuple-element.16), channel_id=1, source_target_pairs={{0,24},{8,16},{16,8},{24,0},{1,25},{9,17},{17,9},{25,1},{2,26},{10... | collective-permute-start | bytes 258056 | tf_op jit(solution)/shard_map/ppermute | solution.py:11

commit v2 on v0

--- a/solution.py
+++ b/solution.py
@@ -1,10 +1,169 @@
 import jax
 import jax.numpy as jnp
 from jax import lax
+from jax.experimental import pallas as pl
+from jax.experimental.pallas import tpu as pltpu
 from jax.sharding import PartitionSpec as P
 
-
-def on_device(tokens, expert_ids, affinity, w_gate, w_up, w_down):
+LANES = 128
+
+
+def swap(value, axis, bits):
+    size = lax.axis_size(axis)
+    return lax.ppermute(value, axis, [(i, i ^ bits) for i in range(size)])
+
+
+def route_shares(affinity):
+    affinity_sum = jnp.sum(affinity, axis=1, keepdims=True)
+    return (2.5 * affinity / affinity_sum).astype(jnp.bfloat16).astype(jnp.float32)
+
+
+def in_vmem(body, out_shapes, cost, *args):
+    return pl.pallas_call(
+        body,
+        out_shape=out_shapes,
+        in_specs=[pl.BlockSpec(memory_space=pltpu.VMEM)] * len(args),
+        out_specs=jax.tree.map(lambda _: pl.BlockSpec(memory_space=pltpu.VMEM), out_shapes),
+        compiler_params=pltpu.CompilerParams(vmem_limit_bytes=24 * 2**20),
+        cost_estimate=pl.CostEstimate(flops=cost, bytes_accessed=2**20, transcendentals=0),
+    )(*args)
+
+
+def shape(*dims):
+    return jax.ShapeDtypeStruct(dims, jnp.bfloat16)
+
+
+def prepare(tokens, expert_ids, affinity, rows):
+    tok_count, width = tokens.shape
+    choices = expert_ids.shape[1]
+
+    def body(tokens_hbm, ids_hbm, affinity_hbm, all_ref, share_ref, ids_ref, affinity_ref, sems):
+        copies = [
+            pltpu.make_async_copy(tokens_hbm, all_ref.at[:, :width], sems.at[0]),
+            pltpu.make_async_copy(ids_hbm, ids_ref, sems.at[1]),
+            pltpu.make_async_copy(affinity_hbm, affinity_ref, sems.at[2]),
+        ]
+        for copy in copies:
+            copy.start()
+        copies[1].wait()
+        copies[2].wait()
+        total = jnp.sum(affinity_ref[...], axis=0, keepdims=True)
+        share = (2.5 * affinity_ref[...] / total).astype(jnp.bfloat16).astype(jnp.float32)
+        ids = ids_ref[...]
+        lane = lax.broadcasted_iota(jnp.int32, (LANES, tok_count), 0)
+        weight = jnp.zeros((LANES, tok_count), jnp.float32)
+        for c in range(choices):
+            weight += jnp.where(ids[c : c + 1, :] == lane, share[c : c + 1, :], 0.0)
+        all_ref[:, width:] = weight.T.astype(jnp.bfloat16)
+        copies[0].wait()
+        for i in range(tok_count // rows):
+
+            @pl.when(lax.axis_index("local") == i)
+            def _():
+                share_ref[...] = all_ref[i * rows : (i + 1) * rows, :]
+
+    return pl.pallas_call(
+        body,
+        out_shape=(shape(tok_count, width + LANES), shape(rows, width + LANES)),
+        in_specs=[pl.BlockSpec(memory_space=pltpu.HBM)] * 3,
+        out_specs=[pl.BlockSpec(memory_space=pltpu.VMEM)] * 2,
+        scratch_shapes=[
+            pltpu.VMEM((choices, tok_count), jnp.int32),
+            pltpu.VMEM((choices, tok_count), jnp.float32),
+            pltpu.SemaphoreType.DMA((3,)),
+        ],
+        compiler_params=pltpu.CompilerParams(vmem_limit_bytes=24 * 2**20),
+        cost_estimate=pl.CostEstimate(flops=10**6, bytes_accessed=2**20, transcendentals=0),
+    )(tokens, expert_ids.T, affinity.T)
+
+
+def project(x, w_gate, w_up):
+    count = x.shape[0]
+    width, hid = w_gate.shape
+
+    def body(x_ref, gate_ref, up_ref, out_ref):
+        rows = x_ref[:, :width]
+        for i, ref in enumerate((gate_ref, up_ref)):
+            part = jnp.dot(rows, ref[...], preferred_element_type=jnp.float32)
+            out_ref[:, i * hid : (i + 1) * hid] = part.astype(jnp.bfloat16)
+
+    return in_vmem(body, shape(count, 2 * hid), 4 * count * width * hid, x, w_gate, w_up)
+
+
+def finish(x, part, other, w_down, group_size):
+    count = x.shape[0]
+    hid, width = w_down.shape
+
+    def body(x_ref, part_ref, other_ref, down_ref, out_ref):
+        both = part_ref[...].astype(jnp.float32) + other_ref[...].astype(jnp.float32)
+        gate, up = both[:, :hid], both[:, hid:]
+        hidden = (gate / (1.0 + jnp.exp(-gate)) * up).astype(jnp.bfloat16)
+        expert = 2 * lax.axis_index("node") + lax.axis_index("local") // group_size
+        lane = lax.broadcasted_iota(jnp.int32, (count, LANES), 1)
+        table = x_ref[:, width:].astype(jnp.float32)
+        scale = jnp.sum(jnp.where(lane == expert, table, 0.0), axis=1, keepdims=True)
+        out = jnp.dot(hidden, down_ref[...], preferred_element_type=jnp.float32)
+        out_ref[...] = (out * scale).astype(jnp.bfloat16)
+
+    return in_vmem(body, shape(count, width), 2 * count * width * hid, x, part, other, w_down)
+
+
+def after(value, *others):
+    return lax.optimization_barrier((value, *others))[0]
+
+
+def dense_on_device(tokens, expert_ids, affinity, w_gate, w_up, w_down):
+    node_count = lax.axis_size("node")
+    local_count = lax.axis_size("local")
+    group_size = local_count // 2
+    tok_count, _ = expert_ids.shape
+    rows = tok_count // local_count
+    my_local = lax.axis_index("local")
+    far = list(range(node_count - 1, 1, -1))
+
+    def quarter(value, j):
+        return lax.dynamic_slice_in_dim(value, (my_local ^ j) * rows, rows, 0)
+
+    def experts(x):
+        part = project(x, w_gate[0], w_up[0])
+        return finish(x, part, swap(part, "cuts", 1), w_down[0], group_size)
+
+    def gathered(value):
+        others = [swap(value, "local", j) for j in range(1, local_count)]
+        return jnp.concatenate([value] + others, axis=0)
+
+    def reduced(blocks):
+        total = blocks[0].astype(jnp.float32)
+        for j in range(1, local_count):
+            total = total + swap(blocks[j], "local", j).astype(jnp.float32)
+        return total
+
+    def split(value):
+        step = value.shape[0] // local_count
+        return [value[j * step : (j + 1) * step] for j in range(local_count)]
+
+    everything, own = prepare(tokens, expert_ids, affinity, rows)
+    arrived = dict(zip(far, lax.optimization_barrier([swap(own, "node", k) for k in far])))
+    near = swap(everything, "node", 1)
+    out_own = experts(everything)
+    x = gathered(jnp.concatenate([arrived[k] for k in far], axis=0))
+    out_near = experts(near)
+    x = after(x, out_own, out_near)
+    out_far = experts(x)
+    near_back = swap(out_near, "node", 1)
+    part = reduced(split(out_far)).astype(jnp.bfloat16)
+    back = {k: swap(part[i * rows : (i + 1) * rows], "node", k) for i, k in enumerate(far)}
+    both = (out_own.astype(jnp.float32) + near_back.astype(jnp.float32)).astype(jnp.bfloat16)
+    own_blocks = [quarter(both, j) for j in range(local_count)]
+    later = [swap(own_blocks[j], "local", j) for j in range(1, local_count)]
+    total = sum(back[k].astype(jnp.float32) for k in far)
+    total, *later = lax.optimization_barrier((total, *later))
+    for value in [own_blocks[0], *later]:
+        total = total + value.astype(jnp.float32)
+    return total.astype(jnp.bfloat16)
+
+
+def slots_on_device(tokens, expert_ids, affinity, w_gate, w_up, w_down):
     node_count = lax.axis_size("node")
     local_count = lax.axis_size("local")
     group_size = local_count // 2
@@ -28,8 +187,7 @@
     outgoing = jnp.einsum(
         "tmc,td->mcd", dispatch.astype(jnp.bfloat16), tokens, preferred_element_type=jnp.float32
     ).astype(jnp.bfloat16)
-    affinity_sum = jnp.sum(affinity, axis=1, keepdims=True)
-    route_share = (2.5 * affinity / affinity_sum).astype(jnp.bfloat16).astype(jnp.float32)
+    route_share = route_shares(affinity)
     pair_range = jnp.arange(2, dtype=jnp.int32)
     expert_grid = 2 * node_range[:, None] + pair_range[None, :]
     own_route = expert_ids[:, :, None, None] == expert_grid[None, None, :, :]
@@ -59,6 +217,18 @@
     return summed.astype(jnp.bfloat16)
 
 
+def on_device(tokens, expert_ids, affinity, w_gate, w_up, w_down):
+    node_count = lax.axis_size("node")
+    local_count = lax.axis_size("local")
+    tok_count, top_count = expert_ids.shape
+    expert_count = 2 * node_count
+    capacity = (5 * tok_count * top_count + 4 * expert_count - 1) // (4 * expert_count)
+    powers = all(size & (size - 1) == 0 for size in (node_count, local_count))
+    everywhere = node_count == top_count // 2 and capacity >= tok_count and expert_count <= LANES
+    chosen = dense_on_device if everywhere and powers and tok_count % local_count == 0 else slots_on_device
+    return chosen(tokens, expert_ids, affinity, w_gate, w_up, w_down)
+
+
 def solution(mesh):
     return jax.shard_map(
         on_device,

time: 183 us -> 57 us (0.31)
  blocking collectives: 81.3 us -> 0 us
  waiting for transfers between devices: 64.8 us -> 23.8 us
  starting transfers between devices: 3.27 us -> 21.2 us
  between operations: 13.5 us -> 0.19 us
  matrix products: 12.3 us -> 0 us
  Pallas kernels: 0 us -> 5.13 us
    all_to_all x3 -> x0, blocking collectives: 81.3 us -> none  [the longest x1 46.4 us: on_device(): lax.all_to_all(outgoing, 'node', split_axis=0, concat_axis=0, tiled=True)]
    reduce_scatter x1 -> x0, waiting for transfers between devices: 49.7 us -> none  [on_device(): lax.psum_scatter(weighted, 'local', scatter_dimension=2, tiled=True)]
    ppermute x0 -> x18, waiting for transfers between devices: none -> 23.8 us  [swap(): return lax.ppermute(value, axis, [(i, i ^ bits) for i in range(size)])]
    ppermute x0 -> x18, starting transfers between devices: none -> 21.2 us  [swap(): return lax.ppermute(value, axis, [(i, i ^ bits) for i in range(size)])]
    dot_general x7 -> x0, matrix products: 12.3 us -> none  [the longest x1 4.47 us: on_device(): slice_out = jnp.dot(hidden, w_down[0], preferred_element_type=jnp.float32)]
    psum x1 -> x0, waiting for transfers between devices: 9.72 us -> none  [on_device(): gate_full, up_full = lax.psum((gate_part, up_part), 'cuts')]
    all_to_all x1 -> x0, waiting for transfers between devices: 5.36 us -> none  [on_device(): lax.all_to_all(slot_weight, 'node', split_axis=0, concat_axis=0, tiled=True)]
    pallas_call x0 -> x7, Pallas kernels: none -> 5.13 us  [the longest x6 4.89 us: in_vmem(): pl.pallas_call(body, out_shape=out_shapes, in_specs=[pl.BlockSpec(memory_...]
  transfers between devices with their start and end apart: 3 -> 18, of which waited for: 3 -> 9; matrix products, arithmetic and copies ran while one was open for 1% -> 0% of each run, Pallas kernels for 0% -> 6%
where the time goes in v2:
time: 57 us; the launch traced here: 56.7 us
  waiting for transfers between devices  23.8 us (42%)
  starting transfers between devices  21.2 us (37%)
  local copies, waits for them, and re-layouts  5.53 us (10%)
  Pallas kernels  5.13 us (9%)
  other arithmetic  0.89 us (2%)
    ppermute x18, waiting for transfers between devices, swap(): return lax.ppermute(value, axis, [(i, i ^ bits) for i in range(size)])  23.8 us
    ppermute x18, starting transfers between devices, swap(): return lax.ppermute(value, axis, [(i, i ^ bits) for i in range(size)])  21.2 us
    unnamed x21, local copies, waits for them, and re-layouts  5.42 us
    pallas_call x6, Pallas kernels, in_vmem(): pl.pallas_call(body, out_shape=out_shapes, in_specs=[pl.BlockSpec(memory_...  4.89 us
  transfers between devices with their start and end apart: 18, of which 9 were waited for; matrix products, arithmetic and copies ran while one was open for 0% of the time, Pallas kernels for 6%

profile of v2, /device:TPU:0, one launch (start us, length us, event | category | flops | bytes accessed | tf_op | source)
XLA Modules:
  0.0 56.7 jit_solution(462832655769613697)
XLA Ops:
  0.0 1.0 %copy-done.5 = bf16[96,1792]{1,0:T(8,128)(2,1)S(1)} copy-done((bf16[96,1792]{1,0:T(8,128)(2,1)S(1)}, bf16[96,1792]{1,0:T(8,128)(2,1)}, u32[]{:S(2)}) %copy-start.5) | copy-done | bytes 344088
  1.0 0.7 %copy-done.7 = s32[96,8]{0,1:T(8,128)S(1)} copy-done((s32[96,8]{0,1:T(8,128)S(1)}, s32[96,8]{0,1:T(8,128)}, u32[]{:S(2)}) %copy-start.7) | copy-done | bytes 3096
  1.7 0.7 %copy-done.8 = f32[96,8]{0,1:T(8,128)S(1)} copy-done((f32[96,8]{0,1:T(8,128)S(1)}, f32[96,8]{0,1:T(8,128)}, u32[]{:S(2)}) %copy-start.8) | copy-done | bytes 3096
  2.6 5.1 %collective-permute-start = (bf16[24,1920]{1,0:T(8,128)(2,1)S(1)}, bf16[24,1920]{1,0:T(8,128)(2,1)S(1)}, u32[]{:S(2)}, u32[]{:S(2)}) collective-permute-start(bf16[24,1920]{1,0:T(8,128)(2,1)S(1)} %get-tuple-element.14), channel_id=1, source_target_pairs={{0,24},{8,16},{16,8},{24,0},{1,25},{9,17},{17,9},{25,1},{2,26},{10... | collective-permute-start | bytes 276488 | tf_op jit(solution)/shard_map/ppermute | solution.py:13
  7.7 1.5 %copy-done = bf16[1,1792,512]{2,1,0:T(8,128)(2,1)S(1)} copy-done((bf16[1,1792,512]{2,1,0:T(8,128)(2,1)S(1)}, bf16[1,1792,512]{2,1,0:T(8,128)(2,1)}, u32[]{:S(2)}) %copy-start) | copy-done | bytes 1835032
  9.2 1.5 %copy-done.2 = bf16[1,1792,512]{2,1,0:T(8,128)(2,1)S(1)} copy-done((bf16[1,1792,512]{2,1,0:T(8,128)(2,1)S(1)}, bf16[1,1792,512]{2,1,0:T(8,128)(2,1)}, u32[]{:S(2)}) %copy-start.2) | copy-done | bytes 1835032
  10.7 0.7 %shard_map.65.part_ref = bf16[96,1024]{1,0:T(8,128)(2,1)S(1)} custom-call(bf16[96,1920]{1,0:T(8,128)(2,1)S(1)} %get-tuple-element.17.x_ref, bf16[1792,512]{1,0:T(8,128)(2,1)S(1)} %bitcast.5, bf16[1792,512]{1,0:T(8,128)(2,1)S(1)} %bitcast.8), custom_call_target="tpu_custom_call" | custom-call | flops 352321536 | bytes 1048576 | tf_op jit(solution)/shard_map/pallas_call | solution.py:22
  11.5 3.9 %collective-permute-done.1 = bf16[24,1920]{1,0:T(8,128)(2,1)S(1)} collective-permute-done((bf16[24,1920]{1,0:T(8,128)(2,1)S(1)}, bf16[24,1920]{1,0:T(8,128)(2,1)S(1)}, u32[]{:S(2)}, u32[]{:S(2)}) %collective-permute-start.1) | collective-permute-done | bytes 92192 | tf_op jit(solution)/shard_map/ppermute | solution.py:13
  15.5 1.6 %collective-permute-start.2 = (bf16[48,1920]{1,0:T(8,128)(2,1)S(1)}, bf16[48,1920]{1,0:T(8,128)(2,1)S(1)}, u32[]{:S(2)}, u32[]{:S(2)}) collective-permute-start(bf16[48,1920]{1,0:T(8,128)(2,1)S(1)} %get-tuple-element.31), channel_id=1, source_target_pairs={{0,2},{2,0},{4,6},{6,4},{1,3},{3,1},{5,7},{7,5},{8,10},{10,8},{12,... | collective-permute-start | bytes 552968 | tf_op jit(solution)/shard_map/ppermute | solution.py:13
  17.1 1.5 %collective-permute-start.3 = (bf16[48,1920]{1,0:T(8,128)(2,1)S(1)}, bf16[48,1920]{1,0:T(8,128)(2,1)S(1)}, u32[]{:S(2)}, u32[]{:S(2)}) collective-permute-start(bf16[48,1920]{1,0:T(8,128)(2,1)S(1)} %get-tuple-element.31), channel_id=1, source_target_pairs={{0,4},{2,6},{4,0},{6,2},{1,5},{3,7},{5,1},{7,3},{8,12},{10,14},{12... | collective-permute-start | bytes 552968 | tf_op jit(solution)/shard_map/ppermute | solution.py:13
  18.6 0.5 collective-permute-start.4
  19.1 0.5 shard_map.66
  19.5 3.3 %collective-permute-done.2 = bf16[48,1920]{1,0:T(8,128)(2,1)S(1)} collective-permute-done((bf16[48,1920]{1,0:T(8,128)(2,1)S(1)}, bf16[48,1920]{1,0:T(8,128)(2,1)S(1)}, u32[]{:S(2)}, u32[]{:S(2)}) %collective-permute-start.2) | collective-permute-done | bytes 184352 | tf_op jit(solution)/shard_map/ppermute | solution.py:13
  22.9 3.7 %collective-permute-done.3 = bf16[48,1920]{1,0:T(8,128)(2,1)S(1)} collective-permute-done((bf16[48,1920]{1,0:T(8,128)(2,1)S(1)}, bf16[48,1920]{1,0:T(8,128)(2,1)S(1)}, u32[]{:S(2)}, u32[]{:S(2)}) %collective-permute-start.3) | collective-permute-done | bytes 184352 | tf_op jit(solution)/shard_map/ppermute | solution.py:13
  26.6 0.7 %shard_map.67.part_ref = bf16[96,1024]{1,0:T(8,128)(2,1)S(1)} custom-call(bf16[96,1920]{1,0:T(8,128)(2,1)S(1)} %collective-permute-done.6.x_ref, bf16[1792,512]{1,0:T(8,128)(2,1)S(1)} %bitcast.6, bf16[1792,512]{1,0:T(8,128)(2,1)S(1)} %bitcast.9), custom_call_target="tpu_custom_call" | custom-call | flops 352321536 | bytes 1048576 | tf_op jit(solution)/shard_map/pallas_call | solution.py:22
  27.4 1.4 %collective-permute-done.7.other_ref = bf16[96,1024]{1,0:T(8,128)(2,1)S(1)} collective-permute-done((bf16[96,1024]{1,0:T(8,128)(2,1)S(1)}, bf16[96,1024]{1,0:T(8,128)(2,1)S(1)}, u32[]{:S(2)}, u32[]{:S(2)}) %collective-permute-start.7) | collective-permute-done | bytes 196640 | tf_op jit(solution)/shard_map/ppermute | solution.py:13
  29.3 0.9 %shard_map.69.part_ref = bf16[192,1024]{1,0:T(8,128)(2,1)S(1)} custom-call(bf16[192,1920]{1,0:T(8,128)(2,1)S(1)} %constant_dynamic-update-slice_fusion.2.x_ref, bf16[1792,512]{1,0:T(8,128)(2,1)S(1)} %bitcast.7, bf16[1792,512]{1,0:T(8,128)(2,1)S(1)} %bitcast.10), custom_call_target="tpu_custom_call" | custom-call | flops 704643072 | bytes 1048576 | tf_op jit(solution)/shard_map/pallas_call | solution.py:22
  30.4 1.8 %collective-permute-start.14 = (bf16[96,1792]{1,0:T(8,128)(2,1)}, bf16[96,1792]{1,0:T(8,128)(2,1)S(1)}, u32[]{:S(2)}, u32[]{:S(2)}) collective-permute-start(bf16[96,1792]{1,0:T(8,128)(2,1)} %copy-done.6), channel_id=1, source_target_pairs={{0,8},{8,0},{16,24},{24,16},{1,9},{9,1},{17,25},{25,17},{2,10},{10... | collective-permute-start | bytes 1032200 | tf_op jit(solution)/shard_map/ppermute | solution.py:13
  32.2 1.6 %shard_map.70 = bf16[192,1792]{1,0:T(8,128)(2,1)S(1)} custom-call(bf16[192,1920]{1,0:T(8,128)(2,1)S(1)} %constant_dynamic-update-slice_fusion.2.x_ref, bf16[192,1024]{1,0:T(8,128)(2,1)S(1)} %shard_map.69.part_ref, bf16[192,1024]{1,0:T(8,128)(2,1)} %collective-permute-done.8.other_ref, bf16[512,1792]{1,0:T(8,128)(2,1)S(1)} %bitcast.13), custom_call_target="tpu_custom_call" | custom-call | flops 352321536 | bytes 1048576 | tf_op jit(solution)/shard_map/pallas_call | solution.py:22
  33.9 1.4 %collective-permute-start.10 = (bf16[48,1792]{1,0:T(8,128)(2,1)S(1)}, bf16[48,1792]{1,0:T(8,128)(2,1)S(1)}, u32[]{:S(2)}, u32[]{:S(2)}) collective-permute-start(bf16[48,1792]{1,0:T(8,128)(2,1)S(1)} %get-tuple-element.25), channel_id=1, source_target_pairs={{0,4},{2,6},{4,0},{6,2},{1,5},{3,7},{5,1},{7,3},{8,12},{10,14},{12... | collective-permute-start | bytes 516104 | tf_op jit(solution)/shard_map/ppermute | solution.py:13
  35.3 0.8 %collective-permute-start.11 = (bf16[48,1792]{1,0:T(8,128)(2,1)S(1)}, bf16[48,1792]{1,0:T(8,128)(2,1)S(1)}, u32[]{:S(2)}, u32[]{:S(2)}) collective-permute-start(bf16[48,1792]{1,0:T(8,128)(2,1)S(1)} %get-tuple-element.24), channel_id=1, source_target_pairs={{0,6},{2,4},{4,2},{6,0},{1,7},{3,5},{5,3},{7,1},{8,14},{10,12},{12... | collective-permute-start | bytes 516104 | tf_op jit(solution)/shard_map/ppermute | solution.py:13
  36.1 1.3 %collective-permute-start.9 = (bf16[48,1792]{1,0:T(8,128)(2,1)S(1)}, bf16[48,1792]{1,0:T(8,128)(2,1)S(1)}, u32[]{:S(2)}, u32[]{:S(2)}) collective-permute-start(bf16[48,1792]{1,0:T(8,128)(2,1)S(1)} %get-tuple-element.23), channel_id=1, source_target_pairs={{0,2},{2,0},{4,6},{6,4},{1,3},{3,1},{5,7},{7,5},{8,10},{10,8},{12,... | collective-permute-start | bytes 516104 | tf_op jit(solution)/shard_map/ppermute | solution.py:13
  37.5 3.5 %collective-permute-done.14 = bf16[96,1792]{1,0:T(8,128)(2,1)S(1)} collective-permute-done((bf16[96,1792]{1,0:T(8,128)(2,1)}, bf16[96,1792]{1,0:T(8,128)(2,1)S(1)}, u32[]{:S(2)}, u32[]{:S(2)}) %collective-permute-start.14) | collective-permute-done | bytes 344096 | tf_op jit(solution)/shard_map/ppermute | solution.py:13
  41.1 2.9 %collective-permute-done.10 = bf16[48,1792]{1,0:T(8,128)(2,1)S(1)} collective-permute-done((bf16[48,1792]{1,0:T(8,128)(2,1)S(1)}, bf16[48,1792]{1,0:T(8,128)(2,1)S(1)}, u32[]{:S(2)}, u32[]{:S(2)}) %collective-permute-start.10) | collective-permute-done | bytes 172064 | tf_op jit(solution)/shard_map/ppermute | solution.py:13
  44.0 1.2 %collective-permute-done.9 = bf16[48,1792]{1,0:T(8,128)(2,1)S(1)} collective-permute-done((bf16[48,1792]{1,0:T(8,128)(2,1)S(1)}, bf16[48,1792]{1,0:T(8,128)(2,1)S(1)}, u32[]{:S(2)}, u32[]{:S(2)}) %collective-permute-start.9) | collective-permute-done | bytes 172064 | tf_op jit(solution)/shard_map/ppermute | solution.py:13
  45.4 2.5 %collective-permute-start.12 = (bf16[24,1792]{1,0:T(8,128)(2,1)S(1)}, bf16[24,1792]{1,0:T(8,128)(2,1)S(1)}, u32[]{:S(2)}, u32[]{:S(2)}) collective-permute-start(bf16[24,1792]{1,0:T(8,128)(2,1)S(1)} %get-tuple-element.29), channel_id=1, source_target_pairs={{0,24},{8,16},{16,8},{24,0},{1,25},{9,17},{17,9},{25,1},{2,26},{10... | collective-permute-start | bytes 258056 | tf_op jit(solution)/shard_map/ppermute | solution.py:13
  47.8 0.8 %collective-permute-start.13 = (bf16[24,1792]{1,0:T(8,128)(2,1)S(1)}, bf16[24,1792]{1,0:T(8,128)(2,1)S(1)}, u32[]{:S(2)}, u32[]{:S(2)}) collective-permute-start(bf16[24,1792]{1,0:T(8,128)(2,1)S(1)} %get-tuple-element.30), channel_id=1, source_target_pairs={{0,16},{8,24},{16,0},{24,8},{1,17},{9,25},{17,1},{25,9},{2,18},{10... | collective-permute-start | bytes 258056 | tf_op jit(solution)/shard_map/ppermute | solution.py:13
  48.7 0.8 %collective-permute-start.15 = (bf16[24,1792]{1,0:T(8,128)(2,1)S(1)}, bf16[24,1792]{1,0:T(8,128)(2,1)S(1)}, u32[]{:S(2)}, u32[]{:S(2)}) collective-permute-start(bf16[24,1792]{1,0:T(8,128)(2,1)S(1)} %get-tuple-element.28), channel_id=1, source_target_pairs={{0,2},{2,0},{4,6},{6,4},{1,3},{3,1},{5,7},{7,5},{8,10},{10,8},{12,... | collective-permute-start | bytes 258056 | tf_op jit(solution)/shard_map/ppermute | solution.py:13
  49.4 1.2 %collective-permute-start.16 = (bf16[24,1792]{1,0:T(8,128)(2,1)S(1)}, bf16[24,1792]{1,0:T(8,128)(2,1)S(1)}, u32[]{:S(2)}, u32[]{:S(2)}) collective-permute-start(bf16[24,1792]{1,0:T(8,128)(2,1)S(1)} %get-tuple-element.27), channel_id=1, source_target_pairs={{0,4},{2,6},{4,0},{6,2},{1,5},{3,7},{5,1},{7,3},{8,12},{10,14},{12... | collective-permute-start | bytes 258056 | tf_op jit(solution)/shard_map/ppermute | solution.py:13
  50.6 1.6 %collective-permute-start.17 = (bf16[24,1792]{1,0:T(8,128)(2,1)S(1)}, bf16[24,1792]{1,0:T(8,128)(2,1)S(1)}, u32[]{:S(2)}, u32[]{:S(2)}) collective-permute-start(bf16[24,1792]{1,0:T(8,128)(2,1)S(1)} %get-tuple-element.26), channel_id=1, source_target_pairs={{0,6},{2,4},{4,2},{6,0},{1,7},{3,5},{5,3},{7,1},{8,14},{10,12},{12... | collective-permute-start | bytes 258056 | tf_op jit(solution)/shard_map/ppermute | solution.py:13
  52.2 3.4 %collective-permute-done.13 = bf16[24,1792]{1,0:T(8,128)(2,1)S(1)} collective-permute-done((bf16[24,1792]{1,0:T(8,128)(2,1)S(1)}, bf16[24,1792]{1,0:T(8,128)(2,1)S(1)}, u32[]{:S(2)}, u32[]{:S(2)}) %collective-permute-start.13) | collective-permute-done | bytes 86048 | tf_op jit(solution)/shard_map/ppermute | solution.py:13
  56.0 0.7 %add_convert_fusion.2 = bf16[24,1792]{1,0:T(8,128)(2,1)} fusion(bf16[24,1792]{1,0:T(8,128)(2,1)S(1)} %collective-permute-done.17, bf16[24,1792]{1,0:T(8,128)(2,1)S(1)} %collective-permute-done.16, bf16[24,1792]{1,0:T(8,128)(2,1)S(1)} %collective-permute-done.15, f32[24,1792]{1,0:T(8,128)S(1)} %convert_add_fusion, bf16[96,1792]{1,0:T(8,128)(2,1)S(1)} %add_convert_fusion, ...), kind=kLoop, calls=%fused_computation.2 | loop fusion | flops 387072 | bytes 602116 | tf_op jit(solution)/shard_map/convert_element_type | solution.py:163
  (41 shorter events, 1.8 us)
Async XLA Ops:
  0.0 1.0 %copy-start.5 = (bf16[96,1792]{1,0:T(8,128)(2,1)S(1)}, bf16[96,1792]{1,0:T(8,128)(2,1)}, u32[]{:S(2)}) copy-start(bf16[96,1792]{1,0:T(8,128)(2,1)} %tokens_hbm.1) | copy-start | bytes 1032196
  1.0 0.7 %copy-start.7 = (s32[96,8]{0,1:T(8,128)S(1)}, s32[96,8]{0,1:T(8,128)}, u32[]{:S(2)}) copy-start(s32[96,8]{0,1:T(8,128)} %param.7) | copy-start | bytes 9220
  1.7 0.7 %copy-start.8 = (f32[96,8]{0,1:T(8,128)S(1)}, f32[96,8]{0,1:T(8,128)}, u32[]{:S(2)}) copy-start(f32[96,8]{0,1:T(8,128)} %param.8) | copy-start | bytes 9220
  2.6 8.9 %collective-permute-start = (bf16[24,1920]{1,0:T(8,128)(2,1)S(1)}, bf16[24,1920]{1,0:T(8,128)(2,1)S(1)}, u32[]{:S(2)}, u32[]{:S(2)}) collective-permute-start(bf16[24,1920]{1,0:T(8,128)(2,1)S(1)} %get-tuple-element.14), channel_id=1, source_target_pairs={{0,24},{8,16},{16,8},{24,0},{1,25},{9,17},{17,9},{25,1},{2,26},{10... | collective-permute-start | bytes 276488 | tf_op jit(solution)/shard_map/ppermute | solution.py:13
  7.7 7.7 %collective-permute-start.1 = (bf16[24,1920]{1,0:T(8,128)(2,1)S(1)}, bf16[24,1920]{1,0:T(8,128)(2,1)S(1)}, u32[]{:S(2)}, u32[]{:S(2)}) collective-permute-start(bf16[24,1920]{1,0:T(8,128)(2,1)S(1)} %get-tuple-element.14), channel_id=1, source_target_pairs={{0,16},{8,24},{16,0},{24,8},{1,17},{9,25},{17,1},{25,9},{2,18},{10... | collective-permute-start | bytes 276488 | tf_op jit(solution)/shard_map/ppermute | solution.py:13
  7.7 1.5 %copy-start = (bf16[1,1792,512]{2,1,0:T(8,128)(2,1)S(1)}, bf16[1,1792,512]{2,1,0:T(8,128)(2,1)}, u32[]{:S(2)}) copy-start(bf16[1,1792,512]{2,1,0:T(8,128)(2,1)} %param.9) | copy-start | bytes 5505028
  9.2 1.5 %copy-start.2 = (bf16[1,1792,512]{2,1,0:T(8,128)(2,1)S(1)}, bf16[1,1792,512]{2,1,0:T(8,128)(2,1)}, u32[]{:S(2)}) copy-start(bf16[1,1792,512]{2,1,0:T(8,128)(2,1)} %param.10) | copy-start | bytes 5505028
  10.7 8.3 %copy-start.4 = (bf16[1,512,1792]{2,1,0:T(8,128)(2,1)S(1)}, bf16[1,512,1792]{2,1,0:T(8,128)(2,1)}, u32[]{:S(2)}) copy-start(bf16[1,512,1792]{2,1,0:T(8,128)(2,1)} %param.11) | copy-start | bytes 5505028
  11.4 7.6 %collective-permute-start.5 = (bf16[96,1024]{1,0:T(8,128)(2,1)S(1)}, bf16[96,1024]{1,0:T(8,128)(2,1)S(1)}, u32[]{:S(2)}, u32[]{:S(2)}) collective-permute-start(bf16[96,1024]{1,0:T(8,128)(2,1)S(1)} %shard_map.65.part_ref), channel_id=1, source_target_pairs={{0,1},{1,0},{2,3},{3,2},{4,5},{5,4},{6,7},{7,6},{8,9},{9,8},{10,11... | collective-permute-start | bytes 589832 | tf_op jit(solution)/shard_map/ppermute | solution.py:13
  15.5 7.4 %collective-permute-start.2 = (bf16[48,1920]{1,0:T(8,128)(2,1)S(1)}, bf16[48,1920]{1,0:T(8,128)(2,1)S(1)}, u32[]{:S(2)}, u32[]{:S(2)}) collective-permute-start(bf16[48,1920]{1,0:T(8,128)(2,1)S(1)} %get-tuple-element.31), channel_id=1, source_target_pairs={{0,2},{2,0},{4,6},{6,4},{1,3},{3,1},{5,7},{7,5},{8,10},{10,8},{12,... | collective-permute-start | bytes 552968 | tf_op jit(solution)/shard_map/ppermute | solution.py:13
  17.1 9.5 %collective-permute-start.6 = (bf16[96,1920]{1,0:T(8,128)(2,1)S(1)}, bf16[96,1920]{1,0:T(8,128)(2,1)S(1)}, u32[]{:S(2)}, u32[]{:S(2)}) collective-permute-start(bf16[96,1920]{1,0:T(8,128)(2,1)S(1)} %get-tuple-element.17.x_ref), channel_id=1, source_target_pairs={{0,8},{8,0},{16,24},{24,16},{1,9},{9,1},{17,25},{25,17},{2,10},{10... | collective-permute-start | bytes 1105928 | tf_op jit(solution)/shard_map/ppermute | solution.py:13
  17.1 9.5 %collective-permute-start.3 = (bf16[48,1920]{1,0:T(8,128)(2,1)S(1)}, bf16[48,1920]{1,0:T(8,128)(2,1)S(1)}, u32[]{:S(2)}, u32[]{:S(2)}) collective-permute-start(bf16[48,1920]{1,0:T(8,128)(2,1)S(1)} %get-tuple-element.31), channel_id=1, source_target_pairs={{0,4},{2,6},{4,0},{6,2},{1,5},{3,7},{5,1},{7,3},{8,12},{10,14},{12... | collective-permute-start | bytes 552968 | tf_op jit(solution)/shard_map/ppermute | solution.py:13
  18.6 8.8 %collective-permute-start.4 = (bf16[48,1920]{1,0:T(8,128)(2,1)S(1)}, bf16[48,1920]{1,0:T(8,128)(2,1)S(1)}, u32[]{:S(2)}, u32[]{:S(2)}) collective-permute-start(bf16[48,1920]{1,0:T(8,128)(2,1)S(1)} %get-tuple-element.31), channel_id=1, source_target_pairs={{0,6},{2,4},{4,2},{6,0},{1,7},{3,5},{5,3},{7,1},{8,14},{10,12},{12... | collective-permute-start | bytes 552968 | tf_op jit(solution)/shard_map/ppermute | solution.py:13
  19.1 7.5 %copy-start.1 = (bf16[1,1792,512]{2,1,0:T(8,128)(2,1)S(1)}, bf16[1,1792,512]{2,1,0:T(8,128)(2,1)}, u32[]{:S(2)}) copy-start(bf16[1,1792,512]{2,1,0:T(8,128)(2,1)} %param.9) | copy-start | bytes 5505028
  19.1 7.5 %copy-start.3 = (bf16[1,1792,512]{2,1,0:T(8,128)(2,1)S(1)}, bf16[1,1792,512]{2,1,0:T(8,128)(2,1)}, u32[]{:S(2)}) copy-start(bf16[1,1792,512]{2,1,0:T(8,128)(2,1)} %param.10) | copy-start | bytes 5505028
  27.3 1.5 %collective-permute-start.7 = (bf16[96,1024]{1,0:T(8,128)(2,1)S(1)}, bf16[96,1024]{1,0:T(8,128)(2,1)S(1)}, u32[]{:S(2)}, u32[]{:S(2)}) collective-permute-start(bf16[96,1024]{1,0:T(8,128)(2,1)S(1)} %shard_map.67.part_ref), channel_id=1, source_target_pairs={{0,1},{1,0},{2,3},{3,2},{4,5},{5,4},{6,7},{7,6},{8,9},{9,8},{10,11... | collective-permute-start | bytes 589832 | tf_op jit(solution)/shard_map/ppermute | solution.py:13
  29.3 0.9 %copy-start.6 = (bf16[96,1792]{1,0:T(8,128)(2,1)}, bf16[96,1792]{1,0:T(8,128)(2,1)S(1)}, u32[]{:S(2)}) copy-start(bf16[96,1792]{1,0:T(8,128)(2,1)S(1)} %shard_map.68) | copy-start | bytes 1032196
  30.2 2.0 %collective-permute-start.8 = (bf16[192,1024]{1,0:T(8,128)(2,1)S(1)}, bf16[192,1024]{1,0:T(8,128)(2,1)}, u32[]{:S(2)}, u32[]{:S(2)}) collective-permute-start(bf16[192,1024]{1,0:T(8,128)(2,1)S(1)} %shard_map.69.part_ref), channel_id=1, source_target_pairs={{0,1},{1,0},{2,3},{3,2},{4,5},{5,4},{6,7},{7,6},{8,9},{9,8},{10,11... | collective-permute-start | bytes 1179656 | tf_op jit(solution)/shard_map/ppermute | solution.py:13
  30.4 10.6 %collective-permute-start.14 = (bf16[96,1792]{1,0:T(8,128)(2,1)}, bf16[96,1792]{1,0:T(8,128)(2,1)S(1)}, u32[]{:S(2)}, u32[]{:S(2)}) collective-permute-start(bf16[96,1792]{1,0:T(8,128)(2,1)} %copy-done.6), channel_id=1, source_target_pairs={{0,8},{8,0},{16,24},{24,16},{1,9},{9,1},{17,25},{25,17},{2,10},{10... | collective-permute-start | bytes 1032200 | tf_op jit(solution)/shard_map/ppermute | solution.py:13
  33.9 10.1 %collective-permute-start.10 = (bf16[48,1792]{1,0:T(8,128)(2,1)S(1)}, bf16[48,1792]{1,0:T(8,128)(2,1)S(1)}, u32[]{:S(2)}, u32[]{:S(2)}) collective-permute-start(bf16[48,1792]{1,0:T(8,128)(2,1)S(1)} %get-tuple-element.25), channel_id=1, source_target_pairs={{0,4},{2,6},{4,0},{6,2},{1,5},{3,7},{5,1},{7,3},{8,12},{10,14},{12... | collective-permute-start | bytes 516104 | tf_op jit(solution)/shard_map/ppermute | solution.py:13
  35.3 8.7 %collective-permute-start.11 = (bf16[48,1792]{1,0:T(8,128)(2,1)S(1)}, bf16[48,1792]{1,0:T(8,128)(2,1)S(1)}, u32[]{:S(2)}, u32[]{:S(2)}) collective-permute-start(bf16[48,1792]{1,0:T(8,128)(2,1)S(1)} %get-tuple-element.24), channel_id=1, source_target_pairs={{0,6},{2,4},{4,2},{6,0},{1,7},{3,5},{5,3},{7,1},{8,14},{10,12},{12... | collective-permute-start | bytes 516104 | tf_op jit(solution)/shard_map/ppermute | solution.py:13
  36.1 9.1 %collective-permute-start.9 = (bf16[48,1792]{1,0:T(8,128)(2,1)S(1)}, bf16[48,1792]{1,0:T(8,128)(2,1)S(1)}, u32[]{:S(2)}, u32[]{:S(2)}) collective-permute-start(bf16[48,1792]{1,0:T(8,128)(2,1)S(1)} %get-tuple-element.23), channel_id=1, source_target_pairs={{0,2},{2,0},{4,6},{6,4},{1,3},{3,1},{5,7},{7,5},{8,10},{10,8},{12,... | collective-permute-start | bytes 516104 | tf_op jit(solution)/shard_map/ppermute | solution.py:13
  45.4 6.9 %collective-permute-start.12 = (bf16[24,1792]{1,0:T(8,128)(2,1)S(1)}, bf16[24,1792]{1,0:T(8,128)(2,1)S(1)}, u32[]{:S(2)}, u32[]{:S(2)}) collective-permute-start(bf16[24,1792]{1,0:T(8,128)(2,1)S(1)} %get-tuple-element.29), channel_id=1, source_target_pairs={{0,24},{8,16},{16,8},{24,0},{1,25},{9,17},{17,9},{25,1},{2,26},{10... | collective-permute-start | bytes 258056 | tf_op jit(solution)/shard_map/ppermute | solution.py:13
  47.8 7.8 %collective-permute-start.13 = (bf16[24,1792]{1,0:T(8,128)(2,1)S(1)}, bf16[24,1792]{1,0:T(8,128)(2,1)S(1)}, u32[]{:S(2)}, u32[]{:S(2)}) collective-permute-start(bf16[24,1792]{1,0:T(8,128)(2,1)S(1)} %get-tuple-element.30), channel_id=1, source_target_pairs={{0,16},{8,24},{16,0},{24,8},{1,17},{9,25},{17,1},{25,9},{2,18},{10... | collective-permute-start | bytes 258056 | tf_op jit(solution)/shard_map/ppermute | solution.py:13
  48.7 7.0 %collective-permute-start.15 = (bf16[24,1792]{1,0:T(8,128)(2,1)S(1)}, bf16[24,1792]{1,0:T(8,128)(2,1)S(1)}, u32[]{:S(2)}, u32[]{:S(2)}) collective-permute-start(bf16[24,1792]{1,0:T(8,128)(2,1)S(1)} %get-tuple-element.28), channel_id=1, source_target_pairs={{0,2},{2,0},{4,6},{6,4},{1,3},{3,1},{5,7},{7,5},{8,10},{10,8},{12,... | collective-permute-start | bytes 258056 | tf_op jit(solution)/shard_map/ppermute | solution.py:13
  49.4 6.2 %collective-permute-start.16 = (bf16[24,1792]{1,0:T(8,128)(2,1)S(1)}, bf16[24,1792]{1,0:T(8,128)(2,1)S(1)}, u32[]{:S(2)}, u32[]{:S(2)}) collective-permute-start(bf16[24,1792]{1,0:T(8,128)(2,1)S(1)} %get-tuple-element.27), channel_id=1, source_target_pairs={{0,4},{2,6},{4,0},{6,2},{1,5},{3,7},{5,1},{7,3},{8,12},{10,14},{12... | collective-permute-start | bytes 258056 | tf_op jit(solution)/shard_map/ppermute | solution.py:13
  50.6 5.4 %collective-permute-start.17 = (bf16[24,1792]{1,0:T(8,128)(2,1)S(1)}, bf16[24,1792]{1,0:T(8,128)(2,1)S(1)}, u32[]{:S(2)}, u32[]{:S(2)}) collective-permute-start(bf16[24,1792]{1,0:T(8,128)(2,1)S(1)} %get-tuple-element.26), channel_id=1, source_target_pairs={{0,6},{2,4},{4,2},{6,0},{1,7},{3,5},{5,3},{7,1},{8,14},{10,12},{12... | collective-permute-start | bytes 258056 | tf_op jit(solution)/shard_map/ppermute | solution.py:13

commit v3 on v2

--- a/solution.py
+++ b/solution.py
@@ -27,6 +27,10 @@
         compiler_params=pltpu.CompilerParams(vmem_limit_bytes=24 * 2**20),
         cost_estimate=pl.CostEstimate(flops=cost, bytes_accessed=2**20, transcendentals=0),
     )(*args)
+
+
+def in_hbm(value):
+    return pltpu.with_memory_space_constraint(value, pltpu.HBM)
 
 
 def shape(*dims):
@@ -74,7 +78,16 @@
         ],
         compiler_params=pltpu.CompilerParams(vmem_limit_bytes=24 * 2**20),
         cost_estimate=pl.CostEstimate(flops=10**6, bytes_accessed=2**20, transcendentals=0),
-    )(tokens, expert_ids.T, affinity.T)
+    )(*(in_hbm(value) for value in (tokens, expert_ids.T, affinity.T)))
+
+
+def project_into(out_ref, rows, weight_refs, copies=()):
+    hid = weight_refs[0].shape[1]
+    for i, ref in enumerate(weight_refs):
+        if copies:
+            copies[i].wait()
+        part = jnp.dot(rows, ref[...], preferred_element_type=jnp.float32)
+        out_ref[:, i * hid : (i + 1) * hid] = part.astype(jnp.bfloat16)
 
 
 def project(x, w_gate, w_up):
@@ -82,12 +95,31 @@
     width, hid = w_gate.shape
 
     def body(x_ref, gate_ref, up_ref, out_ref):
-        rows = x_ref[:, :width]
-        for i, ref in enumerate((gate_ref, up_ref)):
-            part = jnp.dot(rows, ref[...], preferred_element_type=jnp.float32)
-            out_ref[:, i * hid : (i + 1) * hid] = part.astype(jnp.bfloat16)
+        project_into(out_ref, x_ref[:, :width], (gate_ref, up_ref))
 
     return in_vmem(body, shape(count, 2 * hid), 4 * count * width * hid, x, w_gate, w_up)
+
+
+def load_and_project(x, *weights):
+    count = x.shape[0]
+    width, hid = weights[0].shape
+
+    def body(x_ref, gate_hbm, up_hbm, down_hbm, out_ref, gate_ref, up_ref, down_ref, sems):
+        pairs = ((gate_hbm, gate_ref), (up_hbm, up_ref), (down_hbm, down_ref))
+        copies = [pltpu.make_async_copy(src, dst, sems.at[i]) for i, (src, dst) in enumerate(pairs)]
+        for copy in copies:
+            copy.start()
+        project_into(out_ref, x_ref[:, :width], (gate_ref, up_ref), copies)
+        copies[2].wait()
+
+    return pl.pallas_call(
+        body,
+        out_shape=(shape(count, 2 * hid), *(shape(*w.shape) for w in weights)),
+        in_specs=[pl.BlockSpec(memory_space=pltpu.VMEM)] + [pl.BlockSpec(memory_space=pltpu.HBM)] * 3,
+        out_specs=[pl.BlockSpec(memory_space=pltpu.VMEM)] * 4,
+        scratch_shapes=[pltpu.SemaphoreType.DMA((3,))],
+        compiler_params=pltpu.CompilerParams(vmem_limit_bytes=24 * 2**20),
+    )(x, *(in_hbm(w) for w in weights))
 
 
 def finish(x, part, other, w_down, group_size):
@@ -124,43 +156,51 @@
     def quarter(value, j):
         return lax.dynamic_slice_in_dim(value, (my_local ^ j) * rows, rows, 0)
 
-    def experts(x):
-        part = project(x, w_gate[0], w_up[0])
-        return finish(x, part, swap(part, "cuts", 1), w_down[0], group_size)
-
-    def gathered(value):
-        others = [swap(value, "local", j) for j in range(1, local_count)]
-        return jnp.concatenate([value] + others, axis=0)
-
-    def reduced(blocks):
-        total = blocks[0].astype(jnp.float32)
-        for j in range(1, local_count):
-            total = total + swap(blocks[j], "local", j).astype(jnp.float32)
-        return total
-
     def split(value):
         step = value.shape[0] // local_count
         return [value[j * step : (j + 1) * step] for j in range(local_count)]
 
     everything, own = prepare(tokens, expert_ids, affinity, rows)
-    arrived = dict(zip(far, lax.optimization_barrier([swap(own, "node", k) for k in far])))
+    arrived = {k: swap(own, "node", k) for k in far}
     near = swap(everything, "node", 1)
-    out_own = experts(everything)
-    x = gathered(jnp.concatenate([arrived[k] for k in far], axis=0))
-    out_near = experts(near)
-    x = after(x, out_own, out_near)
-    out_far = experts(x)
+    part_own, gate, up, down = load_and_project(everything, w_gate[0], w_up[0], w_down[0])
+
+    def begin(x):
+        part = project(x, gate, up)
+        return x, part, swap(part, "cuts", 1)
+
+    def complete(state, *others):
+        x, part, other = state
+        return finish(x, part, after(other, *others), down, group_size)
+
+    def moved(blocks):
+        return [swap(block, "local", j) for j, block in enumerate(blocks) if j]
+
+    def summed(values):
+        return sum(value.astype(jnp.float32) for value in values)
+
+    arrived[far[0]] = after(arrived[far[0]], part_own)
+    joined = jnp.concatenate([arrived[k] for k in far], axis=0)
+    others = moved([joined] * local_count)
+    near_state = begin(near)
+    others[0] = after(others[0], near_state[1])
+    out_near = complete(near_state)
+    others[1] = after(others[1], out_near)
     near_back = swap(out_near, "node", 1)
-    part = reduced(split(out_far)).astype(jnp.bfloat16)
-    back = {k: swap(part[i * rows : (i + 1) * rows], "node", k) for i, k in enumerate(far)}
+    out_own = complete((everything, part_own, swap(part_own, "cuts", 1)))
+    others[2] = after(others[2], out_own)
+    x = jnp.concatenate([joined, *others], axis=0)
+    out_far = complete(begin(x))
+    blocks = split(out_far)
+    others = moved(blocks)
+    done = summed([blocks[0], *others]).astype(jnp.bfloat16)
+    back = [swap(done[i * rows : (i + 1) * rows], "node", k) for i, k in enumerate(far)]
+    near_back = after(near_back, done)
     both = (out_own.astype(jnp.float32) + near_back.astype(jnp.float32)).astype(jnp.bfloat16)
-    own_blocks = [quarter(both, j) for j in range(local_count)]
-    later = [swap(own_blocks[j], "local", j) for j in range(1, local_count)]
-    total = sum(back[k].astype(jnp.float32) for k in far)
-    total, *later = lax.optimization_barrier((total, *later))
-    for value in [own_blocks[0], *later]:
-        total = total + value.astype(jnp.float32)
-    return total.astype(jnp.bfloat16)
+    blocks = [quarter(both, j) for j in range(local_count)]
+    later = moved(blocks)
+    total, *later = lax.optimization_barrier((summed(back), *later))
+    return (total + summed([blocks[0], *later])).astype(jnp.bfloat16)
 
 
 def slots_on_device(tokens, expert_ids, affinity, w_gate, w_up, w_down):

time: 57 us -> 51 us (0.89)
  local copies, waits for them, and re-layouts: 5.53 us -> 0.18 us
  starting transfers between devices: 21.2 us -> 19.1 us
  Pallas kernels: 5.13 us -> 6.83 us
    unnamed x21 -> x3, local copies, waits for them, and re-layouts: 5.42 us -> 0.06 us
    pallas_call x0 -> x1, Pallas kernels: none -> 2.63 us  [load_and_project(): pl.pallas_call(body, out_shape=(shape(count, 2 * hid), *(shape(*w.shape)...]
    ppermute x18, starting transfers between devices: 21.2 us -> 19.1 us  [swap(): return lax.ppermute(value, axis, [(i, i ^ bits) for i in range(size)])]
    pallas_call x6 -> x5, Pallas kernels: 4.89 us -> 3.19 us  [in_vmem(): pl.pallas_call(body, out_shape=out_shapes, in_specs=[pl.BlockSpec(memory_...]
    pallas_call x1, Pallas kernels: 0.24 us -> 1.01 us  [prepare(): pl.pallas_call(body, out_shape=(shape(tok_count, width + LANES), shape(ro...]
  transfers between devices with their start and end apart: 18 -> 18, of which waited for: 9 -> 12; matrix products, arithmetic and copies ran while one was open for 0% -> 1% of each run, Pallas kernels for 6% -> 8%
where the time goes in v3:
time: 51 us; the launch traced here: 50.8 us
  waiting for transfers between devices  23.6 us (46%)
  starting transfers between devices  19.1 us (37%)
  Pallas kernels  6.83 us (13%)
  other arithmetic  0.88 us (2%)
    ppermute x18, waiting for transfers between devices, swap(): return lax.ppermute(value, axis, [(i, i ^ bits) for i in range(size)])  23.6 us
    ppermute x18, starting transfers between devices, swap(): return lax.ppermute(value, axis, [(i, i ^ bits) for i in range(size)])  19.1 us
    pallas_call x5, Pallas kernels, in_vmem(): pl.pallas_call(body, out_shape=out_shapes, in_specs=[pl.BlockSpec(memory_...  3.19 us
    pallas_call x1, Pallas kernels, load_and_project(): pl.pallas_call(body, out_shape=(shape(count, 2 * hid), *(shape(*w.shape)...  2.63 us
  transfers between devices with their start and end apart: 18, of which 12 were waited for; matrix products, arithmetic and copies ran while one was open for 1% of the time, Pallas kernels for 8%

profile of v3, /device:TPU:0, one launch (start us, length us, event | category | flops | bytes accessed | tf_op | source)
XLA Modules:
  0.0 50.8 jit_solution(8726325794643252288)
XLA Ops:
  0.0 1.0 %shard_map.64 = (bf16[96,1920]{1,0:T(8,128)(2,1)S(1)}, bf16[24,1920]{1,0:T(8,128)(2,1)S(1)}) custom-call(bf16[96,1792]{1,0:T(8,128)(2,1)} %tokens_hbm.1, s32[8,96]{1,0:T(8,128)} %bitcast.8, f32[8,96]{1,0:T(8,128)} %bitcast.9), custom_call_target="tpu_custom_call" | custom-call | flops 1000000 | bytes 1048576 | tf_op jit(solution)/shard_map/pallas_call | solution.py:69
  1.0 5.1 %collective-permute-start = (bf16[24,1920]{1,0:T(8,128)(2,1)S(1)}, bf16[24,1920]{1,0:T(8,128)(2,1)S(1)}, u32[]{:S(2)}, u32[]{:S(2)}) collective-permute-start(bf16[24,1920]{1,0:T(8,128)(2,1)S(1)} %get-tuple-element.20), channel_id=1, source_target_pairs={{0,24},{8,16},{16,8},{24,0},{1,25},{9,17},{17,9},{25,1},{2,26},{10... | collective-permute-start | bytes 276488 | tf_op jit(solution)/shard_map/ppermute | solution.py:13
  6.1 0.6 %collective-permute-start.3 = (bf16[96,1920]{1,0:T(8,128)(2,1)S(1)}, bf16[96,1920]{1,0:T(8,128)(2,1)S(1)}, u32[]{:S(2)}, u32[]{:S(2)}) collective-permute-start(bf16[96,1920]{1,0:T(8,128)(2,1)S(1)} %get-tuple-element.21.x_ref), channel_id=1, source_target_pairs={{0,8},{8,0},{16,24},{24,16},{1,9},{9,1},{17,25},{25,17},{2,10},{10... | collective-permute-start | bytes 1105928 | tf_op jit(solution)/shard_map/ppermute | solution.py:13
  6.8 2.6 %shard_map.65 = (bf16[96,1024]{1,0:T(8,128)(2,1)S(1)}, bf16[1792,512]{1,0:T(8,128)(2,1)S(1)}, bf16[1792,512]{1,0:T(8,128)(2,1)S(1)}, bf16[512,1792]{1,0:T(8,128)(2,1)S(1)}) custom-call(bf16[96,1920]{1,0:T(8,128)(2,1)S(1)} %get-tuple-element.21.x_ref, bf16[1792,512]{1,0:T(8,128)(2,1)} %bitcast.5, bf16[1792,512]{1,0:T(8,128)(2,1)} %bitcast.6, ...), custom_call_target="tpu_custom_call" | custom-call | tf_op jit(solution)/shard_map/pallas_call | solution.py:115
  9.6 4.4 %collective-permute-done.1 = bf16[24,1920]{1,0:T(8,128)(2,1)S(1)} collective-permute-done((bf16[24,1920]{1,0:T(8,128)(2,1)S(1)}, bf16[24,1920]{1,0:T(8,128)(2,1)S(1)}, u32[]{:S(2)}, u32[]{:S(2)}) %collective-permute-start.1) | collective-permute-done | bytes 92192 | tf_op jit(solution)/shard_map/ppermute | solution.py:13
  14.0 2.5 %collective-permute-start.6 = (bf16[48,1920]{1,0:T(8,128)(2,1)S(1)}, bf16[48,1920]{1,0:T(8,128)(2,1)S(1)}, u32[]{:S(2)}, u32[]{:S(2)}) collective-permute-start(bf16[48,1920]{1,0:T(8,128)(2,1)S(1)} %get-tuple-element.43), channel_id=1, source_target_pairs={{0,6},{2,4},{4,2},{6,0},{1,7},{3,5},{5,3},{7,1},{8,14},{10,12},{12... | collective-permute-start | bytes 552968 | tf_op jit(solution)/shard_map/ppermute | solution.py:13
  16.5 0.5 %collective-permute-start.2 = (bf16[48,1920]{1,0:T(8,128)(2,1)S(1)}, bf16[48,1920]{1,0:T(8,128)(2,1)S(1)}, u32[]{:S(2)}, u32[]{:S(2)}) collective-permute-start(bf16[48,1920]{1,0:T(8,128)(2,1)S(1)} %get-tuple-element.43), channel_id=1, source_target_pairs={{0,2},{2,0},{4,6},{6,4},{1,3},{3,1},{5,7},{7,5},{8,10},{10,8},{12,... | collective-permute-start | bytes 552968 | tf_op jit(solution)/shard_map/ppermute | solution.py:13
  17.0 0.5 collective-permute-start.4
  17.6 0.5 shard_map.68
  18.0 4.5 %collective-permute-done.6 = bf16[48,1920]{1,0:T(8,128)(2,1)S(1)} collective-permute-done((bf16[48,1920]{1,0:T(8,128)(2,1)S(1)}, bf16[48,1920]{1,0:T(8,128)(2,1)S(1)}, u32[]{:S(2)}, u32[]{:S(2)}) %collective-permute-start.6) | collective-permute-done | bytes 184352 | tf_op jit(solution)/shard_map/ppermute | solution.py:13
  22.5 0.7 %shard_map.66.part_ref = bf16[96,1024]{1,0:T(8,128)(2,1)S(1)} custom-call(bf16[96,1920]{1,0:T(8,128)(2,1)S(1)} %collective-permute-done.3.x_ref, bf16[1792,512]{1,0:T(8,128)(2,1)S(1)} %get-tuple-element.24.gate_ref, bf16[1792,512]{1,0:T(8,128)(2,1)S(1)} %get-tuple-element.25.up_ref), custom_call_target="tpu_custom_call" | custom-call | flops 352321536 | bytes 1048576 | tf_op jit(solution)/shard_map/pallas_call | solution.py:22
  23.3 1.2 %collective-permute-done.2 = bf16[48,1920]{1,0:T(8,128)(2,1)S(1)} collective-permute-done((bf16[48,1920]{1,0:T(8,128)(2,1)S(1)}, bf16[48,1920]{1,0:T(8,128)(2,1)S(1)}, u32[]{:S(2)}, u32[]{:S(2)}) %collective-permute-start.2) | collective-permute-done | bytes 184352 | tf_op jit(solution)/shard_map/ppermute | solution.py:13
  24.6 0.2 collective-permute-done.5.other_ref
  24.8 0.5 shard_map.67
  25.3 0.9 %shard_map.69.part_ref = bf16[192,1024]{1,0:T(8,128)(2,1)S(1)} custom-call(bf16[192,1920]{1,0:T(8,128)(2,1)S(1)} %constant_dynamic-update-slice_fusion.2.x_ref, bf16[1792,512]{1,0:T(8,128)(2,1)S(1)} %get-tuple-element.24.gate_ref, bf16[1792,512]{1,0:T(8,128)(2,1)S(1)} %get-tuple-element.25.up_ref), custom_call_target="tpu_custom_call" | custom-call | flops 704643072 | bytes 1048576 | tf_op jit(solution)/shard_map/pallas_call | solution.py:22
  26.2 0.2 collective-permute-start.8
  26.4 1.6 %collective-permute-done.8.other_ref = bf16[192,1024]{1,0:T(8,128)(2,1)S(1)} collective-permute-done((bf16[192,1024]{1,0:T(8,128)(2,1)S(1)}, bf16[192,1024]{1,0:T(8,128)(2,1)S(1)}, u32[]{:S(2)}, u32[]{:S(2)}) %collective-permute-start.8) | collective-permute-done | bytes 393248 | tf_op jit(solution)/shard_map/ppermute | solution.py:13
  28.0 0.6 %shard_map.70 = bf16[192,1792]{1,0:T(8,128)(2,1)S(1)} custom-call(bf16[192,1920]{1,0:T(8,128)(2,1)S(1)} %constant_dynamic-update-slice_fusion.2.x_ref, bf16[192,1024]{1,0:T(8,128)(2,1)S(1)} %shard_map.69.part_ref, bf16[192,1024]{1,0:T(8,128)(2,1)S(1)} %collective-permute-done.8.other_ref, bf16[512,1792]{1,0:T(8,128)(2,1)S(1)} %get-tuple-element.27.down_ref), custom_call_target="tpu_custom_call" | custom-call | flops 352321536 | bytes 1048576 | tf_op jit(solution)/shard_map/pallas_call | solution.py:22
  28.7 2.5 %collective-permute-start.11 = (bf16[48,1792]{1,0:T(8,128)(2,1)S(1)}, bf16[48,1792]{1,0:T(8,128)(2,1)S(1)}, u32[]{:S(2)}, u32[]{:S(2)}) collective-permute-start(bf16[48,1792]{1,0:T(8,128)(2,1)S(1)} %get-tuple-element.36), channel_id=1, source_target_pairs={{0,6},{2,4},{4,2},{6,0},{1,7},{3,5},{5,3},{7,1},{8,14},{10,12},{12... | collective-permute-start | bytes 516104 | tf_op jit(solution)/shard_map/ppermute | solution.py:13
  31.2 0.5 collective-permute-start.10
  31.7 0.5 %collective-permute-start.9 = (bf16[48,1792]{1,0:T(8,128)(2,1)S(1)}, bf16[48,1792]{1,0:T(8,128)(2,1)S(1)}, u32[]{:S(2)}, u32[]{:S(2)}) collective-permute-start(bf16[48,1792]{1,0:T(8,128)(2,1)S(1)} %get-tuple-element.35), channel_id=1, source_target_pairs={{0,2},{2,0},{4,6},{6,4},{1,3},{3,1},{5,7},{7,5},{8,10},{10,8},{12,... | collective-permute-start | bytes 516104 | tf_op jit(solution)/shard_map/ppermute | solution.py:13
  32.2 4.6 %collective-permute-done.11 = bf16[48,1792]{1,0:T(8,128)(2,1)S(1)} collective-permute-done((bf16[48,1792]{1,0:T(8,128)(2,1)S(1)}, bf16[48,1792]{1,0:T(8,128)(2,1)S(1)}, u32[]{:S(2)}, u32[]{:S(2)}) %collective-permute-start.11) | collective-permute-done | bytes 172064 | tf_op jit(solution)/shard_map/ppermute | solution.py:13
  36.9 2.9 %collective-permute-done.10 = bf16[48,1792]{1,0:T(8,128)(2,1)S(1)} collective-permute-done((bf16[48,1792]{1,0:T(8,128)(2,1)S(1)}, bf16[48,1792]{1,0:T(8,128)(2,1)S(1)}, u32[]{:S(2)}, u32[]{:S(2)}) %collective-permute-start.10) | collective-permute-done | bytes 172064 | tf_op jit(solution)/shard_map/ppermute | solution.py:13
  39.7 0.1 collective-permute-done.9
  40.0 2.3 %collective-permute-start.12 = (bf16[24,1792]{1,0:T(8,128)(2,1)S(1)}, bf16[24,1792]{1,0:T(8,128)(2,1)S(1)}, u32[]{:S(2)}, u32[]{:S(2)}) collective-permute-start(bf16[24,1792]{1,0:T(8,128)(2,1)S(1)} %get-tuple-element.41), channel_id=1, source_target_pairs={{0,24},{8,16},{16,8},{24,0},{1,25},{9,17},{17,9},{25,1},{2,26},{10... | collective-permute-start | bytes 258056 | tf_op jit(solution)/shard_map/ppermute | solution.py:13
  42.4 1.6 %collective-permute-start.15 = (bf16[24,1792]{1,0:T(8,128)(2,1)S(1)}, bf16[24,1792]{1,0:T(8,128)(2,1)S(1)}, u32[]{:S(2)}, u32[]{:S(2)}) collective-permute-start(bf16[24,1792]{1,0:T(8,128)(2,1)S(1)} %get-tuple-element.40), channel_id=1, source_target_pairs={{0,2},{2,0},{4,6},{6,4},{1,3},{3,1},{5,7},{7,5},{8,10},{10,8},{12,... | collective-permute-start | bytes 258056 | tf_op jit(solution)/shard_map/ppermute | solution.py:13
  44.0 0.7 %collective-permute-start.16 = (bf16[24,1792]{1,0:T(8,128)(2,1)S(1)}, bf16[24,1792]{1,0:T(8,128)(2,1)S(1)}, u32[]{:S(2)}, u32[]{:S(2)}) collective-permute-start(bf16[24,1792]{1,0:T(8,128)(2,1)S(1)} %get-tuple-element.39), channel_id=1, source_target_pairs={{0,4},{2,6},{4,0},{6,2},{1,5},{3,7},{5,1},{7,3},{8,12},{10,14},{12... | collective-permute-start | bytes 258056 | tf_op jit(solution)/shard_map/ppermute | solution.py:13
  44.7 1.3 %collective-permute-start.17 = (bf16[24,1792]{1,0:T(8,128)(2,1)S(1)}, bf16[24,1792]{1,0:T(8,128)(2,1)S(1)}, u32[]{:S(2)}, u32[]{:S(2)}) collective-permute-start(bf16[24,1792]{1,0:T(8,128)(2,1)S(1)} %get-tuple-element.38), channel_id=1, source_target_pairs={{0,6},{2,4},{4,2},{6,0},{1,7},{3,5},{5,3},{7,1},{8,14},{10,12},{12... | collective-permute-start | bytes 258056 | tf_op jit(solution)/shard_map/ppermute | solution.py:13
  46.0 2.6 %collective-permute-done.13 = bf16[24,1792]{1,0:T(8,128)(2,1)S(1)} collective-permute-done((bf16[24,1792]{1,0:T(8,128)(2,1)S(1)}, bf16[24,1792]{1,0:T(8,128)(2,1)S(1)}, u32[]{:S(2)}, u32[]{:S(2)}) %collective-permute-start.13) | collective-permute-done | bytes 86048 | tf_op jit(solution)/shard_map/ppermute | solution.py:13
  48.7 0.4 collective-permute-done.16
  49.1 1.0 %collective-permute-done.17 = bf16[24,1792]{1,0:T(8,128)(2,1)S(1)} collective-permute-done((bf16[24,1792]{1,0:T(8,128)(2,1)S(1)}, bf16[24,1792]{1,0:T(8,128)(2,1)S(1)}, u32[]{:S(2)}, u32[]{:S(2)}) %collective-permute-start.17) | collective-permute-done | bytes 86048 | tf_op jit(solution)/shard_map/ppermute | solution.py:13
  50.1 0.7 %add_convert_fusion.2 = bf16[24,1792]{1,0:T(8,128)(2,1)} fusion(f32[24,1792]{1,0:T(8,128)S(1)} %convert_add_fusion, bf16[24,1792]{1,0:T(8,128)(2,1)S(1)} %collective-permute-done.17, bf16[24,1792]{1,0:T(8,128)(2,1)S(1)} %collective-permute-done.16, bf16[24,1792]{1,0:T(8,128)(2,1)S(1)} %collective-permute-done.15, bf16[96,1792]{1,0:T(8,128)(2,1)S(1)} %add_convert_fusion, ...), kind=kLoop, calls=%fused_computation.2 | loop fusion | flops 387072 | bytes 602116 | tf_op jit(solution)/shard_map/convert_element_type | solution.py:203
  (23 shorter events, 0.7 us)
Async XLA Ops:
  1.0 8.6 %collective-permute-start = (bf16[24,1920]{1,0:T(8,128)(2,1)S(1)}, bf16[24,1920]{1,0:T(8,128)(2,1)S(1)}, u32[]{:S(2)}, u32[]{:S(2)}) collective-permute-start(bf16[24,1920]{1,0:T(8,128)(2,1)S(1)} %get-tuple-element.20), channel_id=1, source_target_pairs={{0,24},{8,16},{16,8},{24,0},{1,25},{9,17},{17,9},{25,1},{2,26},{10... | collective-permute-start | bytes 276488 | tf_op jit(solution)/shard_map/ppermute | solution.py:13
  6.1 7.8 %collective-permute-start.1 = (bf16[24,1920]{1,0:T(8,128)(2,1)S(1)}, bf16[24,1920]{1,0:T(8,128)(2,1)S(1)}, u32[]{:S(2)}, u32[]{:S(2)}) collective-permute-start(bf16[24,1920]{1,0:T(8,128)(2,1)S(1)} %get-tuple-element.20), channel_id=1, source_target_pairs={{0,16},{8,24},{16,0},{24,8},{1,17},{9,25},{17,1},{25,9},{2,18},{10... | collective-permute-start | bytes 276488 | tf_op jit(solution)/shard_map/ppermute | solution.py:13
  6.1 16.4 %collective-permute-start.3 = (bf16[96,1920]{1,0:T(8,128)(2,1)S(1)}, bf16[96,1920]{1,0:T(8,128)(2,1)S(1)}, u32[]{:S(2)}, u32[]{:S(2)}) collective-permute-start(bf16[96,1920]{1,0:T(8,128)(2,1)S(1)} %get-tuple-element.21.x_ref), channel_id=1, source_target_pairs={{0,8},{8,0},{16,24},{24,16},{1,9},{9,1},{17,25},{25,17},{2,10},{10... | collective-permute-start | bytes 1105928 | tf_op jit(solution)/shard_map/ppermute | solution.py:13
  9.4 8.1 %collective-permute-start.7 = (bf16[96,1024]{1,0:T(8,128)(2,1)S(1)}, bf16[96,1024]{1,0:T(8,128)(2,1)S(1)}, u32[]{:S(2)}, u32[]{:S(2)}) collective-permute-start(bf16[96,1024]{1,0:T(8,128)(2,1)S(1)} %get-tuple-element.22.part_ref), channel_id=1, source_target_pairs={{0,1},{1,0},{2,3},{3,2},{4,5},{5,4},{6,7},{7,6},{8,9},{9,8},{10,11... | collective-permute-start | bytes 589832 | tf_op jit(solution)/shard_map/ppermute | solution.py:13
  14.0 8.5 %collective-permute-start.6 = (bf16[48,1920]{1,0:T(8,128)(2,1)S(1)}, bf16[48,1920]{1,0:T(8,128)(2,1)S(1)}, u32[]{:S(2)}, u32[]{:S(2)}) collective-permute-start(bf16[48,1920]{1,0:T(8,128)(2,1)S(1)} %get-tuple-element.43), channel_id=1, source_target_pairs={{0,6},{2,4},{4,2},{6,0},{1,7},{3,5},{5,3},{7,1},{8,14},{10,12},{12... | collective-permute-start | bytes 552968 | tf_op jit(solution)/shard_map/ppermute | solution.py:13
  16.5 8.0 %collective-permute-start.2 = (bf16[48,1920]{1,0:T(8,128)(2,1)S(1)}, bf16[48,1920]{1,0:T(8,128)(2,1)S(1)}, u32[]{:S(2)}, u32[]{:S(2)}) collective-permute-start(bf16[48,1920]{1,0:T(8,128)(2,1)S(1)} %get-tuple-element.43), channel_id=1, source_target_pairs={{0,2},{2,0},{4,6},{6,4},{1,3},{3,1},{5,7},{7,5},{8,10},{10,8},{12,... | collective-permute-start | bytes 552968 | tf_op jit(solution)/shard_map/ppermute | solution.py:13
  17.0 8.2 %collective-permute-start.4 = (bf16[48,1920]{1,0:T(8,128)(2,1)S(1)}, bf16[48,1920]{1,0:T(8,128)(2,1)S(1)}, u32[]{:S(2)}, u32[]{:S(2)}) collective-permute-start(bf16[48,1920]{1,0:T(8,128)(2,1)S(1)} %get-tuple-element.43), channel_id=1, source_target_pairs={{0,4},{2,6},{4,0},{6,2},{1,5},{3,7},{5,1},{7,3},{8,12},{10,14},{12... | collective-permute-start | bytes 552968 | tf_op jit(solution)/shard_map/ppermute | solution.py:13
  23.2 1.5 %collective-permute-start.5 = (bf16[96,1024]{1,0:T(8,128)(2,1)S(1)}, bf16[96,1024]{1,0:T(8,128)(2,1)S(1)}, u32[]{:S(2)}, u32[]{:S(2)}) collective-permute-start(bf16[96,1024]{1,0:T(8,128)(2,1)S(1)} %shard_map.66.part_ref), channel_id=1, source_target_pairs={{0,1},{1,0},{2,3},{3,2},{4,5},{5,4},{6,7},{7,6},{8,9},{9,8},{10,11... | collective-permute-start | bytes 589832 | tf_op jit(solution)/shard_map/ppermute | solution.py:13
  26.2 1.8 %collective-permute-start.8 = (bf16[192,1024]{1,0:T(8,128)(2,1)S(1)}, bf16[192,1024]{1,0:T(8,128)(2,1)S(1)}, u32[]{:S(2)}, u32[]{:S(2)}) collective-permute-start(bf16[192,1024]{1,0:T(8,128)(2,1)S(1)} %shard_map.69.part_ref), channel_id=1, source_target_pairs={{0,1},{1,0},{2,3},{3,2},{4,5},{5,4},{6,7},{7,6},{8,9},{9,8},{10,11... | collective-permute-start | bytes 1179656 | tf_op jit(solution)/shard_map/ppermute | solution.py:13
  28.7 8.2 %collective-permute-start.11 = (bf16[48,1792]{1,0:T(8,128)(2,1)S(1)}, bf16[48,1792]{1,0:T(8,128)(2,1)S(1)}, u32[]{:S(2)}, u32[]{:S(2)}) collective-permute-start(bf16[48,1792]{1,0:T(8,128)(2,1)S(1)} %get-tuple-element.36), channel_id=1, source_target_pairs={{0,6},{2,4},{4,2},{6,0},{1,7},{3,5},{5,3},{7,1},{8,14},{10,12},{12... | collective-permute-start | bytes 516104 | tf_op jit(solution)/shard_map/ppermute | solution.py:13
  31.2 8.5 %collective-permute-start.10 = (bf16[48,1792]{1,0:T(8,128)(2,1)S(1)}, bf16[48,1792]{1,0:T(8,128)(2,1)S(1)}, u32[]{:S(2)}, u32[]{:S(2)}) collective-permute-start(bf16[48,1792]{1,0:T(8,128)(2,1)S(1)} %get-tuple-element.37), channel_id=1, source_target_pairs={{0,4},{2,6},{4,0},{6,2},{1,5},{3,7},{5,1},{7,3},{8,12},{10,14},{12... | collective-permute-start | bytes 516104 | tf_op jit(solution)/shard_map/ppermute | solution.py:13
  31.7 8.1 %collective-permute-start.9 = (bf16[48,1792]{1,0:T(8,128)(2,1)S(1)}, bf16[48,1792]{1,0:T(8,128)(2,1)S(1)}, u32[]{:S(2)}, u32[]{:S(2)}) collective-permute-start(bf16[48,1792]{1,0:T(8,128)(2,1)S(1)} %get-tuple-element.35), channel_id=1, source_target_pairs={{0,2},{2,0},{4,6},{6,4},{1,3},{3,1},{5,7},{7,5},{8,10},{10,8},{12,... | collective-permute-start | bytes 516104 | tf_op jit(solution)/shard_map/ppermute | solution.py:13
  32.2 10.1 %collective-permute-start.14 = (bf16[96,1792]{1,0:T(8,128)(2,1)S(1)}, bf16[96,1792]{1,0:T(8,128)(2,1)S(1)}, u32[]{:S(2)}, u32[]{:S(2)}) collective-permute-start(bf16[96,1792]{1,0:T(8,128)(2,1)S(1)} %shard_map.67), channel_id=1, source_target_pairs={{0,8},{8,0},{16,24},{24,16},{1,9},{9,1},{17,25},{25,17},{2,10},{10... | collective-permute-start | bytes 1032200 | tf_op jit(solution)/shard_map/ppermute | solution.py:13
  39.9 8.7 %collective-permute-start.13 = (bf16[24,1792]{1,0:T(8,128)(2,1)S(1)}, bf16[24,1792]{1,0:T(8,128)(2,1)S(1)}, u32[]{:S(2)}, u32[]{:S(2)}) collective-permute-start(bf16[24,1792]{1,0:T(8,128)(2,1)S(1)} %get-tuple-element.42), channel_id=1, source_target_pairs={{0,16},{8,24},{16,0},{24,8},{1,17},{9,25},{17,1},{25,9},{2,18},{10... | collective-permute-start | bytes 258056 | tf_op jit(solution)/shard_map/ppermute | solution.py:13
  40.0 8.6 %collective-permute-start.12 = (bf16[24,1792]{1,0:T(8,128)(2,1)S(1)}, bf16[24,1792]{1,0:T(8,128)(2,1)S(1)}, u32[]{:S(2)}, u32[]{:S(2)}) collective-permute-start(bf16[24,1792]{1,0:T(8,128)(2,1)S(1)} %get-tuple-element.41), channel_id=1, source_target_pairs={{0,24},{8,16},{16,8},{24,0},{1,25},{9,17},{17,9},{25,1},{2,26},{10... | collective-permute-start | bytes 258056 | tf_op jit(solution)/shard_map/ppermute | solution.py:13
  42.4 6.2 %collective-permute-start.15 = (bf16[24,1792]{1,0:T(8,128)(2,1)S(1)}, bf16[24,1792]{1,0:T(8,128)(2,1)S(1)}, u32[]{:S(2)}, u32[]{:S(2)}) collective-permute-start(bf16[24,1792]{1,0:T(8,128)(2,1)S(1)} %get-tuple-element.40), channel_id=1, source_target_pairs={{0,2},{2,0},{4,6},{6,4},{1,3},{3,1},{5,7},{7,5},{8,10},{10,8},{12,... | collective-permute-start | bytes 258056 | tf_op jit(solution)/shard_map/ppermute | solution.py:13
  44.0 5.1 %collective-permute-start.16 = (bf16[24,1792]{1,0:T(8,128)(2,1)S(1)}, bf16[24,1792]{1,0:T(8,128)(2,1)S(1)}, u32[]{:S(2)}, u32[]{:S(2)}) collective-permute-start(bf16[24,1792]{1,0:T(8,128)(2,1)S(1)} %get-tuple-element.39), channel_id=1, source_target_pairs={{0,4},{2,6},{4,0},{6,2},{1,5},{3,7},{5,1},{7,3},{8,12},{10,14},{12... | collective-permute-start | bytes 258056 | tf_op jit(solution)/shard_map/ppermute | solution.py:13
  44.7 5.4 %collective-permute-start.17 = (bf16[24,1792]{1,0:T(8,128)(2,1)S(1)}, bf16[24,1792]{1,0:T(8,128)(2,1)S(1)}, u32[]{:S(2)}, u32[]{:S(2)}) collective-permute-start(bf16[24,1792]{1,0:T(8,128)(2,1)S(1)} %get-tuple-element.38), channel_id=1, source_target_pairs={{0,6},{2,4},{4,2},{6,0},{1,7},{3,5},{5,3},{7,1},{8,14},{10,12},{12... | collective-permute-start | bytes 258056 | tf_op jit(solution)/shard_map/ppermute | solution.py:13

commit v4 on v3

--- a/solution.py
+++ b/solution.py
@@ -41,7 +41,9 @@
     tok_count, width = tokens.shape
     choices = expert_ids.shape[1]
 
-    def body(tokens_hbm, ids_hbm, affinity_hbm, all_ref, share_ref, ids_ref, affinity_ref, sems):
+    parts = tok_count // rows
+
+    def body(tokens_hbm, ids_hbm, affinity_hbm, all_ref, share_ref, opposite_ref, ids_ref, affinity_ref, sems):
         copies = [
             pltpu.make_async_copy(tokens_hbm, all_ref.at[:, :width], sems.at[0]),
             pltpu.make_async_copy(ids_hbm, ids_ref, sems.at[1]),
@@ -60,17 +62,19 @@
             weight += jnp.where(ids[c : c + 1, :] == lane, share[c : c + 1, :], 0.0)
         all_ref[:, width:] = weight.T.astype(jnp.bfloat16)
         copies[0].wait()
-        for i in range(tok_count // rows):
+        for i in range(parts):
+            other = i ^ (parts - 1)
 
             @pl.when(lax.axis_index("local") == i)
             def _():
                 share_ref[...] = all_ref[i * rows : (i + 1) * rows, :]
+                opposite_ref[...] = all_ref[other * rows : (other + 1) * rows, :]
 
     return pl.pallas_call(
         body,
-        out_shape=(shape(tok_count, width + LANES), shape(rows, width + LANES)),
+        out_shape=(shape(tok_count, width + LANES), *[shape(rows, width + LANES)] * 2),
         in_specs=[pl.BlockSpec(memory_space=pltpu.HBM)] * 3,
-        out_specs=[pl.BlockSpec(memory_space=pltpu.VMEM)] * 2,
+        out_specs=[pl.BlockSpec(memory_space=pltpu.VMEM)] * 3,
         scratch_shapes=[
             pltpu.VMEM((choices, tok_count), jnp.int32),
             pltpu.VMEM((choices, tok_count), jnp.float32),
@@ -140,6 +144,25 @@
     return in_vmem(body, shape(count, width), 2 * count * width * hid, x, part, other, w_down)
 
 
+def merge(rows, partners, *values):
+    count, width = values[0].shape
+    parts = count // rows
+
+    def body(own_ref, near_ref, direct_ref, *out_refs):
+        for i in range(parts):
+
+            @pl.when(lax.axis_index("local") == i)
+            def _():
+                for j, ref in zip((0, *partners), out_refs):
+                    where = pl.ds((i ^ j) * rows, rows)
+                    total = own_ref[where, :].astype(jnp.float32) + near_ref[where, :].astype(jnp.float32)
+                    if j == parts - 1:
+                        total += direct_ref[...].astype(jnp.float32)
+                    ref[...] = total.astype(jnp.bfloat16)
+
+    return in_vmem(body, tuple(shape(rows, width) for _ in range(parts)), 3 * count * width, *values)
+
+
 def after(value, *others):
     return lax.optimization_barrier((value, *others))[0]
 
@@ -150,18 +173,15 @@
     group_size = local_count // 2
     tok_count, _ = expert_ids.shape
     rows = tok_count // local_count
-    my_local = lax.axis_index("local")
     far = list(range(node_count - 1, 1, -1))
-
-    def quarter(value, j):
-        return lax.dynamic_slice_in_dim(value, (my_local ^ j) * rows, rows, 0)
 
     def split(value):
         step = value.shape[0] // local_count
         return [value[j * step : (j + 1) * step] for j in range(local_count)]
 
-    everything, own = prepare(tokens, expert_ids, affinity, rows)
+    everything, own, opposite = prepare(tokens, expert_ids, affinity, rows)
     arrived = {k: swap(own, "node", k) for k in far}
+    direct = swap(opposite, "node", far[-1])
     near = swap(everything, "node", 1)
     part_own, gate, up, down = load_and_project(everything, w_gate[0], w_up[0], w_down[0])
 
@@ -173,34 +193,42 @@
         x, part, other = state
         return finish(x, part, after(other, *others), down, group_size)
 
+    partners = sorted(range(1, local_count), key=lambda j: (-j.bit_count(), j))
+
+    def exchanged(blocks):
+        return [swap(block, "local", j) for j, block in zip(partners, blocks)]
+
     def moved(blocks):
-        return [swap(block, "local", j) for j, block in enumerate(blocks) if j]
+        return exchanged([blocks[j] for j in partners])
 
     def summed(values):
         return sum(value.astype(jnp.float32) for value in values)
 
     arrived[far[0]] = after(arrived[far[0]], part_own)
     joined = jnp.concatenate([arrived[k] for k in far], axis=0)
-    others = moved([joined] * local_count)
-    near_state = begin(near)
-    others[0] = after(others[0], near_state[1])
-    out_near = complete(near_state)
-    others[1] = after(others[1], out_near)
+    others = moved([joined] * (local_count - 1) + [jnp.concatenate([arrived[k] for k in far[:-1]], axis=0)])
+    out_own = complete((everything, part_own, swap(part_own, "cuts", 1)))
+    x_near, part_near, other_near = begin(near)
+    *others, direct, part_near, out_own = lax.optimization_barrier((*others, direct, part_near, out_own))
+    by_partner = [joined] + [others[partners.index(j)] for j in range(1, local_count)] + [direct]
+    state = begin(jnp.concatenate(by_partner, axis=0))
+    out_far = complete(state)
+    out_near = complete((x_near, part_near, other_near), out_far)
     near_back = swap(out_near, "node", 1)
-    out_own = complete((everything, part_own, swap(part_own, "cuts", 1)))
-    others[2] = after(others[2], out_own)
-    x = jnp.concatenate([joined, *others], axis=0)
-    out_far = complete(begin(x))
     blocks = split(out_far)
-    others = moved(blocks)
-    done = summed([blocks[0], *others]).astype(jnp.bfloat16)
-    back = [swap(done[i * rows : (i + 1) * rows], "node", k) for i, k in enumerate(far)]
-    near_back = after(near_back, done)
-    both = (out_own.astype(jnp.float32) + near_back.astype(jnp.float32)).astype(jnp.bfloat16)
-    blocks = [quarter(both, j) for j in range(local_count)]
-    later = moved(blocks)
+    direct_back = swap(blocks[-1][-rows:], "node", far[-1])
+    blocks[-1] = blocks[-1][:-rows]
+    first, *others = moved(blocks)
+    begun = summed([blocks[0][:-rows], first])
+    begun, *others = lax.optimization_barrier((begun, *others))
+    done = [begun[i * rows : (i + 1) * rows] for i in range(len(far) - 1)] + [blocks[0][-rows:].astype(jnp.float32)]
+    done = [(v + summed([o[i * rows : (i + 1) * rows] for o in others])).astype(jnp.bfloat16) for i, v in enumerate(done)]
+    back = [swap(value, "node", k) for value, k in zip(done, far)]
+    out_own = after(out_own, *done)
+    mine, *blocks = merge(rows, partners, out_own, near_back, direct_back)
+    later = exchanged(blocks)
     total, *later = lax.optimization_barrier((summed(back), *later))
-    return (total + summed([blocks[0], *later])).astype(jnp.bfloat16)
+    return (total + summed([mine, *later])).astype(jnp.bfloat16)
 
 
 def slots_on_device(tokens, expert_ids, affinity, w_gate, w_up, w_down):

time: 51 us -> 49.1 us (0.963)
  waiting for transfers between devices: 23.6 us -> 17.7 us
  starting transfers between devices: 19.1 us -> 23.2 us
    ppermute x18 -> x20, waiting for transfers between devices: 23.6 us -> 17.7 us  [swap(): return lax.ppermute(value, axis, [(i, i ^ bits) for i in range(size)])]
    ppermute x18 -> x20, starting transfers between devices: 19.1 us -> 23.2 us  [swap(): return lax.ppermute(value, axis, [(i, i ^ bits) for i in range(size)])]
    pallas_call x5 -> x6, Pallas kernels: 3.19 us -> 3.31 us  [in_vmem(): pl.pallas_call(body, out_shape=out_shapes, in_specs=[pl.BlockSpec(memory_...]
  transfers between devices with their start and end apart: 18 -> 20, of which waited for: 12 -> 9; matrix products, arithmetic and copies ran while one was open for 1% -> 0% of each run, Pallas kernels for 8% -> 10%
where the time goes in v4:
time: 49.1 us; the launch traced here: 48.9 us
  starting transfers between devices  23.2 us (47%)
  waiting for transfers between devices  17.7 us (36%)
  Pallas kernels  6.97 us (14%)
  other arithmetic  0.8 us (2%)
    ppermute x20, starting transfers between devices, swap(): return lax.ppermute(value, axis, [(i, i ^ bits) for i in range(size)])  23.2 us
    ppermute x20, waiting for transfers between devices, swap(): return lax.ppermute(value, axis, [(i, i ^ bits) for i in range(size)])  17.7 us
    pallas_call x6, Pallas kernels, in_vmem(): pl.pallas_call(body, out_shape=out_shapes, in_specs=[pl.BlockSpec(memory_...  3.31 us
    pallas_call x1, Pallas kernels, load_and_project(): pl.pallas_call(body, out_shape=(shape(count, 2 * hid), *(shape(*w.shape)...  2.63 us
    pallas_call x1, Pallas kernels, prepare(): pl.pallas_call(body, out_shape=(shape(tok_count, width + LANES), *[shape(...  1.03 us
  transfers between devices with their start and end apart: 20, of which 9 were waited for; matrix products, arithmetic and copies ran while one was open for 0% of the time, Pallas kernels for 10%

profile of v4, /device:TPU:0, one launch (start us, length us, event | category | flops | bytes accessed | tf_op | source)
XLA Modules:
  0.0 48.9 jit_solution(17781855240186773527)
XLA Ops:
  0.0 1.0 %shard_map.64 = (bf16[96,1920]{1,0:T(8,128)(2,1)S(1)}, bf16[24,1920]{1,0:T(8,128)(2,1)S(1)}, bf16[24,1920]{1,0:T(8,128)(2,1)S(1)}) custom-call(bf16[96,1792]{1,0:T(8,128)(2,1)} %tokens_hbm.1, s32[8,96]{1,0:T(8,128)} %bitcast.8, f32[8,96]{1,0:T(8,128)} %bitcast.9), custom_call_target="tpu_custom_call" | custom-call | flops 1000000 | bytes 1048576 | tf_op jit(solution)/shard_map/pallas_call | solution.py:73
  1.0 5.1 %collective-permute-start = (bf16[24,1920]{1,0:T(8,128)(2,1)S(1)}, bf16[24,1920]{1,0:T(8,128)(2,1)S(1)}, u32[]{:S(2)}, u32[]{:S(2)}) collective-permute-start(bf16[24,1920]{1,0:T(8,128)(2,1)S(1)} %get-tuple-element.32), channel_id=1, source_target_pairs={{0,24},{8,16},{16,8},{24,0},{1,25},{9,17},{17,9},{25,1},{2,26},{10... | collective-permute-start | bytes 276488 | tf_op jit(solution)/shard_map/ppermute | solution.py:13
  6.2 0.6 %collective-permute-start.6 = (bf16[96,1920]{1,0:T(8,128)(2,1)S(1)}, bf16[96,1920]{1,0:T(8,128)(2,1)S(1)}, u32[]{:S(2)}, u32[]{:S(2)}) collective-permute-start(bf16[96,1920]{1,0:T(8,128)(2,1)S(1)} %get-tuple-element.33.x_ref), channel_id=1, source_target_pairs={{0,8},{8,0},{16,24},{24,16},{1,9},{9,1},{17,25},{25,17},{2,10},{10... | collective-permute-start | bytes 1105928 | tf_op jit(solution)/shard_map/ppermute | solution.py:13
  6.8 2.6 %shard_map.65 = (bf16[96,1024]{1,0:T(8,128)(2,1)S(1)}, bf16[1792,512]{1,0:T(8,128)(2,1)S(1)}, bf16[1792,512]{1,0:T(8,128)(2,1)S(1)}, bf16[512,1792]{1,0:T(8,128)(2,1)S(1)}) custom-call(bf16[96,1920]{1,0:T(8,128)(2,1)S(1)} %get-tuple-element.33.x_ref, bf16[1792,512]{1,0:T(8,128)(2,1)} %bitcast.5, bf16[1792,512]{1,0:T(8,128)(2,1)} %bitcast.6, ...), custom_call_target="tpu_custom_call" | custom-call | tf_op jit(solution)/shard_map/pallas_call | solution.py:119
  9.6 4.4 %collective-permute-done.1 = bf16[24,1920]{1,0:T(8,128)(2,1)S(1)} collective-permute-done((bf16[24,1920]{1,0:T(8,128)(2,1)S(1)}, bf16[24,1920]{1,0:T(8,128)(2,1)S(1)}, u32[]{:S(2)}, u32[]{:S(2)}) %collective-permute-start.1) | collective-permute-done | bytes 92192 | tf_op jit(solution)/shard_map/ppermute | solution.py:13
  14.0 1.6 %collective-permute-start.3 = (bf16[48,1920]{1,0:T(8,128)(2,1)S(1)}, bf16[48,1920]{1,0:T(8,128)(2,1)S(1)}, u32[]{:S(2)}, u32[]{:S(2)}) collective-permute-start(bf16[48,1920]{1,0:T(8,128)(2,1)S(1)} %get-tuple-element.65), channel_id=1, source_target_pairs={{0,2},{2,0},{4,6},{6,4},{1,3},{3,1},{5,7},{7,5},{8,10},{10,8},{12,... | collective-permute-start | bytes 552968 | tf_op jit(solution)/shard_map/ppermute | solution.py:13
  15.6 1.5 %collective-permute-start.4 = (bf16[48,1920]{1,0:T(8,128)(2,1)S(1)}, bf16[48,1920]{1,0:T(8,128)(2,1)S(1)}, u32[]{:S(2)}, u32[]{:S(2)}) collective-permute-start(bf16[48,1920]{1,0:T(8,128)(2,1)S(1)} %get-tuple-element.65), channel_id=1, source_target_pairs={{0,4},{2,6},{4,0},{6,2},{1,5},{3,7},{5,1},{7,3},{8,12},{10,14},{12... | collective-permute-start | bytes 552968 | tf_op jit(solution)/shard_map/ppermute | solution.py:13
  17.1 0.6 %collective-permute-start.5 = (bf16[24,1920]{1,0:T(8,128)(2,1)S(1)}, bf16[24,1920]{1,0:T(8,128)(2,1)S(1)}, u32[]{:S(2)}, u32[]{:S(2)}) collective-permute-start(bf16[24,1920]{1,0:T(8,128)(2,1)S(1)} %get-tuple-element.36), channel_id=1, source_target_pairs={{0,16},{8,24},{16,0},{24,8},{1,17},{9,25},{17,1},{25,9},{2,18},{10... | collective-permute-start | bytes 276488 | tf_op jit(solution)/shard_map/ppermute | solution.py:13
  17.7 0.5 collective-permute-start.2
  18.2 0.5 shard_map.67.own_ref
  18.7 0.3 collective-permute-done.6.x_ref
  19.0 0.7 %shard_map.66.part_ref = bf16[96,1024]{1,0:T(8,128)(2,1)S(1)} custom-call(bf16[96,1920]{1,0:T(8,128)(2,1)S(1)} %collective-permute-done.6.x_ref, bf16[1792,512]{1,0:T(8,128)(2,1)S(1)} %get-tuple-element.37.gate_ref, bf16[1792,512]{1,0:T(8,128)(2,1)S(1)} %get-tuple-element.38.up_ref), custom_call_target="tpu_custom_call" | custom-call | flops 352321536 | bytes 1048576 | tf_op jit(solution)/shard_map/pallas_call | solution.py:22
  19.7 3.4 %collective-permute-done.5 = bf16[24,1920]{1,0:T(8,128)(2,1)S(1)} collective-permute-done((bf16[24,1920]{1,0:T(8,128)(2,1)S(1)}, bf16[24,1920]{1,0:T(8,128)(2,1)S(1)}, u32[]{:S(2)}, u32[]{:S(2)}) %collective-permute-start.5) | collective-permute-done | bytes 92192 | tf_op jit(solution)/shard_map/ppermute | solution.py:13
  23.3 0.9 %shard_map.68.part_ref = bf16[192,1024]{1,0:T(8,128)(2,1)S(1)} custom-call(bf16[192,1920]{1,0:T(8,128)(2,1)S(1)} %constant_dynamic-update-slice_fusion.2.x_ref, bf16[1792,512]{1,0:T(8,128)(2,1)S(1)} %get-tuple-element.37.gate_ref, bf16[1792,512]{1,0:T(8,128)(2,1)S(1)} %get-tuple-element.38.up_ref), custom_call_target="tpu_custom_call" | custom-call | flops 704643072 | bytes 1048576 | tf_op jit(solution)/shard_map/pallas_call | solution.py:22
  24.2 0.5 %collective-permute-start.14 = (bf16[96,1024]{1,0:T(8,128)(2,1)S(1)}, bf16[96,1024]{1,0:T(8,128)(2,1)S(1)}, u32[]{:S(2)}, u32[]{:S(2)}) collective-permute-start(bf16[96,1024]{1,0:T(8,128)(2,1)S(1)} %shard_map.66.part_ref), channel_id=1, source_target_pairs={{0,1},{1,0},{2,3},{3,2},{4,5},{5,4},{6,7},{7,6},{8,9},{9,8},{10,11... | collective-permute-start | bytes 589832 | tf_op jit(solution)/shard_map/ppermute | solution.py:13
  24.7 1.2 %collective-permute-done.8.other_ref = bf16[192,1024]{1,0:T(8,128)(2,1)S(1)} collective-permute-done((bf16[192,1024]{1,0:T(8,128)(2,1)S(1)}, bf16[192,1024]{1,0:T(8,128)(2,1)S(1)}, u32[]{:S(2)}, u32[]{:S(2)}) %collective-permute-start.8) | collective-permute-done | bytes 393248 | tf_op jit(solution)/shard_map/ppermute | solution.py:13
  25.9 0.6 %shard_map.69 = bf16[192,1792]{1,0:T(8,128)(2,1)S(1)} custom-call(bf16[192,1920]{1,0:T(8,128)(2,1)S(1)} %constant_dynamic-update-slice_fusion.2.x_ref, bf16[192,1024]{1,0:T(8,128)(2,1)S(1)} %shard_map.68.part_ref, bf16[192,1024]{1,0:T(8,128)(2,1)S(1)} %collective-permute-done.8.other_ref, bf16[512,1792]{1,0:T(8,128)(2,1)S(1)} %get-tuple-element.39.down_ref), custom_call_target="tpu_custom_call" | custom-call | flops 352321536 | bytes 1048576 | tf_op jit(solution)/shard_map/pallas_call | solution.py:22
  26.6 1.2 %collective-permute-start.9 = (bf16[24,1792]{1,0:T(8,128)(2,1)S(1)}, bf16[24,1792]{1,0:T(8,128)(2,1)S(1)}, u32[]{:S(2)}, u32[]{:S(2)}) collective-permute-start(bf16[24,1792]{1,0:T(8,128)(2,1)S(1)} %get-tuple-element.60), channel_id=1, source_target_pairs={{0,6},{2,4},{4,2},{6,0},{1,7},{3,5},{5,3},{7,1},{8,14},{10,12},{12... | collective-permute-start | bytes 258056 | tf_op jit(solution)/shard_map/ppermute | solution.py:13
  27.9 0.5 shard_map.70
  28.4 1.9 %collective-permute-start.15 = (bf16[96,1792]{1,0:T(8,128)(2,1)S(1)}, bf16[96,1792]{1,0:T(8,128)(2,1)S(1)}, u32[]{:S(2)}, u32[]{:S(2)}) collective-permute-start(bf16[96,1792]{1,0:T(8,128)(2,1)S(1)} %shard_map.70), channel_id=1, source_target_pairs={{0,8},{8,0},{16,24},{24,16},{1,9},{9,1},{17,25},{25,17},{2,10},{10... | collective-permute-start | bytes 1032200 | tf_op jit(solution)/shard_map/ppermute | solution.py:13
  30.2 1.5 %collective-permute-start.10 = (bf16[48,1792]{1,0:T(8,128)(2,1)S(1)}, bf16[48,1792]{1,0:T(8,128)(2,1)S(1)}, u32[]{:S(2)}, u32[]{:S(2)}) collective-permute-start(bf16[48,1792]{1,0:T(8,128)(2,1)S(1)} %get-tuple-element.62), channel_id=1, source_target_pairs={{0,2},{2,0},{4,6},{6,4},{1,3},{3,1},{5,7},{7,5},{8,10},{10,8},{12,... | collective-permute-start | bytes 516104 | tf_op jit(solution)/shard_map/ppermute | solution.py:13
  31.7 1.5 %collective-permute-start.11 = (bf16[48,1792]{1,0:T(8,128)(2,1)S(1)}, bf16[48,1792]{1,0:T(8,128)(2,1)S(1)}, u32[]{:S(2)}, u32[]{:S(2)}) collective-permute-start(bf16[48,1792]{1,0:T(8,128)(2,1)S(1)} %get-tuple-element.61), channel_id=1, source_target_pairs={{0,4},{2,6},{4,0},{6,2},{1,5},{3,7},{5,1},{7,3},{8,12},{10,14},{12... | collective-permute-start | bytes 516104 | tf_op jit(solution)/shard_map/ppermute | solution.py:13
  33.2 0.3 collective-permute-start.16
  33.6 2.5 %collective-permute-done.10 = bf16[48,1792]{1,0:T(8,128)(2,1)S(1)} collective-permute-done((bf16[48,1792]{1,0:T(8,128)(2,1)S(1)}, bf16[48,1792]{1,0:T(8,128)(2,1)S(1)}, u32[]{:S(2)}, u32[]{:S(2)}) %collective-permute-start.10) | collective-permute-done | bytes 172064 | tf_op jit(solution)/shard_map/ppermute | solution.py:13
  36.1 1.2 %collective-permute-done.11 = bf16[48,1792]{1,0:T(8,128)(2,1)S(1)} collective-permute-done((bf16[48,1792]{1,0:T(8,128)(2,1)S(1)}, bf16[48,1792]{1,0:T(8,128)(2,1)S(1)}, u32[]{:S(2)}, u32[]{:S(2)}) %collective-permute-start.11) | collective-permute-done | bytes 172064 | tf_op jit(solution)/shard_map/ppermute | solution.py:13
  37.4 1.3 %collective-permute-start.12 = (bf16[24,1792]{1,0:T(8,128)(2,1)S(1)}, bf16[24,1792]{1,0:T(8,128)(2,1)S(1)}, u32[]{:S(2)}, u32[]{:S(2)}) collective-permute-start(bf16[24,1792]{1,0:T(8,128)(2,1)S(1)} %get-tuple-element.63), channel_id=1, source_target_pairs={{0,24},{8,16},{16,8},{24,0},{1,25},{9,17},{17,9},{25,1},{2,26},{10... | collective-permute-start | bytes 258056 | tf_op jit(solution)/shard_map/ppermute | solution.py:13
  38.7 1.3 %collective-permute-start.13 = (bf16[24,1792]{1,0:T(8,128)(2,1)S(1)}, bf16[24,1792]{1,0:T(8,128)(2,1)S(1)}, u32[]{:S(2)}, u32[]{:S(2)}) collective-permute-start(bf16[24,1792]{1,0:T(8,128)(2,1)S(1)} %get-tuple-element.64), channel_id=1, source_target_pairs={{0,16},{8,24},{16,0},{24,8},{1,17},{9,25},{17,1},{25,9},{2,18},{10... | collective-permute-start | bytes 258056 | tf_op jit(solution)/shard_map/ppermute | solution.py:13
  40.0 0.6 %collective-permute-done.16.direct_ref = bf16[24,1792]{1,0:T(8,128)(2,1)S(1)} collective-permute-done((bf16[24,1792]{1,0:T(8,128)(2,1)S(1)}, bf16[24,1792]{1,0:T(8,128)(2,1)S(1)}, u32[]{:S(2)}, u32[]{:S(2)}) %collective-permute-start.16) | collective-permute-done | bytes 86048 | tf_op jit(solution)/shard_map/ppermute | solution.py:13
  40.7 2.9 %collective-permute-start.17 = (bf16[24,1792]{1,0:T(8,128)(2,1)S(1)}, bf16[24,1792]{1,0:T(8,128)(2,1)S(1)}, u32[]{:S(2)}, u32[]{:S(2)}) collective-permute-start(bf16[24,1792]{1,0:T(8,128)(2,1)S(1)} %get-tuple-element.51), channel_id=1, source_target_pairs={{0,6},{2,4},{4,2},{6,0},{1,7},{3,5},{5,3},{7,1},{8,14},{10,12},{12... | collective-permute-start | bytes 258056 | tf_op jit(solution)/shard_map/ppermute | solution.py:13
  43.7 0.5 %collective-permute-start.19 = (bf16[24,1792]{1,0:T(8,128)(2,1)S(1)}, bf16[24,1792]{1,0:T(8,128)(2,1)S(1)}, u32[]{:S(2)}, u32[]{:S(2)}) collective-permute-start(bf16[24,1792]{1,0:T(8,128)(2,1)S(1)} %get-tuple-element.53), channel_id=1, source_target_pairs={{0,4},{2,6},{4,0},{6,2},{1,5},{3,7},{5,1},{7,3},{8,12},{10,14},{12... | collective-permute-start | bytes 258056 | tf_op jit(solution)/shard_map/ppermute | solution.py:13
  44.2 3.9 %collective-permute-done.13 = bf16[24,1792]{1,0:T(8,128)(2,1)S(1)} collective-permute-done((bf16[24,1792]{1,0:T(8,128)(2,1)S(1)}, bf16[24,1792]{1,0:T(8,128)(2,1)S(1)}, u32[]{:S(2)}, u32[]{:S(2)}) %collective-permute-start.13) | collective-permute-done | bytes 86048 | tf_op jit(solution)/shard_map/ppermute | solution.py:13
  48.2 0.7 %add_convert_fusion = bf16[24,1792]{1,0:T(8,128)(2,1)} fusion(f32[24,1792]{1,0:T(8,128)S(1)} %convert_add_fusion, bf16[24,1792]{1,0:T(8,128)(2,1)S(1)} %collective-permute-done.19, bf16[24,1792]{1,0:T(8,128)(2,1)S(1)} %collective-permute-done.18, bf16[24,1792]{1,0:T(8,128)(2,1)S(1)} %collective-permute-done.17, bf16[24,1792]{1,0:T(8,128)(2,1)S(1)} %get-tuple-element.55), kind=kLoop, calls=%fused_computation | loop fusion | flops 387072 | bytes 602112 | tf_op jit(solution)/shard_map/convert_element_type | solution.py:231
  (28 shorter events, 0.8 us)
Async XLA Ops:
  1.0 8.6 %collective-permute-start = (bf16[24,1920]{1,0:T(8,128)(2,1)S(1)}, bf16[24,1920]{1,0:T(8,128)(2,1)S(1)}, u32[]{:S(2)}, u32[]{:S(2)}) collective-permute-start(bf16[24,1920]{1,0:T(8,128)(2,1)S(1)} %get-tuple-element.32), channel_id=1, source_target_pairs={{0,24},{8,16},{16,8},{24,0},{1,25},{9,17},{17,9},{25,1},{2,26},{10... | collective-permute-start | bytes 276488 | tf_op jit(solution)/shard_map/ppermute | solution.py:13
  6.2 7.8 %collective-permute-start.1 = (bf16[24,1920]{1,0:T(8,128)(2,1)S(1)}, bf16[24,1920]{1,0:T(8,128)(2,1)S(1)}, u32[]{:S(2)}, u32[]{:S(2)}) collective-permute-start(bf16[24,1920]{1,0:T(8,128)(2,1)S(1)} %get-tuple-element.32), channel_id=1, source_target_pairs={{0,16},{8,24},{16,0},{24,8},{1,17},{9,25},{17,1},{25,9},{2,18},{10... | collective-permute-start | bytes 276488 | tf_op jit(solution)/shard_map/ppermute | solution.py:13
  6.2 12.8 %collective-permute-start.6 = (bf16[96,1920]{1,0:T(8,128)(2,1)S(1)}, bf16[96,1920]{1,0:T(8,128)(2,1)S(1)}, u32[]{:S(2)}, u32[]{:S(2)}) collective-permute-start(bf16[96,1920]{1,0:T(8,128)(2,1)S(1)} %get-tuple-element.33.x_ref), channel_id=1, source_target_pairs={{0,8},{8,0},{16,24},{24,16},{1,9},{9,1},{17,25},{25,17},{2,10},{10... | collective-permute-start | bytes 1105928 | tf_op jit(solution)/shard_map/ppermute | solution.py:13
  9.4 8.3 %collective-permute-start.7 = (bf16[96,1024]{1,0:T(8,128)(2,1)S(1)}, bf16[96,1024]{1,0:T(8,128)(2,1)S(1)}, u32[]{:S(2)}, u32[]{:S(2)}) collective-permute-start(bf16[96,1024]{1,0:T(8,128)(2,1)S(1)} %get-tuple-element.34.part_ref), channel_id=1, source_target_pairs={{0,1},{1,0},{2,3},{3,2},{4,5},{5,4},{6,7},{7,6},{8,9},{9,8},{10,11... | collective-permute-start | bytes 589832 | tf_op jit(solution)/shard_map/ppermute | solution.py:13
  14.0 9.1 %collective-permute-start.3 = (bf16[48,1920]{1,0:T(8,128)(2,1)S(1)}, bf16[48,1920]{1,0:T(8,128)(2,1)S(1)}, u32[]{:S(2)}, u32[]{:S(2)}) collective-permute-start(bf16[48,1920]{1,0:T(8,128)(2,1)S(1)} %get-tuple-element.65), channel_id=1, source_target_pairs={{0,2},{2,0},{4,6},{6,4},{1,3},{3,1},{5,7},{7,5},{8,10},{10,8},{12,... | collective-permute-start | bytes 552968 | tf_op jit(solution)/shard_map/ppermute | solution.py:13
  15.6 7.6 %collective-permute-start.4 = (bf16[48,1920]{1,0:T(8,128)(2,1)S(1)}, bf16[48,1920]{1,0:T(8,128)(2,1)S(1)}, u32[]{:S(2)}, u32[]{:S(2)}) collective-permute-start(bf16[48,1920]{1,0:T(8,128)(2,1)S(1)} %get-tuple-element.65), channel_id=1, source_target_pairs={{0,4},{2,6},{4,0},{6,2},{1,5},{3,7},{5,1},{7,3},{8,12},{10,14},{12... | collective-permute-start | bytes 552968 | tf_op jit(solution)/shard_map/ppermute | solution.py:13
  17.1 6.0 %collective-permute-start.5 = (bf16[24,1920]{1,0:T(8,128)(2,1)S(1)}, bf16[24,1920]{1,0:T(8,128)(2,1)S(1)}, u32[]{:S(2)}, u32[]{:S(2)}) collective-permute-start(bf16[24,1920]{1,0:T(8,128)(2,1)S(1)} %get-tuple-element.36), channel_id=1, source_target_pairs={{0,16},{8,24},{16,0},{24,8},{1,17},{9,25},{17,1},{25,9},{2,18},{10... | collective-permute-start | bytes 276488 | tf_op jit(solution)/shard_map/ppermute | solution.py:13
  17.7 5.5 %collective-permute-start.2 = (bf16[24,1920]{1,0:T(8,128)(2,1)S(1)}, bf16[24,1920]{1,0:T(8,128)(2,1)S(1)}, u32[]{:S(2)}, u32[]{:S(2)}) collective-permute-start(bf16[24,1920]{1,0:T(8,128)(2,1)S(1)} %collective-permute-done), channel_id=1, source_target_pairs={{0,6},{2,4},{4,2},{6,0},{1,7},{3,5},{5,3},{7,1},{8,14},{10,12},{12... | collective-permute-start | bytes 276488 | tf_op jit(solution)/shard_map/ppermute | solution.py:13
  24.1 1.8 %collective-permute-start.8 = (bf16[192,1024]{1,0:T(8,128)(2,1)S(1)}, bf16[192,1024]{1,0:T(8,128)(2,1)S(1)}, u32[]{:S(2)}, u32[]{:S(2)}) collective-permute-start(bf16[192,1024]{1,0:T(8,128)(2,1)S(1)} %shard_map.68.part_ref), channel_id=1, source_target_pairs={{0,1},{1,0},{2,3},{3,2},{4,5},{5,4},{6,7},{7,6},{8,9},{9,8},{10,11... | collective-permute-start | bytes 1179656 | tf_op jit(solution)/shard_map/ppermute | solution.py:13
  24.2 3.6 %collective-permute-start.14 = (bf16[96,1024]{1,0:T(8,128)(2,1)S(1)}, bf16[96,1024]{1,0:T(8,128)(2,1)S(1)}, u32[]{:S(2)}, u32[]{:S(2)}) collective-permute-start(bf16[96,1024]{1,0:T(8,128)(2,1)S(1)} %shard_map.66.part_ref), channel_id=1, source_target_pairs={{0,1},{1,0},{2,3},{3,2},{4,5},{5,4},{6,7},{7,6},{8,9},{9,8},{10,11... | collective-permute-start | bytes 589832 | tf_op jit(solution)/shard_map/ppermute | solution.py:13
  26.6 6.9 %collective-permute-start.9 = (bf16[24,1792]{1,0:T(8,128)(2,1)S(1)}, bf16[24,1792]{1,0:T(8,128)(2,1)S(1)}, u32[]{:S(2)}, u32[]{:S(2)}) collective-permute-start(bf16[24,1792]{1,0:T(8,128)(2,1)S(1)} %get-tuple-element.60), channel_id=1, source_target_pairs={{0,6},{2,4},{4,2},{6,0},{1,7},{3,5},{5,3},{7,1},{8,14},{10,12},{12... | collective-permute-start | bytes 258056 | tf_op jit(solution)/shard_map/ppermute | solution.py:13
  28.4 12.2 %collective-permute-start.15 = (bf16[96,1792]{1,0:T(8,128)(2,1)S(1)}, bf16[96,1792]{1,0:T(8,128)(2,1)S(1)}, u32[]{:S(2)}, u32[]{:S(2)}) collective-permute-start(bf16[96,1792]{1,0:T(8,128)(2,1)S(1)} %shard_map.70), channel_id=1, source_target_pairs={{0,8},{8,0},{16,24},{24,16},{1,9},{9,1},{17,25},{25,17},{2,10},{10... | collective-permute-start | bytes 1032200 | tf_op jit(solution)/shard_map/ppermute | solution.py:13
  30.2 5.9 %collective-permute-start.10 = (bf16[48,1792]{1,0:T(8,128)(2,1)S(1)}, bf16[48,1792]{1,0:T(8,128)(2,1)S(1)}, u32[]{:S(2)}, u32[]{:S(2)}) collective-permute-start(bf16[48,1792]{1,0:T(8,128)(2,1)S(1)} %get-tuple-element.62), channel_id=1, source_target_pairs={{0,2},{2,0},{4,6},{6,4},{1,3},{3,1},{5,7},{7,5},{8,10},{10,8},{12,... | collective-permute-start | bytes 516104 | tf_op jit(solution)/shard_map/ppermute | solution.py:13
  31.7 5.6 %collective-permute-start.11 = (bf16[48,1792]{1,0:T(8,128)(2,1)S(1)}, bf16[48,1792]{1,0:T(8,128)(2,1)S(1)}, u32[]{:S(2)}, u32[]{:S(2)}) collective-permute-start(bf16[48,1792]{1,0:T(8,128)(2,1)S(1)} %get-tuple-element.61), channel_id=1, source_target_pairs={{0,4},{2,6},{4,0},{6,2},{1,5},{3,7},{5,1},{7,3},{8,12},{10,14},{12... | collective-permute-start | bytes 516104 | tf_op jit(solution)/shard_map/ppermute | solution.py:13
  33.2 7.4 %collective-permute-start.16 = (bf16[24,1792]{1,0:T(8,128)(2,1)S(1)}, bf16[24,1792]{1,0:T(8,128)(2,1)S(1)}, u32[]{:S(2)}, u32[]{:S(2)}) collective-permute-start(bf16[24,1792]{1,0:T(8,128)(2,1)S(1)} %get-tuple-element.59), channel_id=1, source_target_pairs={{0,16},{8,24},{16,0},{24,8},{1,17},{9,25},{17,1},{25,9},{2,18},{10... | collective-permute-start | bytes 258056 | tf_op jit(solution)/shard_map/ppermute | solution.py:13
  37.4 6.9 %collective-permute-start.12 = (bf16[24,1792]{1,0:T(8,128)(2,1)S(1)}, bf16[24,1792]{1,0:T(8,128)(2,1)S(1)}, u32[]{:S(2)}, u32[]{:S(2)}) collective-permute-start(bf16[24,1792]{1,0:T(8,128)(2,1)S(1)} %get-tuple-element.63), channel_id=1, source_target_pairs={{0,24},{8,16},{16,8},{24,0},{1,25},{9,17},{17,9},{25,1},{2,26},{10... | collective-permute-start | bytes 258056 | tf_op jit(solution)/shard_map/ppermute | solution.py:13
  38.7 9.5 %collective-permute-start.13 = (bf16[24,1792]{1,0:T(8,128)(2,1)S(1)}, bf16[24,1792]{1,0:T(8,128)(2,1)S(1)}, u32[]{:S(2)}, u32[]{:S(2)}) collective-permute-start(bf16[24,1792]{1,0:T(8,128)(2,1)S(1)} %get-tuple-element.64), channel_id=1, source_target_pairs={{0,16},{8,24},{16,0},{24,8},{1,17},{9,25},{17,1},{25,9},{2,18},{10... | collective-permute-start | bytes 258056 | tf_op jit(solution)/shard_map/ppermute | solution.py:13
  40.7 7.5 %collective-permute-start.17 = (bf16[24,1792]{1,0:T(8,128)(2,1)S(1)}, bf16[24,1792]{1,0:T(8,128)(2,1)S(1)}, u32[]{:S(2)}, u32[]{:S(2)}) collective-permute-start(bf16[24,1792]{1,0:T(8,128)(2,1)S(1)} %get-tuple-element.51), channel_id=1, source_target_pairs={{0,6},{2,4},{4,2},{6,0},{1,7},{3,5},{5,3},{7,1},{8,14},{10,12},{12... | collective-permute-start | bytes 258056 | tf_op jit(solution)/shard_map/ppermute | solution.py:13
  43.6 4.6 %collective-permute-start.18 = (bf16[24,1792]{1,0:T(8,128)(2,1)S(1)}, bf16[24,1792]{1,0:T(8,128)(2,1)S(1)}, u32[]{:S(2)}, u32[]{:S(2)}) collective-permute-start(bf16[24,1792]{1,0:T(8,128)(2,1)S(1)} %get-tuple-element.52), channel_id=1, source_target_pairs={{0,2},{2,0},{4,6},{6,4},{1,3},{3,1},{5,7},{7,5},{8,10},{10,8},{12,... | collective-permute-start | bytes 258056 | tf_op jit(solution)/shard_map/ppermute | solution.py:13
  43.7 4.5 %collective-permute-start.19 = (bf16[24,1792]{1,0:T(8,128)(2,1)S(1)}, bf16[24,1792]{1,0:T(8,128)(2,1)S(1)}, u32[]{:S(2)}, u32[]{:S(2)}) collective-permute-start(bf16[24,1792]{1,0:T(8,128)(2,1)S(1)} %get-tuple-element.53), channel_id=1, source_target_pairs={{0,4},{2,6},{4,0},{6,2},{1,5},{3,7},{5,1},{7,3},{8,12},{10,14},{12... | collective-permute-start | bytes 258056 | tf_op jit(solution)/shard_map/ppermute | solution.py:13

commit v5 on v4

--- a/solution.py
+++ b/solution.py
@@ -181,7 +181,6 @@
 
     everything, own, opposite = prepare(tokens, expert_ids, affinity, rows)
     arrived = {k: swap(own, "node", k) for k in far}
-    direct = swap(opposite, "node", far[-1])
     near = swap(everything, "node", 1)
     part_own, gate, up, down = load_and_project(everything, w_gate[0], w_up[0], w_down[0])
 
@@ -208,13 +207,15 @@
     joined = jnp.concatenate([arrived[k] for k in far], axis=0)
     others = moved([joined] * (local_count - 1) + [jnp.concatenate([arrived[k] for k in far[:-1]], axis=0)])
     out_own = complete((everything, part_own, swap(part_own, "cuts", 1)))
-    x_near, part_near, other_near = begin(near)
-    *others, direct, part_near, out_own = lax.optimization_barrier((*others, direct, part_near, out_own))
+    direct = swap(after(opposite, out_own), "node", far[-1])
+    near_state = begin(near)
+    others[1] = after(others[1], near_state[1])
+    others[2] = after(others[2], near_state[2])
     by_partner = [joined] + [others[partners.index(j)] for j in range(1, local_count)] + [direct]
-    state = begin(jnp.concatenate(by_partner, axis=0))
-    out_far = complete(state)
-    out_near = complete((x_near, part_near, other_near), out_far)
+    state = begin(after(jnp.concatenate(by_partner, axis=0), out_own))
+    out_near = complete(near_state, state[1])
     near_back = swap(out_near, "node", 1)
+    out_far = complete(state, out_near)
     blocks = split(out_far)
     direct_back = swap(blocks[-1][-rows:], "node", far[-1])
     blocks[-1] = blocks[-1][:-rows]

time: 49.1 us -> 48.2 us (0.982)
  starting transfers between devices: 23.2 us -> 21.2 us
  waiting for transfers between devices: 17.7 us -> 18.7 us
    ppermute x20, starting transfers between devices: 23.2 us -> 21.2 us  [swap(): return lax.ppermute(value, axis, [(i, i ^ bits) for i in range(size)])]
    ppermute x20, waiting for transfers between devices: 17.7 us -> 18.7 us  [swap(): return lax.ppermute(value, axis, [(i, i ^ bits) for i in range(size)])]
  transfers between devices with their start and end apart: 20 -> 20, of which waited for: 9 -> 12; matrix products, arithmetic and copies ran while one was open for 0% -> 0% of each run, Pallas kernels for 10% -> 11%
where the time goes in v5:
time: 48.2 us; the launch traced here: 48 us
  starting transfers between devices  21.2 us (44%)
  waiting for transfers between devices  18.7 us (39%)
  Pallas kernels  6.98 us (14%)
  other arithmetic  0.8 us (2%)
    ppermute x20, starting transfers between devices, swap(): return lax.ppermute(value, axis, [(i, i ^ bits) for i in range(size)])  21.2 us
    ppermute x20, waiting for transfers between devices, swap(): return lax.ppermute(value, axis, [(i, i ^ bits) for i in range(size)])  18.7 us
    pallas_call x6, Pallas kernels, in_vmem(): pl.pallas_call(body, out_shape=out_shapes, in_specs=[pl.BlockSpec(memory_...  3.32 us
    pallas_call x1, Pallas kernels, load_and_project(): pl.pallas_call(body, out_shape=(shape(count, 2 * hid), *(shape(*w.shape)...  2.63 us
    pallas_call x1, Pallas kernels, prepare(): pl.pallas_call(body, out_shape=(shape(tok_count, width + LANES), *[shape(...  1.03 us
  transfers between devices with their start and end apart: 20, of which 12 were waited for; matrix products, arithmetic and copies ran while one was open for 0% of the time, Pallas kernels for 11%

profile of v5, /device:TPU:0, one launch (start us, length us, event | category | flops | bytes accessed | tf_op | source)
XLA Modules:
  0.0 48.0 jit_solution(18072569626312609810)
XLA Ops:
  0.0 1.0 %shard_map.64 = (bf16[96,1920]{1,0:T(8,128)(2,1)S(1)}, bf16[24,1920]{1,0:T(8,128)(2,1)S(1)}, bf16[24,1920]{1,0:T(8,128)(2,1)S(1)}) custom-call(bf16[96,1792]{1,0:T(8,128)(2,1)} %tokens_hbm.1, s32[8,96]{1,0:T(8,128)} %bitcast.8, f32[8,96]{1,0:T(8,128)} %bitcast.9), custom_call_target="tpu_custom_call" | custom-call | flops 1000000 | bytes 1048576 | tf_op jit(solution)/shard_map/pallas_call | solution.py:73
  1.0 5.1 %collective-permute-start = (bf16[24,1920]{1,0:T(8,128)(2,1)S(1)}, bf16[24,1920]{1,0:T(8,128)(2,1)S(1)}, u32[]{:S(2)}, u32[]{:S(2)}) collective-permute-start(bf16[24,1920]{1,0:T(8,128)(2,1)S(1)} %get-tuple-element.31), channel_id=1, source_target_pairs={{0,24},{8,16},{16,8},{24,0},{1,25},{9,17},{17,9},{25,1},{2,26},{10... | collective-permute-start | bytes 276488 | tf_op jit(solution)/shard_map/ppermute | solution.py:13
  6.2 0.6 %collective-permute-start.3 = (bf16[96,1920]{1,0:T(8,128)(2,1)S(1)}, bf16[96,1920]{1,0:T(8,128)(2,1)S(1)}, u32[]{:S(2)}, u32[]{:S(2)}) collective-permute-start(bf16[96,1920]{1,0:T(8,128)(2,1)S(1)} %get-tuple-element.32.x_ref), channel_id=1, source_target_pairs={{0,8},{8,0},{16,24},{24,16},{1,9},{9,1},{17,25},{25,17},{2,10},{10... | collective-permute-start | bytes 1105928 | tf_op jit(solution)/shard_map/ppermute | solution.py:13
  6.8 2.6 %shard_map.65 = (bf16[96,1024]{1,0:T(8,128)(2,1)S(1)}, bf16[1792,512]{1,0:T(8,128)(2,1)S(1)}, bf16[1792,512]{1,0:T(8,128)(2,1)S(1)}, bf16[512,1792]{1,0:T(8,128)(2,1)S(1)}) custom-call(bf16[96,1920]{1,0:T(8,128)(2,1)S(1)} %get-tuple-element.32.x_ref, bf16[1792,512]{1,0:T(8,128)(2,1)} %bitcast.5, bf16[1792,512]{1,0:T(8,128)(2,1)} %bitcast.6, ...), custom_call_target="tpu_custom_call" | custom-call | tf_op jit(solution)/shard_map/pallas_call | solution.py:119
  9.6 4.4 %collective-permute-done.1 = bf16[24,1920]{1,0:T(8,128)(2,1)S(1)} collective-permute-done((bf16[24,1920]{1,0:T(8,128)(2,1)S(1)}, bf16[24,1920]{1,0:T(8,128)(2,1)S(1)}, u32[]{:S(2)}, u32[]{:S(2)}) %collective-permute-start.1) | collective-permute-done | bytes 92192 | tf_op jit(solution)/shard_map/ppermute | solution.py:13
  14.0 1.6 %collective-permute-start.2 = (bf16[48,1920]{1,0:T(8,128)(2,1)S(1)}, bf16[48,1920]{1,0:T(8,128)(2,1)S(1)}, u32[]{:S(2)}, u32[]{:S(2)}) collective-permute-start(bf16[48,1920]{1,0:T(8,128)(2,1)S(1)} %get-tuple-element.63), channel_id=1, source_target_pairs={{0,2},{2,0},{4,6},{6,4},{1,3},{3,1},{5,7},{7,5},{8,10},{10,8},{12,... | collective-permute-start | bytes 552968 | tf_op jit(solution)/shard_map/ppermute | solution.py:13
  15.6 1.5 %collective-permute-start.4 = (bf16[48,1920]{1,0:T(8,128)(2,1)S(1)}, bf16[48,1920]{1,0:T(8,128)(2,1)S(1)}, u32[]{:S(2)}, u32[]{:S(2)}) collective-permute-start(bf16[48,1920]{1,0:T(8,128)(2,1)S(1)} %get-tuple-element.63), channel_id=1, source_target_pairs={{0,4},{2,6},{4,0},{6,2},{1,5},{3,7},{5,1},{7,3},{8,12},{10,14},{12... | collective-permute-start | bytes 552968 | tf_op jit(solution)/shard_map/ppermute | solution.py:13
  17.1 0.5 %collective-permute-start.6 = (bf16[24,1920]{1,0:T(8,128)(2,1)S(1)}, bf16[24,1920]{1,0:T(8,128)(2,1)S(1)}, u32[]{:S(2)}, u32[]{:S(2)}) collective-permute-start(bf16[24,1920]{1,0:T(8,128)(2,1)S(1)} %collective-permute-done), channel_id=1, source_target_pairs={{0,6},{2,4},{4,2},{6,0},{1,7},{3,5},{5,3},{7,1},{8,14},{10,12},{12... | collective-permute-start | bytes 276488 | tf_op jit(solution)/shard_map/ppermute | solution.py:13
  17.6 0.5 %shard_map.67.own_ref = bf16[96,1792]{1,0:T(8,128)(2,1)S(1)} custom-call(bf16[96,1920]{1,0:T(8,128)(2,1)S(1)} %get-tuple-element.32.x_ref, bf16[96,1024]{1,0:T(8,128)(2,1)S(1)} %get-tuple-element.33.part_ref, bf16[96,1024]{1,0:T(8,128)(2,1)S(1)} %collective-permute-done.7.other_ref, bf16[512,1792]{1,0:T(8,128)(2,1)S(1)} %get-tuple-element.40.down_ref), custom_call_target="tpu_custom_call" | custom-call | flops 176160768 | bytes 1048576 | tf_op jit(solution)/shard_map/pallas_call | solution.py:22
  18.1 0.7 %collective-permute-start.8 = (bf16[24,1920]{1,0:T(8,128)(2,1)S(1)}, bf16[24,1920]{1,0:T(8,128)(2,1)S(1)}, u32[]{:S(2)}, u32[]{:S(2)}) collective-permute-start(bf16[24,1920]{1,0:T(8,128)(2,1)S(1)} %get-tuple-element.41), channel_id=1, source_target_pairs={{0,16},{8,24},{16,0},{24,8},{1,17},{9,25},{17,1},{25,9},{2,18},{10... | collective-permute-start | bytes 276488 | tf_op jit(solution)/shard_map/ppermute | solution.py:13
  19.0 0.7 %shard_map.66.part_ref = bf16[96,1024]{1,0:T(8,128)(2,1)S(1)} custom-call(bf16[96,1920]{1,0:T(8,128)(2,1)S(1)} %collective-permute-done.3.x_ref, bf16[1792,512]{1,0:T(8,128)(2,1)S(1)} %get-tuple-element.35.gate_ref, bf16[1792,512]{1,0:T(8,128)(2,1)S(1)} %get-tuple-element.36.up_ref), custom_call_target="tpu_custom_call" | custom-call | flops 352321536 | bytes 1048576 | tf_op jit(solution)/shard_map/pallas_call | solution.py:22
  19.8 0.9 %collective-permute-done.2 = bf16[48,1920]{1,0:T(8,128)(2,1)S(1)} collective-permute-done((bf16[48,1920]{1,0:T(8,128)(2,1)S(1)}, bf16[48,1920]{1,0:T(8,128)(2,1)S(1)}, u32[]{:S(2)}, u32[]{:S(2)}) %collective-permute-start.2) | collective-permute-done | bytes 184352 | tf_op jit(solution)/shard_map/ppermute | solution.py:13
  20.7 2.3 %collective-permute-done.4 = bf16[48,1920]{1,0:T(8,128)(2,1)S(1)} collective-permute-done((bf16[48,1920]{1,0:T(8,128)(2,1)S(1)}, bf16[48,1920]{1,0:T(8,128)(2,1)S(1)}, u32[]{:S(2)}, u32[]{:S(2)}) %collective-permute-start.4) | collective-permute-done | bytes 184352 | tf_op jit(solution)/shard_map/ppermute | solution.py:13
  23.1 1.1 %collective-permute-done.8 = bf16[24,1920]{1,0:T(8,128)(2,1)S(1)} collective-permute-done((bf16[24,1920]{1,0:T(8,128)(2,1)S(1)}, bf16[24,1920]{1,0:T(8,128)(2,1)S(1)}, u32[]{:S(2)}, u32[]{:S(2)}) %collective-permute-start.8) | collective-permute-done | bytes 92192 | tf_op jit(solution)/shard_map/ppermute | solution.py:13
  24.2 0.9 %shard_map.68.part_ref = bf16[192,1024]{1,0:T(8,128)(2,1)S(1)} custom-call(bf16[192,1920]{1,0:T(8,128)(2,1)S(1)} %constant_dynamic-update-slice_fusion.2.x_ref, bf16[1792,512]{1,0:T(8,128)(2,1)S(1)} %get-tuple-element.35.gate_ref, bf16[1792,512]{1,0:T(8,128)(2,1)S(1)} %get-tuple-element.36.up_ref), custom_call_target="tpu_custom_call" | custom-call | flops 704643072 | bytes 1048576 | tf_op jit(solution)/shard_map/pallas_call | solution.py:22
  25.2 0.5 shard_map.69
  25.7 1.2 %collective-permute-done.9.other_ref = bf16[192,1024]{1,0:T(8,128)(2,1)S(1)} collective-permute-done((bf16[192,1024]{1,0:T(8,128)(2,1)S(1)}, bf16[192,1024]{1,0:T(8,128)(2,1)S(1)}, u32[]{:S(2)}, u32[]{:S(2)}) %collective-permute-start.9) | collective-permute-done | bytes 393248 | tf_op jit(solution)/shard_map/ppermute | solution.py:13
  26.9 0.7 %shard_map.70 = bf16[192,1792]{1,0:T(8,128)(2,1)S(1)} custom-call(bf16[192,1920]{1,0:T(8,128)(2,1)S(1)} %constant_dynamic-update-slice_fusion.2.x_ref, bf16[192,1024]{1,0:T(8,128)(2,1)S(1)} %shard_map.68.part_ref, bf16[192,1024]{1,0:T(8,128)(2,1)S(1)} %collective-permute-done.9.other_ref, bf16[512,1792]{1,0:T(8,128)(2,1)S(1)} %get-tuple-element.40.down_ref), custom_call_target="tpu_custom_call" | custom-call | flops 352321536 | bytes 1048576 | tf_op jit(solution)/shard_map/pallas_call | solution.py:22
  27.6 2.5 %collective-permute-start.10 = (bf16[24,1792]{1,0:T(8,128)(2,1)S(1)}, bf16[24,1792]{1,0:T(8,128)(2,1)S(1)}, u32[]{:S(2)}, u32[]{:S(2)}) collective-permute-start(bf16[24,1792]{1,0:T(8,128)(2,1)S(1)} %get-tuple-element.58), channel_id=1, source_target_pairs={{0,6},{2,4},{4,2},{6,0},{1,7},{3,5},{5,3},{7,1},{8,14},{10,12},{12... | collective-permute-start | bytes 258056 | tf_op jit(solution)/shard_map/ppermute | solution.py:13
  30.1 0.6 %collective-permute-start.11 = (bf16[48,1792]{1,0:T(8,128)(2,1)S(1)}, bf16[48,1792]{1,0:T(8,128)(2,1)S(1)}, u32[]{:S(2)}, u32[]{:S(2)}) collective-permute-start(bf16[48,1792]{1,0:T(8,128)(2,1)S(1)} %get-tuple-element.60), channel_id=1, source_target_pairs={{0,2},{2,0},{4,6},{6,4},{1,3},{3,1},{5,7},{7,5},{8,10},{10,8},{12,... | collective-permute-start | bytes 516104 | tf_op jit(solution)/shard_map/ppermute | solution.py:13
  30.7 0.5 %collective-permute-start.12 = (bf16[48,1792]{1,0:T(8,128)(2,1)S(1)}, bf16[48,1792]{1,0:T(8,128)(2,1)S(1)}, u32[]{:S(2)}, u32[]{:S(2)}) collective-permute-start(bf16[48,1792]{1,0:T(8,128)(2,1)S(1)} %get-tuple-element.59), channel_id=1, source_target_pairs={{0,4},{2,6},{4,0},{6,2},{1,5},{3,7},{5,1},{7,3},{8,12},{10,14},{12... | collective-permute-start | bytes 516104 | tf_op jit(solution)/shard_map/ppermute | solution.py:13
  31.2 1.3 %collective-permute-start.16 = (bf16[24,1792]{1,0:T(8,128)(2,1)S(1)}, bf16[24,1792]{1,0:T(8,128)(2,1)S(1)}, u32[]{:S(2)}, u32[]{:S(2)}) collective-permute-start(bf16[24,1792]{1,0:T(8,128)(2,1)S(1)} %get-tuple-element.57), channel_id=1, source_target_pairs={{0,16},{8,24},{16,0},{24,8},{1,17},{9,25},{17,1},{25,9},{2,18},{10... | collective-permute-start | bytes 258056 | tf_op jit(solution)/shard_map/ppermute | solution.py:13
  32.5 1.2 %collective-permute-done.10 = bf16[24,1792]{1,0:T(8,128)(2,1)S(1)} collective-permute-done((bf16[24,1792]{1,0:T(8,128)(2,1)S(1)}, bf16[24,1792]{1,0:T(8,128)(2,1)S(1)}, u32[]{:S(2)}, u32[]{:S(2)}) %collective-permute-start.10) | collective-permute-done | bytes 86048 | tf_op jit(solution)/shard_map/ppermute | solution.py:13
  33.7 3.1 %collective-permute-done.11 = bf16[48,1792]{1,0:T(8,128)(2,1)S(1)} collective-permute-done((bf16[48,1792]{1,0:T(8,128)(2,1)S(1)}, bf16[48,1792]{1,0:T(8,128)(2,1)S(1)}, u32[]{:S(2)}, u32[]{:S(2)}) %collective-permute-start.11) | collective-permute-done | bytes 172064 | tf_op jit(solution)/shard_map/ppermute | solution.py:13
  37.0 2.0 %collective-permute-start.13 = (bf16[24,1792]{1,0:T(8,128)(2,1)S(1)}, bf16[24,1792]{1,0:T(8,128)(2,1)S(1)}, u32[]{:S(2)}, u32[]{:S(2)}) collective-permute-start(bf16[24,1792]{1,0:T(8,128)(2,1)S(1)} %get-tuple-element.61), channel_id=1, source_target_pairs={{0,24},{8,16},{16,8},{24,0},{1,25},{9,17},{17,9},{25,1},{2,26},{10... | collective-permute-start | bytes 258056 | tf_op jit(solution)/shard_map/ppermute | solution.py:13
  39.0 0.5 %collective-permute-start.14 = (bf16[24,1792]{1,0:T(8,128)(2,1)S(1)}, bf16[24,1792]{1,0:T(8,128)(2,1)S(1)}, u32[]{:S(2)}, u32[]{:S(2)}) collective-permute-start(bf16[24,1792]{1,0:T(8,128)(2,1)S(1)} %get-tuple-element.62), channel_id=1, source_target_pairs={{0,16},{8,24},{16,0},{24,8},{1,17},{9,25},{17,1},{25,9},{2,18},{10... | collective-permute-start | bytes 258056 | tf_op jit(solution)/shard_map/ppermute | solution.py:13
  39.6 2.3 %collective-permute-start.17 = (bf16[24,1792]{1,0:T(8,128)(2,1)S(1)}, bf16[24,1792]{1,0:T(8,128)(2,1)S(1)}, u32[]{:S(2)}, u32[]{:S(2)}) collective-permute-start(bf16[24,1792]{1,0:T(8,128)(2,1)S(1)} %get-tuple-element.49), channel_id=1, source_target_pairs={{0,6},{2,4},{4,2},{6,0},{1,7},{3,5},{5,3},{7,1},{8,14},{10,12},{12... | collective-permute-start | bytes 258056 | tf_op jit(solution)/shard_map/ppermute | solution.py:13
  41.9 0.5 %collective-permute-start.18 = (bf16[24,1792]{1,0:T(8,128)(2,1)S(1)}, bf16[24,1792]{1,0:T(8,128)(2,1)S(1)}, u32[]{:S(2)}, u32[]{:S(2)}) collective-permute-start(bf16[24,1792]{1,0:T(8,128)(2,1)S(1)} %get-tuple-element.50), channel_id=1, source_target_pairs={{0,2},{2,0},{4,6},{6,4},{1,3},{3,1},{5,7},{7,5},{8,10},{10,8},{12,... | collective-permute-start | bytes 258056 | tf_op jit(solution)/shard_map/ppermute | solution.py:13
  42.5 0.7 %collective-permute-start.19 = (bf16[24,1792]{1,0:T(8,128)(2,1)S(1)}, bf16[24,1792]{1,0:T(8,128)(2,1)S(1)}, u32[]{:S(2)}, u32[]{:S(2)}) collective-permute-start(bf16[24,1792]{1,0:T(8,128)(2,1)S(1)} %get-tuple-element.51), channel_id=1, source_target_pairs={{0,4},{2,6},{4,0},{6,2},{1,5},{3,7},{5,1},{7,3},{8,12},{10,14},{12... | collective-permute-start | bytes 258056 | tf_op jit(solution)/shard_map/ppermute | solution.py:13
  43.2 0.5 %collective-permute-done.13 = bf16[24,1792]{1,0:T(8,128)(2,1)S(1)} collective-permute-done((bf16[24,1792]{1,0:T(8,128)(2,1)S(1)}, bf16[24,1792]{1,0:T(8,128)(2,1)S(1)}, u32[]{:S(2)}, u32[]{:S(2)}) %collective-permute-start.13) | collective-permute-done | bytes 86048 | tf_op jit(solution)/shard_map/ppermute | solution.py:13
  43.7 3.6 %collective-permute-done.14 = bf16[24,1792]{1,0:T(8,128)(2,1)S(1)} collective-permute-done((bf16[24,1792]{1,0:T(8,128)(2,1)S(1)}, bf16[24,1792]{1,0:T(8,128)(2,1)S(1)}, u32[]{:S(2)}, u32[]{:S(2)}) %collective-permute-start.14) | collective-permute-done | bytes 86048 | tf_op jit(solution)/shard_map/ppermute | solution.py:13
  47.3 0.7 %add_convert_fusion = bf16[24,1792]{1,0:T(8,128)(2,1)} fusion(f32[24,1792]{1,0:T(8,128)S(1)} %convert_add_fusion, bf16[24,1792]{1,0:T(8,128)(2,1)S(1)} %collective-permute-done.19, bf16[24,1792]{1,0:T(8,128)(2,1)S(1)} %collective-permute-done.18, bf16[24,1792]{1,0:T(8,128)(2,1)S(1)} %collective-permute-done.17, bf16[24,1792]{1,0:T(8,128)(2,1)S(1)} %get-tuple-element.53), kind=kLoop, calls=%fused_computation | loop fusion | flops 387072 | bytes 602112 | tf_op jit(solution)/shard_map/convert_element_type | solution.py:232
  (28 shorter events, 1.1 us)
Async XLA Ops:
  1.0 8.6 %collective-permute-start = (bf16[24,1920]{1,0:T(8,128)(2,1)S(1)}, bf16[24,1920]{1,0:T(8,128)(2,1)S(1)}, u32[]{:S(2)}, u32[]{:S(2)}) collective-permute-start(bf16[24,1920]{1,0:T(8,128)(2,1)S(1)} %get-tuple-element.31), channel_id=1, source_target_pairs={{0,24},{8,16},{16,8},{24,0},{1,25},{9,17},{17,9},{25,1},{2,26},{10... | collective-permute-start | bytes 276488 | tf_op jit(solution)/shard_map/ppermute | solution.py:13
  6.2 7.8 %collective-permute-start.1 = (bf16[24,1920]{1,0:T(8,128)(2,1)S(1)}, bf16[24,1920]{1,0:T(8,128)(2,1)S(1)}, u32[]{:S(2)}, u32[]{:S(2)}) collective-permute-start(bf16[24,1920]{1,0:T(8,128)(2,1)S(1)} %get-tuple-element.31), channel_id=1, source_target_pairs={{0,16},{8,24},{16,0},{24,8},{1,17},{9,25},{17,1},{25,9},{2,18},{10... | collective-permute-start | bytes 276488 | tf_op jit(solution)/shard_map/ppermute | solution.py:13
  6.2 12.8 %collective-permute-start.3 = (bf16[96,1920]{1,0:T(8,128)(2,1)S(1)}, bf16[96,1920]{1,0:T(8,128)(2,1)S(1)}, u32[]{:S(2)}, u32[]{:S(2)}) collective-permute-start(bf16[96,1920]{1,0:T(8,128)(2,1)S(1)} %get-tuple-element.32.x_ref), channel_id=1, source_target_pairs={{0,8},{8,0},{16,24},{24,16},{1,9},{9,1},{17,25},{25,17},{2,10},{10... | collective-permute-start | bytes 1105928 | tf_op jit(solution)/shard_map/ppermute | solution.py:13
  9.4 8.1 %collective-permute-start.7 = (bf16[96,1024]{1,0:T(8,128)(2,1)S(1)}, bf16[96,1024]{1,0:T(8,128)(2,1)S(1)}, u32[]{:S(2)}, u32[]{:S(2)}) collective-permute-start(bf16[96,1024]{1,0:T(8,128)(2,1)S(1)} %get-tuple-element.33.part_ref), channel_id=1, source_target_pairs={{0,1},{1,0},{2,3},{3,2},{4,5},{5,4},{6,7},{7,6},{8,9},{9,8},{10,11... | collective-permute-start | bytes 589832 | tf_op jit(solution)/shard_map/ppermute | solution.py:13
  14.0 6.6 %collective-permute-start.2 = (bf16[48,1920]{1,0:T(8,128)(2,1)S(1)}, bf16[48,1920]{1,0:T(8,128)(2,1)S(1)}, u32[]{:S(2)}, u32[]{:S(2)}) collective-permute-start(bf16[48,1920]{1,0:T(8,128)(2,1)S(1)} %get-tuple-element.63), channel_id=1, source_target_pairs={{0,2},{2,0},{4,6},{6,4},{1,3},{3,1},{5,7},{7,5},{8,10},{10,8},{12,... | collective-permute-start | bytes 552968 | tf_op jit(solution)/shard_map/ppermute | solution.py:13
  15.6 7.4 %collective-permute-start.4 = (bf16[48,1920]{1,0:T(8,128)(2,1)S(1)}, bf16[48,1920]{1,0:T(8,128)(2,1)S(1)}, u32[]{:S(2)}, u32[]{:S(2)}) collective-permute-start(bf16[48,1920]{1,0:T(8,128)(2,1)S(1)} %get-tuple-element.63), channel_id=1, source_target_pairs={{0,4},{2,6},{4,0},{6,2},{1,5},{3,7},{5,1},{7,3},{8,12},{10,14},{12... | collective-permute-start | bytes 552968 | tf_op jit(solution)/shard_map/ppermute | solution.py:13
  17.1 6.0 %collective-permute-start.6 = (bf16[24,1920]{1,0:T(8,128)(2,1)S(1)}, bf16[24,1920]{1,0:T(8,128)(2,1)S(1)}, u32[]{:S(2)}, u32[]{:S(2)}) collective-permute-start(bf16[24,1920]{1,0:T(8,128)(2,1)S(1)} %collective-permute-done), channel_id=1, source_target_pairs={{0,6},{2,4},{4,2},{6,0},{1,7},{3,5},{5,3},{7,1},{8,14},{10,12},{12... | collective-permute-start | bytes 276488 | tf_op jit(solution)/shard_map/ppermute | solution.py:13
  18.1 6.1 %collective-permute-start.8 = (bf16[24,1920]{1,0:T(8,128)(2,1)S(1)}, bf16[24,1920]{1,0:T(8,128)(2,1)S(1)}, u32[]{:S(2)}, u32[]{:S(2)}) collective-permute-start(bf16[24,1920]{1,0:T(8,128)(2,1)S(1)} %get-tuple-element.41), channel_id=1, source_target_pairs={{0,16},{8,24},{16,0},{24,8},{1,17},{9,25},{17,1},{25,9},{2,18},{10... | collective-permute-start | bytes 276488 | tf_op jit(solution)/shard_map/ppermute | solution.py:13
  19.7 3.3 %collective-permute-start.5 = (bf16[96,1024]{1,0:T(8,128)(2,1)S(1)}, bf16[96,1024]{1,0:T(8,128)(2,1)S(1)}, u32[]{:S(2)}, u32[]{:S(2)}) collective-permute-start(bf16[96,1024]{1,0:T(8,128)(2,1)S(1)} %shard_map.66.part_ref), channel_id=1, source_target_pairs={{0,1},{1,0},{2,3},{3,2},{4,5},{5,4},{6,7},{7,6},{8,9},{9,8},{10,11... | collective-permute-start | bytes 589832 | tf_op jit(solution)/shard_map/ppermute | solution.py:13
  25.1 1.8 %collective-permute-start.9 = (bf16[192,1024]{1,0:T(8,128)(2,1)S(1)}, bf16[192,1024]{1,0:T(8,128)(2,1)S(1)}, u32[]{:S(2)}, u32[]{:S(2)}) collective-permute-start(bf16[192,1024]{1,0:T(8,128)(2,1)S(1)} %shard_map.68.part_ref), channel_id=1, source_target_pairs={{0,1},{1,0},{2,3},{3,2},{4,5},{5,4},{6,7},{7,6},{8,9},{9,8},{10,11... | collective-permute-start | bytes 1179656 | tf_op jit(solution)/shard_map/ppermute | solution.py:13
  25.6 13.9 %collective-permute-start.15 = (bf16[96,1792]{1,0:T(8,128)(2,1)S(1)}, bf16[96,1792]{1,0:T(8,128)(2,1)S(1)}, u32[]{:S(2)}, u32[]{:S(2)}) collective-permute-start(bf16[96,1792]{1,0:T(8,128)(2,1)S(1)} %shard_map.69), channel_id=1, source_target_pairs={{0,8},{8,0},{16,24},{24,16},{1,9},{9,1},{17,25},{25,17},{2,10},{10... | collective-permute-start | bytes 1032200 | tf_op jit(solution)/shard_map/ppermute | solution.py:13
  27.6 6.2 %collective-permute-start.10 = (bf16[24,1792]{1,0:T(8,128)(2,1)S(1)}, bf16[24,1792]{1,0:T(8,128)(2,1)S(1)}, u32[]{:S(2)}, u32[]{:S(2)}) collective-permute-start(bf16[24,1792]{1,0:T(8,128)(2,1)S(1)} %get-tuple-element.58), channel_id=1, source_target_pairs={{0,6},{2,4},{4,2},{6,0},{1,7},{3,5},{5,3},{7,1},{8,14},{10,12},{12... | collective-permute-start | bytes 258056 | tf_op jit(solution)/shard_map/ppermute | solution.py:13
  30.1 6.8 %collective-permute-start.11 = (bf16[48,1792]{1,0:T(8,128)(2,1)S(1)}, bf16[48,1792]{1,0:T(8,128)(2,1)S(1)}, u32[]{:S(2)}, u32[]{:S(2)}) collective-permute-start(bf16[48,1792]{1,0:T(8,128)(2,1)S(1)} %get-tuple-element.60), channel_id=1, source_target_pairs={{0,2},{2,0},{4,6},{6,4},{1,3},{3,1},{5,7},{7,5},{8,10},{10,8},{12,... | collective-permute-start | bytes 516104 | tf_op jit(solution)/shard_map/ppermute | solution.py:13
  30.7 6.3 %collective-permute-start.12 = (bf16[48,1792]{1,0:T(8,128)(2,1)S(1)}, bf16[48,1792]{1,0:T(8,128)(2,1)S(1)}, u32[]{:S(2)}, u32[]{:S(2)}) collective-permute-start(bf16[48,1792]{1,0:T(8,128)(2,1)S(1)} %get-tuple-element.59), channel_id=1, source_target_pairs={{0,4},{2,6},{4,0},{6,2},{1,5},{3,7},{5,1},{7,3},{8,12},{10,14},{12... | collective-permute-start | bytes 516104 | tf_op jit(solution)/shard_map/ppermute | solution.py:13
  31.2 8.3 %collective-permute-start.16 = (bf16[24,1792]{1,0:T(8,128)(2,1)S(1)}, bf16[24,1792]{1,0:T(8,128)(2,1)S(1)}, u32[]{:S(2)}, u32[]{:S(2)}) collective-permute-start(bf16[24,1792]{1,0:T(8,128)(2,1)S(1)} %get-tuple-element.57), channel_id=1, source_target_pairs={{0,16},{8,24},{16,0},{24,8},{1,17},{9,25},{17,1},{25,9},{2,18},{10... | collective-permute-start | bytes 258056 | tf_op jit(solution)/shard_map/ppermute | solution.py:13
  37.0 6.7 %collective-permute-start.13 = (bf16[24,1792]{1,0:T(8,128)(2,1)S(1)}, bf16[24,1792]{1,0:T(8,128)(2,1)S(1)}, u32[]{:S(2)}, u32[]{:S(2)}) collective-permute-start(bf16[24,1792]{1,0:T(8,128)(2,1)S(1)} %get-tuple-element.61), channel_id=1, source_target_pairs={{0,24},{8,16},{16,8},{24,0},{1,25},{9,17},{17,9},{25,1},{2,26},{10... | collective-permute-start | bytes 258056 | tf_op jit(solution)/shard_map/ppermute | solution.py:13
  39.0 8.3 %collective-permute-start.14 = (bf16[24,1792]{1,0:T(8,128)(2,1)S(1)}, bf16[24,1792]{1,0:T(8,128)(2,1)S(1)}, u32[]{:S(2)}, u32[]{:S(2)}) collective-permute-start(bf16[24,1792]{1,0:T(8,128)(2,1)S(1)} %get-tuple-element.62), channel_id=1, source_target_pairs={{0,16},{8,24},{16,0},{24,8},{1,17},{9,25},{17,1},{25,9},{2,18},{10... | collective-permute-start | bytes 258056 | tf_op jit(solution)/shard_map/ppermute | solution.py:13
  39.6 7.7 %collective-permute-start.17 = (bf16[24,1792]{1,0:T(8,128)(2,1)S(1)}, bf16[24,1792]{1,0:T(8,128)(2,1)S(1)}, u32[]{:S(2)}, u32[]{:S(2)}) collective-permute-start(bf16[24,1792]{1,0:T(8,128)(2,1)S(1)} %get-tuple-element.49), channel_id=1, source_target_pairs={{0,6},{2,4},{4,2},{6,0},{1,7},{3,5},{5,3},{7,1},{8,14},{10,12},{12... | collective-permute-start | bytes 258056 | tf_op jit(solution)/shard_map/ppermute | solution.py:13
  41.9 5.4 %collective-permute-start.18 = (bf16[24,1792]{1,0:T(8,128)(2,1)S(1)}, bf16[24,1792]{1,0:T(8,128)(2,1)S(1)}, u32[]{:S(2)}, u32[]{:S(2)}) collective-permute-start(bf16[24,1792]{1,0:T(8,128)(2,1)S(1)} %get-tuple-element.50), channel_id=1, source_target_pairs={{0,2},{2,0},{4,6},{6,4},{1,3},{3,1},{5,7},{7,5},{8,10},{10,8},{12,... | collective-permute-start | bytes 258056 | tf_op jit(solution)/shard_map/ppermute | solution.py:13
  42.5 4.9 %collective-permute-start.19 = (bf16[24,1792]{1,0:T(8,128)(2,1)S(1)}, bf16[24,1792]{1,0:T(8,128)(2,1)S(1)}, u32[]{:S(2)}, u32[]{:S(2)}) collective-permute-start(bf16[24,1792]{1,0:T(8,128)(2,1)S(1)} %get-tuple-element.51), channel_id=1, source_target_pairs={{0,4},{2,6},{4,0},{6,2},{1,5},{3,7},{5,1},{7,3},{8,12},{10,14},{12... | collective-permute-start | bytes 258056 | tf_op jit(solution)/shard_map/ppermute | solution.py:13

commit v6 on v5

--- a/solution.py
+++ b/solution.py
@@ -192,42 +192,46 @@
         x, part, other = state
         return finish(x, part, after(other, *others), down, group_size)
 
-    partners = sorted(range(1, local_count), key=lambda j: (-j.bit_count(), j))
-
-    def exchanged(blocks):
-        return [swap(block, "local", j) for j, block in zip(partners, blocks)]
-
-    def moved(blocks):
-        return exchanged([blocks[j] for j in partners])
+    gather_order = sorted(range(1, local_count), key=lambda j: (j.bit_count(), -j))
+    sum_order = sorted(range(1, local_count), key=lambda j: (-j.bit_count(), j))
+
+    def exchanged(blocks, order):
+        return [swap(block, "local", j) for j, block in zip(order, blocks)]
 
     def summed(values):
         return sum(value.astype(jnp.float32) for value in values)
 
     arrived[far[0]] = after(arrived[far[0]], part_own)
     joined = jnp.concatenate([arrived[k] for k in far], axis=0)
-    others = moved([joined] * (local_count - 1) + [jnp.concatenate([arrived[k] for k in far[:-1]], axis=0)])
+    fewer = jnp.concatenate([arrived[k] for k in far[:-1]], axis=0)
+    others = exchanged([fewer if j == local_count - 1 else joined for j in gather_order], gather_order)
     out_own = complete((everything, part_own, swap(part_own, "cuts", 1)))
-    direct = swap(after(opposite, out_own), "node", far[-1])
+    direct = swap(after(opposite, *arrived.values()), "node", far[-1])
     near_state = begin(near)
+    out_near = complete(near_state)
     others[1] = after(others[1], near_state[1])
-    others[2] = after(others[2], near_state[2])
-    by_partner = [joined] + [others[partners.index(j)] for j in range(1, local_count)] + [direct]
+    others[2] = after(others[2], out_near)
+    by_partner = [joined] + [others[gather_order.index(j)] for j in range(1, local_count)] + [direct]
     state = begin(after(jnp.concatenate(by_partner, axis=0), out_own))
-    out_near = complete(near_state, state[1])
     near_back = swap(out_near, "node", 1)
     out_far = complete(state, out_near)
     blocks = split(out_far)
     direct_back = swap(blocks[-1][-rows:], "node", far[-1])
     blocks[-1] = blocks[-1][:-rows]
-    first, *others = moved(blocks)
-    begun = summed([blocks[0][:-rows], first])
-    begun, *others = lax.optimization_barrier((begun, *others))
+    got = dict(zip(sum_order, exchanged([blocks[j] for j in sum_order], sum_order)))
+    def piece(j, i):
+        return got[j][i * rows : (i + 1) * rows]
+
+    begun = summed([blocks[0][:-rows], got[local_count - 1]])
+    rest = [j for j in sum_order if j != local_count - 1]
+    begun, *values = lax.optimization_barrier((begun, *[got[j] for j in rest]))
+    got.update(zip(rest, values))
     done = [begun[i * rows : (i + 1) * rows] for i in range(len(far) - 1)] + [blocks[0][-rows:].astype(jnp.float32)]
-    done = [(v + summed([o[i * rows : (i + 1) * rows] for o in others])).astype(jnp.bfloat16) for i, v in enumerate(done)]
+    done = [(value + summed([piece(j, i) for j in rest])).astype(jnp.bfloat16) for i, value in enumerate(done)]
     back = [swap(value, "node", k) for value, k in zip(done, far)]
     out_own = after(out_own, *done)
-    mine, *blocks = merge(rows, partners, out_own, near_back, direct_back)
-    later = exchanged(blocks)
+    mine, *blocks = merge(rows, sum_order, out_own, near_back, direct_back)
+    later = exchanged(blocks, sum_order)
     total, *later = lax.optimization_barrier((summed(back), *later))
     return (total + summed([mine, *later])).astype(jnp.bfloat16)
 
@@ -294,6 +298,7 @@
     capacity = (5 * tok_count * top_count + 4 * expert_count - 1) // (4 * expert_count)
     powers = all(size & (size - 1) == 0 for size in (node_count, local_count))
     everywhere = node_count == top_count // 2 and capacity >= tok_count and expert_count <= LANES
+    everywhere = everywhere and node_count > 2 and local_count > 2
     chosen = dense_on_device if everywhere and powers and tok_count % local_count == 0 else slots_on_device
     return chosen(tokens, expert_ids, affinity, w_gate, w_up, w_down)
 

time: 48.2 us -> 47.5 us (0.985)
  waiting for transfers between devices: 18.7 us -> 17.7 us
    ppermute x20, waiting for transfers between devices: 18.7 us -> 17.7 us  [swap(): return lax.ppermute(value, axis, [(i, i ^ bits) for i in range(size)])]
where the time goes in v6:
time: 47.5 us; the launch traced here: 47.3 us
  starting transfers between devices  21.6 us (45%)
  waiting for transfers between devices  17.7 us (37%)
  Pallas kernels  6.97 us (15%)
  other arithmetic  0.8 us (2%)
    ppermute x20, starting transfers between devices, swap(): return lax.ppermute(value, axis, [(i, i ^ bits) for i in range(size)])  21.6 us
    ppermute x20, waiting for transfers between devices, swap(): return lax.ppermute(value, axis, [(i, i ^ bits) for i in range(size)])  17.7 us
    pallas_call x6, Pallas kernels, in_vmem(): pl.pallas_call(body, out_shape=out_shapes, in_specs=[pl.BlockSpec(memory_...  3.31 us
    pallas_call x1, Pallas kernels, load_and_project(): pl.pallas_call(body, out_shape=(shape(count, 2 * hid), *(shape(*w.shape)...  2.63 us
    pallas_call x1, Pallas kernels, prepare(): pl.pallas_call(body, out_shape=(shape(tok_count, width + LANES), *[shape(...  1.03 us
  transfers between devices with their start and end apart: 20, of which 12 were waited for; matrix products, arithmetic and copies ran while one was open for 0% of the time, Pallas kernels for 11%

profile of v6, /device:TPU:0, one launch (start us, length us, event | category | flops | bytes accessed | tf_op | source)
XLA Modules:
  0.0 47.3 jit_solution(14412547294548965786)
XLA Ops:
  0.0 1.0 %shard_map.64 = (bf16[96,1920]{1,0:T(8,128)(2,1)S(1)}, bf16[24,1920]{1,0:T(8,128)(2,1)S(1)}, bf16[24,1920]{1,0:T(8,128)(2,1)S(1)}) custom-call(bf16[96,1792]{1,0:T(8,128)(2,1)} %tokens_hbm.1, s32[8,96]{1,0:T(8,128)} %bitcast.8, f32[8,96]{1,0:T(8,128)} %bitcast.9), custom_call_target="tpu_custom_call" | custom-call | flops 1000000 | bytes 1048576 | tf_op jit(solution)/shard_map/pallas_call | solution.py:73
  1.0 5.1 %collective-permute-start = (bf16[24,1920]{1,0:T(8,128)(2,1)S(1)}, bf16[24,1920]{1,0:T(8,128)(2,1)S(1)}, u32[]{:S(2)}, u32[]{:S(2)}) collective-permute-start(bf16[24,1920]{1,0:T(8,128)(2,1)S(1)} %get-tuple-element.30), channel_id=1, source_target_pairs={{0,24},{8,16},{16,8},{24,0},{1,25},{9,17},{17,9},{25,1},{2,26},{10... | collective-permute-start | bytes 276488 | tf_op jit(solution)/shard_map/ppermute | solution.py:13
  6.2 0.6 %collective-permute-start.3 = (bf16[96,1920]{1,0:T(8,128)(2,1)S(1)}, bf16[96,1920]{1,0:T(8,128)(2,1)S(1)}, u32[]{:S(2)}, u32[]{:S(2)}) collective-permute-start(bf16[96,1920]{1,0:T(8,128)(2,1)S(1)} %get-tuple-element.31.x_ref), channel_id=1, source_target_pairs={{0,8},{8,0},{16,24},{24,16},{1,9},{9,1},{17,25},{25,17},{2,10},{10... | collective-permute-start | bytes 1105928 | tf_op jit(solution)/shard_map/ppermute | solution.py:13
  6.8 2.6 %shard_map.65 = (bf16[96,1024]{1,0:T(8,128)(2,1)S(1)}, bf16[1792,512]{1,0:T(8,128)(2,1)S(1)}, bf16[1792,512]{1,0:T(8,128)(2,1)S(1)}, bf16[512,1792]{1,0:T(8,128)(2,1)S(1)}) custom-call(bf16[96,1920]{1,0:T(8,128)(2,1)S(1)} %get-tuple-element.31.x_ref, bf16[1792,512]{1,0:T(8,128)(2,1)} %bitcast.5, bf16[1792,512]{1,0:T(8,128)(2,1)} %bitcast.6, ...), custom_call_target="tpu_custom_call" | custom-call | tf_op jit(solution)/shard_map/pallas_call | solution.py:119
  9.6 4.4 %collective-permute-done.1 = bf16[24,1920]{1,0:T(8,128)(2,1)S(1)} collective-permute-done((bf16[24,1920]{1,0:T(8,128)(2,1)S(1)}, bf16[24,1920]{1,0:T(8,128)(2,1)S(1)}, u32[]{:S(2)}, u32[]{:S(2)}) %collective-permute-start.1) | collective-permute-done | bytes 92192 | tf_op jit(solution)/shard_map/ppermute | solution.py:13
  14.0 1.6 %collective-permute-start.2 = (bf16[48,1920]{1,0:T(8,128)(2,1)S(1)}, bf16[48,1920]{1,0:T(8,128)(2,1)S(1)}, u32[]{:S(2)}, u32[]{:S(2)}) collective-permute-start(bf16[48,1920]{1,0:T(8,128)(2,1)S(1)} %get-tuple-element.61), channel_id=1, source_target_pairs={{0,2},{2,0},{4,6},{6,4},{1,3},{3,1},{5,7},{7,5},{8,10},{10,8},{12,... | collective-permute-start | bytes 552968 | tf_op jit(solution)/shard_map/ppermute | solution.py:13
  15.6 1.5 %collective-permute-start.4 = (bf16[48,1920]{1,0:T(8,128)(2,1)S(1)}, bf16[48,1920]{1,0:T(8,128)(2,1)S(1)}, u32[]{:S(2)}, u32[]{:S(2)}) collective-permute-start(bf16[48,1920]{1,0:T(8,128)(2,1)S(1)} %get-tuple-element.61), channel_id=1, source_target_pairs={{0,4},{2,6},{4,0},{6,2},{1,5},{3,7},{5,1},{7,3},{8,12},{10,14},{12... | collective-permute-start | bytes 552968 | tf_op jit(solution)/shard_map/ppermute | solution.py:13
  17.1 0.5 %collective-permute-start.5 = (bf16[24,1920]{1,0:T(8,128)(2,1)S(1)}, bf16[24,1920]{1,0:T(8,128)(2,1)S(1)}, u32[]{:S(2)}, u32[]{:S(2)}) collective-permute-start(bf16[24,1920]{1,0:T(8,128)(2,1)S(1)} %collective-permute-done), channel_id=1, source_target_pairs={{0,6},{2,4},{4,2},{6,0},{1,7},{3,5},{5,3},{7,1},{8,14},{10,12},{12... | collective-permute-start | bytes 276488 | tf_op jit(solution)/shard_map/ppermute | solution.py:13
  17.6 0.6 %collective-permute-start.7 = (bf16[24,1920]{1,0:T(8,128)(2,1)S(1)}, bf16[24,1920]{1,0:T(8,128)(2,1)S(1)}, u32[]{:S(2)}, u32[]{:S(2)}) collective-permute-start(bf16[24,1920]{1,0:T(8,128)(2,1)S(1)} %get-tuple-element.40), channel_id=1, source_target_pairs={{0,16},{8,24},{16,0},{24,8},{1,17},{9,25},{17,1},{25,9},{2,18},{10... | collective-permute-start | bytes 276488 | tf_op jit(solution)/shard_map/ppermute | solution.py:13
  18.2 0.5 %shard_map.68.own_ref = bf16[96,1792]{1,0:T(8,128)(2,1)S(1)} custom-call(bf16[96,1920]{1,0:T(8,128)(2,1)S(1)} %get-tuple-element.31.x_ref, bf16[96,1024]{1,0:T(8,128)(2,1)S(1)} %get-tuple-element.32.part_ref, bf16[96,1024]{1,0:T(8,128)(2,1)S(1)} %collective-permute-done.8.other_ref, bf16[512,1792]{1,0:T(8,128)(2,1)S(1)} %get-tuple-element.37.down_ref), custom_call_target="tpu_custom_call" | custom-call | flops 176160768 | bytes 1048576 | tf_op jit(solution)/shard_map/pallas_call | solution.py:22
  18.7 0.3 collective-permute-done.3.x_ref
  19.0 0.7 %shard_map.66.part_ref = bf16[96,1024]{1,0:T(8,128)(2,1)S(1)} custom-call(bf16[96,1920]{1,0:T(8,128)(2,1)S(1)} %collective-permute-done.3.x_ref, bf16[1792,512]{1,0:T(8,128)(2,1)S(1)} %get-tuple-element.34.gate_ref, bf16[1792,512]{1,0:T(8,128)(2,1)S(1)} %get-tuple-element.35.up_ref), custom_call_target="tpu_custom_call" | custom-call | flops 352321536 | bytes 1048576 | tf_op jit(solution)/shard_map/pallas_call | solution.py:22
  19.8 0.9 %collective-permute-done.2 = bf16[48,1920]{1,0:T(8,128)(2,1)S(1)} collective-permute-done((bf16[48,1920]{1,0:T(8,128)(2,1)S(1)}, bf16[48,1920]{1,0:T(8,128)(2,1)S(1)}, u32[]{:S(2)}, u32[]{:S(2)}) %collective-permute-start.2) | collective-permute-done | bytes 184352 | tf_op jit(solution)/shard_map/ppermute | solution.py:13
  20.7 2.3 %collective-permute-done.4 = bf16[48,1920]{1,0:T(8,128)(2,1)S(1)} collective-permute-done((bf16[48,1920]{1,0:T(8,128)(2,1)S(1)}, bf16[48,1920]{1,0:T(8,128)(2,1)S(1)}, u32[]{:S(2)}, u32[]{:S(2)}) %collective-permute-start.4) | collective-permute-done | bytes 184352 | tf_op jit(solution)/shard_map/ppermute | solution.py:13
  23.0 0.5 %shard_map.67 = bf16[96,1792]{1,0:T(8,128)(2,1)S(1)} custom-call(bf16[96,1920]{1,0:T(8,128)(2,1)S(1)} %collective-permute-done.3.x_ref, bf16[96,1024]{1,0:T(8,128)(2,1)S(1)} %shard_map.66.part_ref, bf16[96,1024]{1,0:T(8,128)(2,1)S(1)} %collective-permute-done.6.other_ref, bf16[512,1792]{1,0:T(8,128)(2,1)S(1)} %get-tuple-element.37.down_ref), custom_call_target="tpu_custom_call" | custom-call | flops 176160768 | bytes 1048576 | tf_op jit(solution)/shard_map/pallas_call | solution.py:22
  23.6 0.9 %shard_map.69.part_ref = bf16[192,1024]{1,0:T(8,128)(2,1)S(1)} custom-call(bf16[192,1920]{1,0:T(8,128)(2,1)S(1)} %constant_dynamic-update-slice_fusion.2.x_ref, bf16[1792,512]{1,0:T(8,128)(2,1)S(1)} %get-tuple-element.34.gate_ref, bf16[1792,512]{1,0:T(8,128)(2,1)S(1)} %get-tuple-element.35.up_ref), custom_call_target="tpu_custom_call" | custom-call | flops 704643072 | bytes 1048576 | tf_op jit(solution)/shard_map/pallas_call | solution.py:22
  24.6 0.7 %collective-permute-start.15 = (bf16[96,1792]{1,0:T(8,128)(2,1)S(1)}, bf16[96,1792]{1,0:T(8,128)(2,1)S(1)}, u32[]{:S(2)}, u32[]{:S(2)}) collective-permute-start(bf16[96,1792]{1,0:T(8,128)(2,1)S(1)} %shard_map.67), channel_id=1, source_target_pairs={{0,8},{8,0},{16,24},{24,16},{1,9},{9,1},{17,25},{25,17},{2,10},{10... | collective-permute-start | bytes 1032200 | tf_op jit(solution)/shard_map/ppermute | solution.py:13
  25.3 1.0 %collective-permute-done.9.other_ref = bf16[192,1024]{1,0:T(8,128)(2,1)S(1)} collective-permute-done((bf16[192,1024]{1,0:T(8,128)(2,1)S(1)}, bf16[192,1024]{1,0:T(8,128)(2,1)S(1)}, u32[]{:S(2)}, u32[]{:S(2)}) %collective-permute-start.9) | collective-permute-done | bytes 393248 | tf_op jit(solution)/shard_map/ppermute | solution.py:13
  26.3 0.6 %shard_map.70 = bf16[192,1792]{1,0:T(8,128)(2,1)S(1)} custom-call(bf16[192,1920]{1,0:T(8,128)(2,1)S(1)} %constant_dynamic-update-slice_fusion.2.x_ref, bf16[192,1024]{1,0:T(8,128)(2,1)S(1)} %shard_map.69.part_ref, bf16[192,1024]{1,0:T(8,128)(2,1)S(1)} %collective-permute-done.9.other_ref, bf16[512,1792]{1,0:T(8,128)(2,1)S(1)} %get-tuple-element.37.down_ref), custom_call_target="tpu_custom_call" | custom-call | flops 352321536 | bytes 1048576 | tf_op jit(solution)/shard_map/pallas_call | solution.py:22
  27.0 2.5 %collective-permute-start.10 = (bf16[24,1792]{1,0:T(8,128)(2,1)S(1)}, bf16[24,1792]{1,0:T(8,128)(2,1)S(1)}, u32[]{:S(2)}, u32[]{:S(2)}) collective-permute-start(bf16[24,1792]{1,0:T(8,128)(2,1)S(1)} %get-tuple-element.56), channel_id=1, source_target_pairs={{0,6},{2,4},{4,2},{6,0},{1,7},{3,5},{5,3},{7,1},{8,14},{10,12},{12... | collective-permute-start | bytes 258056 | tf_op jit(solution)/shard_map/ppermute | solution.py:13
  29.5 0.6 %collective-permute-start.11 = (bf16[48,1792]{1,0:T(8,128)(2,1)S(1)}, bf16[48,1792]{1,0:T(8,128)(2,1)S(1)}, u32[]{:S(2)}, u32[]{:S(2)}) collective-permute-start(bf16[48,1792]{1,0:T(8,128)(2,1)S(1)} %get-tuple-element.58), channel_id=1, source_target_pairs={{0,2},{2,0},{4,6},{6,4},{1,3},{3,1},{5,7},{7,5},{8,10},{10,8},{12,... | collective-permute-start | bytes 516104 | tf_op jit(solution)/shard_map/ppermute | solution.py:13
  30.1 0.5 %collective-permute-start.12 = (bf16[48,1792]{1,0:T(8,128)(2,1)S(1)}, bf16[48,1792]{1,0:T(8,128)(2,1)S(1)}, u32[]{:S(2)}, u32[]{:S(2)}) collective-permute-start(bf16[48,1792]{1,0:T(8,128)(2,1)S(1)} %get-tuple-element.57), channel_id=1, source_target_pairs={{0,4},{2,6},{4,0},{6,2},{1,5},{3,7},{5,1},{7,3},{8,12},{10,14},{12... | collective-permute-start | bytes 516104 | tf_op jit(solution)/shard_map/ppermute | solution.py:13
  30.6 1.3 %collective-permute-start.16 = (bf16[24,1792]{1,0:T(8,128)(2,1)S(1)}, bf16[24,1792]{1,0:T(8,128)(2,1)S(1)}, u32[]{:S(2)}, u32[]{:S(2)}) collective-permute-start(bf16[24,1792]{1,0:T(8,128)(2,1)S(1)} %get-tuple-element.55), channel_id=1, source_target_pairs={{0,16},{8,24},{16,0},{24,8},{1,17},{9,25},{17,1},{25,9},{2,18},{10... | collective-permute-start | bytes 258056 | tf_op jit(solution)/shard_map/ppermute | solution.py:13
  31.9 1.3 %collective-permute-done.10 = bf16[24,1792]{1,0:T(8,128)(2,1)S(1)} collective-permute-done((bf16[24,1792]{1,0:T(8,128)(2,1)S(1)}, bf16[24,1792]{1,0:T(8,128)(2,1)S(1)}, u32[]{:S(2)}, u32[]{:S(2)}) %collective-permute-start.10) | collective-permute-done | bytes 86048 | tf_op jit(solution)/shard_map/ppermute | solution.py:13
  33.2 3.1 %collective-permute-done.11 = bf16[48,1792]{1,0:T(8,128)(2,1)S(1)} collective-permute-done((bf16[48,1792]{1,0:T(8,128)(2,1)S(1)}, bf16[48,1792]{1,0:T(8,128)(2,1)S(1)}, u32[]{:S(2)}, u32[]{:S(2)}) %collective-permute-start.11) | collective-permute-done | bytes 172064 | tf_op jit(solution)/shard_map/ppermute | solution.py:13
  36.5 2.3 %collective-permute-start.13 = (bf16[24,1792]{1,0:T(8,128)(2,1)S(1)}, bf16[24,1792]{1,0:T(8,128)(2,1)S(1)}, u32[]{:S(2)}, u32[]{:S(2)}) collective-permute-start(bf16[24,1792]{1,0:T(8,128)(2,1)S(1)} %get-tuple-element.59), channel_id=1, source_target_pairs={{0,24},{8,16},{16,8},{24,0},{1,25},{9,17},{17,9},{25,1},{2,26},{10... | collective-permute-start | bytes 258056 | tf_op jit(solution)/shard_map/ppermute | solution.py:13
  38.9 2.1 %collective-permute-start.17 = (bf16[24,1792]{1,0:T(8,128)(2,1)S(1)}, bf16[24,1792]{1,0:T(8,128)(2,1)S(1)}, u32[]{:S(2)}, u32[]{:S(2)}) collective-permute-start(bf16[24,1792]{1,0:T(8,128)(2,1)S(1)} %get-tuple-element.47), channel_id=1, source_target_pairs={{0,6},{2,4},{4,2},{6,0},{1,7},{3,5},{5,3},{7,1},{8,14},{10,12},{12... | collective-permute-start | bytes 258056 | tf_op jit(solution)/shard_map/ppermute | solution.py:13
  41.0 0.5 %collective-permute-start.18 = (bf16[24,1792]{1,0:T(8,128)(2,1)S(1)}, bf16[24,1792]{1,0:T(8,128)(2,1)S(1)}, u32[]{:S(2)}, u32[]{:S(2)}) collective-permute-start(bf16[24,1792]{1,0:T(8,128)(2,1)S(1)} %get-tuple-element.48), channel_id=1, source_target_pairs={{0,2},{2,0},{4,6},{6,4},{1,3},{3,1},{5,7},{7,5},{8,10},{10,8},{12,... | collective-permute-start | bytes 258056 | tf_op jit(solution)/shard_map/ppermute | solution.py:13
  41.5 0.9 %collective-permute-start.19 = (bf16[24,1792]{1,0:T(8,128)(2,1)S(1)}, bf16[24,1792]{1,0:T(8,128)(2,1)S(1)}, u32[]{:S(2)}, u32[]{:S(2)}) collective-permute-start(bf16[24,1792]{1,0:T(8,128)(2,1)S(1)} %get-tuple-element.49), channel_id=1, source_target_pairs={{0,4},{2,6},{4,0},{6,2},{1,5},{3,7},{5,1},{7,3},{8,12},{10,14},{12... | collective-permute-start | bytes 258056 | tf_op jit(solution)/shard_map/ppermute | solution.py:13
  42.5 0.7 %collective-permute-done.13 = bf16[24,1792]{1,0:T(8,128)(2,1)S(1)} collective-permute-done((bf16[24,1792]{1,0:T(8,128)(2,1)S(1)}, bf16[24,1792]{1,0:T(8,128)(2,1)S(1)}, u32[]{:S(2)}, u32[]{:S(2)}) %collective-permute-start.13) | collective-permute-done | bytes 86048 | tf_op jit(solution)/shard_map/ppermute | solution.py:13
  43.2 3.4 %collective-permute-done.14 = bf16[24,1792]{1,0:T(8,128)(2,1)S(1)} collective-permute-done((bf16[24,1792]{1,0:T(8,128)(2,1)S(1)}, bf16[24,1792]{1,0:T(8,128)(2,1)S(1)}, u32[]{:S(2)}, u32[]{:S(2)}) %collective-permute-start.14) | collective-permute-done | bytes 86048 | tf_op jit(solution)/shard_map/ppermute | solution.py:13
  46.6 0.7 %add_convert_fusion = bf16[24,1792]{1,0:T(8,128)(2,1)} fusion(f32[24,1792]{1,0:T(8,128)S(1)} %convert_add_fusion, bf16[24,1792]{1,0:T(8,128)(2,1)S(1)} %collective-permute-done.19, bf16[24,1792]{1,0:T(8,128)(2,1)S(1)} %collective-permute-done.18, bf16[24,1792]{1,0:T(8,128)(2,1)S(1)} %collective-permute-done.17, bf16[24,1792]{1,0:T(8,128)(2,1)S(1)} %get-tuple-element.51), kind=kLoop, calls=%fused_computation | loop fusion | flops 387072 | bytes 602112 | tf_op jit(solution)/shard_map/convert_element_type | solution.py:236
  (28 shorter events, 0.9 us)
Async XLA Ops:
  1.0 8.6 %collective-permute-start = (bf16[24,1920]{1,0:T(8,128)(2,1)S(1)}, bf16[24,1920]{1,0:T(8,128)(2,1)S(1)}, u32[]{:S(2)}, u32[]{:S(2)}) collective-permute-start(bf16[24,1920]{1,0:T(8,128)(2,1)S(1)} %get-tuple-element.30), channel_id=1, source_target_pairs={{0,24},{8,16},{16,8},{24,0},{1,25},{9,17},{17,9},{25,1},{2,26},{10... | collective-permute-start | bytes 276488 | tf_op jit(solution)/shard_map/ppermute | solution.py:13
  6.2 7.8 %collective-permute-start.1 = (bf16[24,1920]{1,0:T(8,128)(2,1)S(1)}, bf16[24,1920]{1,0:T(8,128)(2,1)S(1)}, u32[]{:S(2)}, u32[]{:S(2)}) collective-permute-start(bf16[24,1920]{1,0:T(8,128)(2,1)S(1)} %get-tuple-element.30), channel_id=1, source_target_pairs={{0,16},{8,24},{16,0},{24,8},{1,17},{9,25},{17,1},{25,9},{2,18},{10... | collective-permute-start | bytes 276488 | tf_op jit(solution)/shard_map/ppermute | solution.py:13
  6.2 12.8 %collective-permute-start.3 = (bf16[96,1920]{1,0:T(8,128)(2,1)S(1)}, bf16[96,1920]{1,0:T(8,128)(2,1)S(1)}, u32[]{:S(2)}, u32[]{:S(2)}) collective-permute-start(bf16[96,1920]{1,0:T(8,128)(2,1)S(1)} %get-tuple-element.31.x_ref), channel_id=1, source_target_pairs={{0,8},{8,0},{16,24},{24,16},{1,9},{9,1},{17,25},{25,17},{2,10},{10... | collective-permute-start | bytes 1105928 | tf_op jit(solution)/shard_map/ppermute | solution.py:13
  9.4 8.1 %collective-permute-start.8 = (bf16[96,1024]{1,0:T(8,128)(2,1)S(1)}, bf16[96,1024]{1,0:T(8,128)(2,1)S(1)}, u32[]{:S(2)}, u32[]{:S(2)}) collective-permute-start(bf16[96,1024]{1,0:T(8,128)(2,1)S(1)} %get-tuple-element.32.part_ref), channel_id=1, source_target_pairs={{0,1},{1,0},{2,3},{3,2},{4,5},{5,4},{6,7},{7,6},{8,9},{9,8},{10,11... | collective-permute-start | bytes 589832 | tf_op jit(solution)/shard_map/ppermute | solution.py:13
  14.0 6.6 %collective-permute-start.2 = (bf16[48,1920]{1,0:T(8,128)(2,1)S(1)}, bf16[48,1920]{1,0:T(8,128)(2,1)S(1)}, u32[]{:S(2)}, u32[]{:S(2)}) collective-permute-start(bf16[48,1920]{1,0:T(8,128)(2,1)S(1)} %get-tuple-element.61), channel_id=1, source_target_pairs={{0,2},{2,0},{4,6},{6,4},{1,3},{3,1},{5,7},{7,5},{8,10},{10,8},{12,... | collective-permute-start | bytes 552968 | tf_op jit(solution)/shard_map/ppermute | solution.py:13
  15.6 7.4 %collective-permute-start.4 = (bf16[48,1920]{1,0:T(8,128)(2,1)S(1)}, bf16[48,1920]{1,0:T(8,128)(2,1)S(1)}, u32[]{:S(2)}, u32[]{:S(2)}) collective-permute-start(bf16[48,1920]{1,0:T(8,128)(2,1)S(1)} %get-tuple-element.61), channel_id=1, source_target_pairs={{0,4},{2,6},{4,0},{6,2},{1,5},{3,7},{5,1},{7,3},{8,12},{10,14},{12... | collective-permute-start | bytes 552968 | tf_op jit(solution)/shard_map/ppermute | solution.py:13
  17.1 6.4 %collective-permute-start.5 = (bf16[24,1920]{1,0:T(8,128)(2,1)S(1)}, bf16[24,1920]{1,0:T(8,128)(2,1)S(1)}, u32[]{:S(2)}, u32[]{:S(2)}) collective-permute-start(bf16[24,1920]{1,0:T(8,128)(2,1)S(1)} %collective-permute-done), channel_id=1, source_target_pairs={{0,6},{2,4},{4,2},{6,0},{1,7},{3,5},{5,3},{7,1},{8,14},{10,12},{12... | collective-permute-start | bytes 276488 | tf_op jit(solution)/shard_map/ppermute | solution.py:13
  17.6 6.0 %collective-permute-start.7 = (bf16[24,1920]{1,0:T(8,128)(2,1)S(1)}, bf16[24,1920]{1,0:T(8,128)(2,1)S(1)}, u32[]{:S(2)}, u32[]{:S(2)}) collective-permute-start(bf16[24,1920]{1,0:T(8,128)(2,1)S(1)} %get-tuple-element.40), channel_id=1, source_target_pairs={{0,16},{8,24},{16,0},{24,8},{1,17},{9,25},{17,1},{25,9},{2,18},{10... | collective-permute-start | bytes 276488 | tf_op jit(solution)/shard_map/ppermute | solution.py:13
  19.7 3.3 %collective-permute-start.6 = (bf16[96,1024]{1,0:T(8,128)(2,1)S(1)}, bf16[96,1024]{1,0:T(8,128)(2,1)S(1)}, u32[]{:S(2)}, u32[]{:S(2)}) collective-permute-start(bf16[96,1024]{1,0:T(8,128)(2,1)S(1)} %shard_map.66.part_ref), channel_id=1, source_target_pairs={{0,1},{1,0},{2,3},{3,2},{4,5},{5,4},{6,7},{7,6},{8,9},{9,8},{10,11... | collective-permute-start | bytes 589832 | tf_op jit(solution)/shard_map/ppermute | solution.py:13
  24.5 1.8 %collective-permute-start.9 = (bf16[192,1024]{1,0:T(8,128)(2,1)S(1)}, bf16[192,1024]{1,0:T(8,128)(2,1)S(1)}, u32[]{:S(2)}, u32[]{:S(2)}) collective-permute-start(bf16[192,1024]{1,0:T(8,128)(2,1)S(1)} %shard_map.69.part_ref), channel_id=1, source_target_pairs={{0,1},{1,0},{2,3},{3,2},{4,5},{5,4},{6,7},{7,6},{8,9},{9,8},{10,11... | collective-permute-start | bytes 1179656 | tf_op jit(solution)/shard_map/ppermute | solution.py:13
  24.6 14.2 %collective-permute-start.15 = (bf16[96,1792]{1,0:T(8,128)(2,1)S(1)}, bf16[96,1792]{1,0:T(8,128)(2,1)S(1)}, u32[]{:S(2)}, u32[]{:S(2)}) collective-permute-start(bf16[96,1792]{1,0:T(8,128)(2,1)S(1)} %shard_map.67), channel_id=1, source_target_pairs={{0,8},{8,0},{16,24},{24,16},{1,9},{9,1},{17,25},{25,17},{2,10},{10... | collective-permute-start | bytes 1032200 | tf_op jit(solution)/shard_map/ppermute | solution.py:13
  27.0 6.2 %collective-permute-start.10 = (bf16[24,1792]{1,0:T(8,128)(2,1)S(1)}, bf16[24,1792]{1,0:T(8,128)(2,1)S(1)}, u32[]{:S(2)}, u32[]{:S(2)}) collective-permute-start(bf16[24,1792]{1,0:T(8,128)(2,1)S(1)} %get-tuple-element.56), channel_id=1, source_target_pairs={{0,6},{2,4},{4,2},{6,0},{1,7},{3,5},{5,3},{7,1},{8,14},{10,12},{12... | collective-permute-start | bytes 258056 | tf_op jit(solution)/shard_map/ppermute | solution.py:13
  29.5 6.7 %collective-permute-start.11 = (bf16[48,1792]{1,0:T(8,128)(2,1)S(1)}, bf16[48,1792]{1,0:T(8,128)(2,1)S(1)}, u32[]{:S(2)}, u32[]{:S(2)}) collective-permute-start(bf16[48,1792]{1,0:T(8,128)(2,1)S(1)} %get-tuple-element.58), channel_id=1, source_target_pairs={{0,2},{2,0},{4,6},{6,4},{1,3},{3,1},{5,7},{7,5},{8,10},{10,8},{12,... | collective-permute-start | bytes 516104 | tf_op jit(solution)/shard_map/ppermute | solution.py:13
  30.1 6.3 %collective-permute-start.12 = (bf16[48,1792]{1,0:T(8,128)(2,1)S(1)}, bf16[48,1792]{1,0:T(8,128)(2,1)S(1)}, u32[]{:S(2)}, u32[]{:S(2)}) collective-permute-start(bf16[48,1792]{1,0:T(8,128)(2,1)S(1)} %get-tuple-element.57), channel_id=1, source_target_pairs={{0,4},{2,6},{4,0},{6,2},{1,5},{3,7},{5,1},{7,3},{8,12},{10,14},{12... | collective-permute-start | bytes 516104 | tf_op jit(solution)/shard_map/ppermute | solution.py:13
  30.6 8.2 %collective-permute-start.16 = (bf16[24,1792]{1,0:T(8,128)(2,1)S(1)}, bf16[24,1792]{1,0:T(8,128)(2,1)S(1)}, u32[]{:S(2)}, u32[]{:S(2)}) collective-permute-start(bf16[24,1792]{1,0:T(8,128)(2,1)S(1)} %get-tuple-element.55), channel_id=1, source_target_pairs={{0,16},{8,24},{16,0},{24,8},{1,17},{9,25},{17,1},{25,9},{2,18},{10... | collective-permute-start | bytes 258056 | tf_op jit(solution)/shard_map/ppermute | solution.py:13
  36.5 6.7 %collective-permute-start.13 = (bf16[24,1792]{1,0:T(8,128)(2,1)S(1)}, bf16[24,1792]{1,0:T(8,128)(2,1)S(1)}, u32[]{:S(2)}, u32[]{:S(2)}) collective-permute-start(bf16[24,1792]{1,0:T(8,128)(2,1)S(1)} %get-tuple-element.59), channel_id=1, source_target_pairs={{0,24},{8,16},{16,8},{24,0},{1,25},{9,17},{17,9},{25,1},{2,26},{10... | collective-permute-start | bytes 258056 | tf_op jit(solution)/shard_map/ppermute | solution.py:13
  38.8 7.8 %collective-permute-start.14 = (bf16[24,1792]{1,0:T(8,128)(2,1)S(1)}, bf16[24,1792]{1,0:T(8,128)(2,1)S(1)}, u32[]{:S(2)}, u32[]{:S(2)}) collective-permute-start(bf16[24,1792]{1,0:T(8,128)(2,1)S(1)} %get-tuple-element.60), channel_id=1, source_target_pairs={{0,16},{8,24},{16,0},{24,8},{1,17},{9,25},{17,1},{25,9},{2,18},{10... | collective-permute-start | bytes 258056 | tf_op jit(solution)/shard_map/ppermute | solution.py:13
  38.9 7.7 %collective-permute-start.17 = (bf16[24,1792]{1,0:T(8,128)(2,1)S(1)}, bf16[24,1792]{1,0:T(8,128)(2,1)S(1)}, u32[]{:S(2)}, u32[]{:S(2)}) collective-permute-start(bf16[24,1792]{1,0:T(8,128)(2,1)S(1)} %get-tuple-element.47), channel_id=1, source_target_pairs={{0,6},{2,4},{4,2},{6,0},{1,7},{3,5},{5,3},{7,1},{8,14},{10,12},{12... | collective-permute-start | bytes 258056 | tf_op jit(solution)/shard_map/ppermute | solution.py:13
  41.0 5.6 %collective-permute-start.18 = (bf16[24,1792]{1,0:T(8,128)(2,1)S(1)}, bf16[24,1792]{1,0:T(8,128)(2,1)S(1)}, u32[]{:S(2)}, u32[]{:S(2)}) collective-permute-start(bf16[24,1792]{1,0:T(8,128)(2,1)S(1)} %get-tuple-element.48), channel_id=1, source_target_pairs={{0,2},{2,0},{4,6},{6,4},{1,3},{3,1},{5,7},{7,5},{8,10},{10,8},{12,... | collective-permute-start | bytes 258056 | tf_op jit(solution)/shard_map/ppermute | solution.py:13
  41.5 5.1 %collective-permute-start.19 = (bf16[24,1792]{1,0:T(8,128)(2,1)S(1)}, bf16[24,1792]{1,0:T(8,128)(2,1)S(1)}, u32[]{:S(2)}, u32[]{:S(2)}) collective-permute-start(bf16[24,1792]{1,0:T(8,128)(2,1)S(1)} %get-tuple-element.49), channel_id=1, source_target_pairs={{0,4},{2,6},{4,0},{6,2},{1,5},{3,7},{5,1},{7,3},{8,12},{10,14},{12... | collective-permute-start | bytes 258056 | tf_op jit(solution)/shard_map/ppermute | solution.py:13

commit v7 on v6

--- a/solution.py
+++ b/solution.py
@@ -180,8 +180,8 @@
         return [value[j * step : (j + 1) * step] for j in range(local_count)]
 
     everything, own, opposite = prepare(tokens, expert_ids, affinity, rows)
+    near = swap(everything, "node", 1)
     arrived = {k: swap(own, "node", k) for k in far}
-    near = swap(everything, "node", 1)
     part_own, gate, up, down = load_and_project(everything, w_gate[0], w_up[0], w_down[0])
 
     def begin(x):
@@ -192,8 +192,8 @@
         x, part, other = state
         return finish(x, part, after(other, *others), down, group_size)
 
-    gather_order = sorted(range(1, local_count), key=lambda j: (j.bit_count(), -j))
-    sum_order = sorted(range(1, local_count), key=lambda j: (-j.bit_count(), j))
+    sum_order = list(range(1, local_count))
+    gather_order = sorted(sum_order, key=lambda j: (-j.bit_count(), j))
 
     def exchanged(blocks, order):
         return [swap(block, "local", j) for j, block in zip(order, blocks)]
@@ -207,18 +207,19 @@
     others = exchanged([fewer if j == local_count - 1 else joined for j in gather_order], gather_order)
     out_own = complete((everything, part_own, swap(part_own, "cuts", 1)))
     direct = swap(after(opposite, *arrived.values()), "node", far[-1])
-    near_state = begin(near)
+    near_state = begin(after(near, out_own))
     out_near = complete(near_state)
     others[1] = after(others[1], near_state[1])
     others[2] = after(others[2], out_near)
     by_partner = [joined] + [others[gather_order.index(j)] for j in range(1, local_count)] + [direct]
-    state = begin(after(jnp.concatenate(by_partner, axis=0), out_own))
+    state = begin(jnp.concatenate(by_partner, axis=0))
     near_back = swap(out_near, "node", 1)
     out_far = complete(state, out_near)
     blocks = split(out_far)
-    direct_back = swap(blocks[-1][-rows:], "node", far[-1])
+    direct_back = swap(after(blocks[-1][-rows:], out_near), "node", far[-1])
     blocks[-1] = blocks[-1][:-rows]
     got = dict(zip(sum_order, exchanged([blocks[j] for j in sum_order], sum_order)))
+
     def piece(j, i):
         return got[j][i * rows : (i + 1) * rows]
 
@@ -230,10 +231,13 @@
     done = [(value + summed([piece(j, i) for j in rest])).astype(jnp.bfloat16) for i, value in enumerate(done)]
     back = [swap(value, "node", k) for value, k in zip(done, far)]
     out_own = after(out_own, *done)
-    mine, *blocks = merge(rows, sum_order, out_own, near_back, direct_back)
-    later = exchanged(blocks, sum_order)
-    total, *later = lax.optimization_barrier((summed(back), *later))
-    return (total + summed([mine, *later])).astype(jnp.bfloat16)
+    mine, *blocks = merge(rows, gather_order, out_own, near_back, direct_back)
+    later = exchanged(blocks, gather_order)
+    *back, last = back
+    total = summed([*back, mine])
+    total, *later = lax.optimization_barrier((total, *later))
+    total, last = lax.optimization_barrier((total + summed(later), last))
+    return (total + last.astype(jnp.float32)).astype(jnp.bfloat16)
 
 
 def slots_on_device(tokens, expert_ids, affinity, w_gate, w_up, w_down):

time: 47.5 us -> 47.3 us (level)
  waiting for transfers between devices: 17.7 us -> 17 us
  starting transfers between devices: 21.6 us -> 22.1 us
    ppermute x20, waiting for transfers between devices: 17.7 us -> 17 us  [swap(): return lax.ppermute(value, axis, [(i, i ^ bits) for i in range(size)])]
    ppermute x20, starting transfers between devices: 21.6 us -> 22.1 us  [swap(): return lax.ppermute(value, axis, [(i, i ^ bits) for i in range(size)])]
  transfers between devices with their start and end apart: 20 -> 20, of which waited for: 12 -> 14; matrix products, arithmetic and copies ran while one was open for 0% -> 1% of each run, Pallas kernels for 11% -> 11%
where the time goes in v7:
time: 47.3 us; the launch traced here: 47.1 us
  starting transfers between devices  22.1 us (47%)
  waiting for transfers between devices  17 us (36%)
  Pallas kernels  6.95 us (15%)
  other arithmetic  0.8 us (2%)
    ppermute x20, starting transfers between devices, swap(): return lax.ppermute(value, axis, [(i, i ^ bits) for i in range(size)])  22.1 us
    ppermute x20, waiting for transfers between devices, swap(): return lax.ppermute(value, axis, [(i, i ^ bits) for i in range(size)])  17 us
    pallas_call x6, Pallas kernels, in_vmem(): pl.pallas_call(body, out_shape=out_shapes, in_specs=[pl.BlockSpec(memory_...  3.29 us
    pallas_call x1, Pallas kernels, load_and_project(): pl.pallas_call(body, out_shape=(shape(count, 2 * hid), *(shape(*w.shape)...  2.63 us
    pallas_call x1, Pallas kernels, prepare(): pl.pallas_call(body, out_shape=(shape(tok_count, width + LANES), *[shape(...  1.03 us
  transfers between devices with their start and end apart: 20, of which 14 were waited for; matrix products, arithmetic and copies ran while one was open for 1% of the time, Pallas kernels for 11%

profile of v7, /device:TPU:0, one launch (start us, length us, event | category | flops | bytes accessed | tf_op | source)
XLA Modules:
  0.0 47.1 jit_solution(9726965789766936422)
XLA Ops:
  0.0 1.0 %shard_map.64 = (bf16[96,1920]{1,0:T(8,128)(2,1)S(1)}, bf16[24,1920]{1,0:T(8,128)(2,1)S(1)}, bf16[24,1920]{1,0:T(8,128)(2,1)S(1)}) custom-call(bf16[96,1792]{1,0:T(8,128)(2,1)} %tokens_hbm.1, s32[8,96]{1,0:T(8,128)} %bitcast.8, f32[8,96]{1,0:T(8,128)} %bitcast.9), custom_call_target="tpu_custom_call" | custom-call | flops 1000000 | bytes 1048576 | tf_op jit(solution)/shard_map/pallas_call | solution.py:73
  1.0 5.1 %collective-permute-start = (bf16[24,1920]{1,0:T(8,128)(2,1)S(1)}, bf16[24,1920]{1,0:T(8,128)(2,1)S(1)}, u32[]{:S(2)}, u32[]{:S(2)}) collective-permute-start(bf16[24,1920]{1,0:T(8,128)(2,1)S(1)} %get-tuple-element.33), channel_id=1, source_target_pairs={{0,24},{8,16},{16,8},{24,0},{1,25},{9,17},{17,9},{25,1},{2,26},{10... | collective-permute-start | bytes 276488 | tf_op jit(solution)/shard_map/ppermute | solution.py:13
  6.2 0.6 %collective-permute-start.3 = (bf16[96,1920]{1,0:T(8,128)(2,1)S(1)}, bf16[96,1920]{1,0:T(8,128)(2,1)S(1)}, u32[]{:S(2)}, u32[]{:S(2)}) collective-permute-start(bf16[96,1920]{1,0:T(8,128)(2,1)S(1)} %get-tuple-element.34.x_ref), channel_id=1, source_target_pairs={{0,8},{8,0},{16,24},{24,16},{1,9},{9,1},{17,25},{25,17},{2,10},{10... | collective-permute-start | bytes 1105928 | tf_op jit(solution)/shard_map/ppermute | solution.py:13
  6.8 2.6 %shard_map.65 = (bf16[96,1024]{1,0:T(8,128)(2,1)S(1)}, bf16[1792,512]{1,0:T(8,128)(2,1)S(1)}, bf16[1792,512]{1,0:T(8,128)(2,1)S(1)}, bf16[512,1792]{1,0:T(8,128)(2,1)S(1)}) custom-call(bf16[96,1920]{1,0:T(8,128)(2,1)S(1)} %get-tuple-element.34.x_ref, bf16[1792,512]{1,0:T(8,128)(2,1)} %bitcast.5, bf16[1792,512]{1,0:T(8,128)(2,1)} %bitcast.6, ...), custom_call_target="tpu_custom_call" | custom-call | tf_op jit(solution)/shard_map/pallas_call | solution.py:119
  9.6 4.4 %collective-permute-done.1 = bf16[24,1920]{1,0:T(8,128)(2,1)S(1)} collective-permute-done((bf16[24,1920]{1,0:T(8,128)(2,1)S(1)}, bf16[24,1920]{1,0:T(8,128)(2,1)S(1)}, u32[]{:S(2)}, u32[]{:S(2)}) %collective-permute-start.1) | collective-permute-done | bytes 92192 | tf_op jit(solution)/shard_map/ppermute | solution.py:13
  14.0 1.6 %collective-permute-start.2 = (bf16[48,1920]{1,0:T(8,128)(2,1)S(1)}, bf16[48,1920]{1,0:T(8,128)(2,1)S(1)}, u32[]{:S(2)}, u32[]{:S(2)}) collective-permute-start(bf16[48,1920]{1,0:T(8,128)(2,1)S(1)} %get-tuple-element.67), channel_id=1, source_target_pairs={{0,2},{2,0},{4,6},{6,4},{1,3},{3,1},{5,7},{7,5},{8,10},{10,8},{12,... | collective-permute-start | bytes 552968 | tf_op jit(solution)/shard_map/ppermute | solution.py:13
  15.6 1.5 %collective-permute-start.5 = (bf16[48,1920]{1,0:T(8,128)(2,1)S(1)}, bf16[48,1920]{1,0:T(8,128)(2,1)S(1)}, u32[]{:S(2)}, u32[]{:S(2)}) collective-permute-start(bf16[48,1920]{1,0:T(8,128)(2,1)S(1)} %get-tuple-element.67), channel_id=1, source_target_pairs={{0,4},{2,6},{4,0},{6,2},{1,5},{3,7},{5,1},{7,3},{8,12},{10,14},{12... | collective-permute-start | bytes 552968 | tf_op jit(solution)/shard_map/ppermute | solution.py:13
  17.6 0.6 %collective-permute-start.8 = (bf16[24,1920]{1,0:T(8,128)(2,1)S(1)}, bf16[24,1920]{1,0:T(8,128)(2,1)S(1)}, u32[]{:S(2)}, u32[]{:S(2)}) collective-permute-start(bf16[24,1920]{1,0:T(8,128)(2,1)S(1)} %get-tuple-element.44), channel_id=1, source_target_pairs={{0,16},{8,24},{16,0},{24,8},{1,17},{9,25},{17,1},{25,9},{2,18},{10... | collective-permute-start | bytes 276488 | tf_op jit(solution)/shard_map/ppermute | solution.py:13
  19.0 0.7 %shard_map.67.part_ref = bf16[96,1024]{1,0:T(8,128)(2,1)S(1)} custom-call(bf16[96,1920]{1,0:T(8,128)(2,1)S(1)} %collective-permute-done.3.x_ref, bf16[1792,512]{1,0:T(8,128)(2,1)S(1)} %get-tuple-element.39.gate_ref, bf16[1792,512]{1,0:T(8,128)(2,1)S(1)} %get-tuple-element.40.up_ref), custom_call_target="tpu_custom_call" | custom-call | flops 352321536 | bytes 1048576 | tf_op jit(solution)/shard_map/pallas_call | solution.py:22
  19.8 0.9 %collective-permute-done.2 = bf16[48,1920]{1,0:T(8,128)(2,1)S(1)} collective-permute-done((bf16[48,1920]{1,0:T(8,128)(2,1)S(1)}, bf16[48,1920]{1,0:T(8,128)(2,1)S(1)}, u32[]{:S(2)}, u32[]{:S(2)}) %collective-permute-start.2) | collective-permute-done | bytes 184352 | tf_op jit(solution)/shard_map/ppermute | solution.py:13
  20.7 0.5 %collective-permute-done.6.other_ref = bf16[96,1024]{1,0:T(8,128)(2,1)S(1)} collective-permute-done((bf16[96,1024]{1,0:T(8,128)(2,1)S(1)}, bf16[96,1024]{1,0:T(8,128)(2,1)S(1)}, u32[]{:S(2)}, u32[]{:S(2)}) %collective-permute-start.6) | collective-permute-done | bytes 196640 | tf_op jit(solution)/shard_map/ppermute | solution.py:13
  21.7 1.3 %collective-permute-done.5 = bf16[48,1920]{1,0:T(8,128)(2,1)S(1)} collective-permute-done((bf16[48,1920]{1,0:T(8,128)(2,1)S(1)}, bf16[48,1920]{1,0:T(8,128)(2,1)S(1)}, u32[]{:S(2)}, u32[]{:S(2)}) %collective-permute-start.5) | collective-permute-done | bytes 184352 | tf_op jit(solution)/shard_map/ppermute | solution.py:13
  23.1 0.6 %collective-permute-done.8 = bf16[24,1920]{1,0:T(8,128)(2,1)S(1)} collective-permute-done((bf16[24,1920]{1,0:T(8,128)(2,1)S(1)}, bf16[24,1920]{1,0:T(8,128)(2,1)S(1)}, u32[]{:S(2)}, u32[]{:S(2)}) %collective-permute-start.8) | collective-permute-done | bytes 92192 | tf_op jit(solution)/shard_map/ppermute | solution.py:13
  23.6 0.9 %shard_map.69.part_ref = bf16[192,1024]{1,0:T(8,128)(2,1)S(1)} custom-call(bf16[192,1920]{1,0:T(8,128)(2,1)S(1)} %constant_dynamic-update-slice_fusion.2.x_ref, bf16[1792,512]{1,0:T(8,128)(2,1)S(1)} %get-tuple-element.39.gate_ref, bf16[1792,512]{1,0:T(8,128)(2,1)S(1)} %get-tuple-element.40.up_ref), custom_call_target="tpu_custom_call" | custom-call | flops 704643072 | bytes 1048576 | tf_op jit(solution)/shard_map/pallas_call | solution.py:22
  24.6 0.8 %collective-permute-start.14 = (bf16[96,1792]{1,0:T(8,128)(2,1)S(1)}, bf16[96,1792]{1,0:T(8,128)(2,1)S(1)}, u32[]{:S(2)}, u32[]{:S(2)}) collective-permute-start(bf16[96,1792]{1,0:T(8,128)(2,1)S(1)} %shard_map.68), channel_id=1, source_target_pairs={{0,8},{8,0},{16,24},{24,16},{1,9},{9,1},{17,25},{25,17},{2,10},{10... | collective-permute-start | bytes 1032200 | tf_op jit(solution)/shard_map/ppermute | solution.py:13
  25.4 0.9 %collective-permute-done.9.other_ref = bf16[192,1024]{1,0:T(8,128)(2,1)S(1)} collective-permute-done((bf16[192,1024]{1,0:T(8,128)(2,1)S(1)}, bf16[192,1024]{1,0:T(8,128)(2,1)S(1)}, u32[]{:S(2)}, u32[]{:S(2)}) %collective-permute-start.9) | collective-permute-done | bytes 393248 | tf_op jit(solution)/shard_map/ppermute | solution.py:13
  26.3 0.6 %shard_map.70 = bf16[192,1792]{1,0:T(8,128)(2,1)S(1)} custom-call(bf16[192,1920]{1,0:T(8,128)(2,1)S(1)} %constant_dynamic-update-slice_fusion.2.x_ref, bf16[192,1024]{1,0:T(8,128)(2,1)S(1)} %shard_map.69.part_ref, bf16[192,1024]{1,0:T(8,128)(2,1)S(1)} %collective-permute-done.9.other_ref, bf16[512,1792]{1,0:T(8,128)(2,1)S(1)} %get-tuple-element.37.down_ref), custom_call_target="tpu_custom_call" | custom-call | flops 352321536 | bytes 1048576 | tf_op jit(solution)/shard_map/pallas_call | solution.py:22
  27.0 2.5 %collective-permute-start.10 = (bf16[24,1792]{1,0:T(8,128)(2,1)S(1)}, bf16[24,1792]{1,0:T(8,128)(2,1)S(1)}, u32[]{:S(2)}, u32[]{:S(2)}) collective-permute-start(bf16[24,1792]{1,0:T(8,128)(2,1)S(1)} %get-tuple-element.62), channel_id=1, source_target_pairs={{0,6},{2,4},{4,2},{6,0},{1,7},{3,5},{5,3},{7,1},{8,14},{10,12},{12... | collective-permute-start | bytes 258056 | tf_op jit(solution)/shard_map/ppermute | solution.py:13
  29.5 0.9 %collective-permute-start.15 = (bf16[24,1792]{1,0:T(8,128)(2,1)S(1)}, bf16[24,1792]{1,0:T(8,128)(2,1)S(1)}, u32[]{:S(2)}, u32[]{:S(2)}) collective-permute-start(bf16[24,1792]{1,0:T(8,128)(2,1)S(1)} %get-tuple-element.50), channel_id=1, source_target_pairs={{0,16},{8,24},{16,0},{24,8},{1,17},{9,25},{17,1},{25,9},{2,18},{10... | collective-permute-start | bytes 258056 | tf_op jit(solution)/shard_map/ppermute | solution.py:13
  30.4 0.5 %collective-permute-start.11 = (bf16[48,1792]{1,0:T(8,128)(2,1)S(1)}, bf16[48,1792]{1,0:T(8,128)(2,1)S(1)}, u32[]{:S(2)}, u32[]{:S(2)}) collective-permute-start(bf16[48,1792]{1,0:T(8,128)(2,1)S(1)} %get-tuple-element.64), channel_id=1, source_target_pairs={{0,2},{2,0},{4,6},{6,4},{1,3},{3,1},{5,7},{7,5},{8,10},{10,8},{12,... | collective-permute-start | bytes 516104 | tf_op jit(solution)/shard_map/ppermute | solution.py:13
  31.0 0.5 %collective-permute-start.12 = (bf16[48,1792]{1,0:T(8,128)(2,1)S(1)}, bf16[48,1792]{1,0:T(8,128)(2,1)S(1)}, u32[]{:S(2)}, u32[]{:S(2)}) collective-permute-start(bf16[48,1792]{1,0:T(8,128)(2,1)S(1)} %get-tuple-element.63), channel_id=1, source_target_pairs={{0,4},{2,6},{4,0},{6,2},{1,5},{3,7},{5,1},{7,3},{8,12},{10,14},{12... | collective-permute-start | bytes 516104 | tf_op jit(solution)/shard_map/ppermute | solution.py:13
  31.5 1.0 %collective-permute-done.10 = bf16[24,1792]{1,0:T(8,128)(2,1)S(1)} collective-permute-done((bf16[24,1792]{1,0:T(8,128)(2,1)S(1)}, bf16[24,1792]{1,0:T(8,128)(2,1)S(1)}, u32[]{:S(2)}, u32[]{:S(2)}) %collective-permute-start.10) | collective-permute-done | bytes 86048 | tf_op jit(solution)/shard_map/ppermute | solution.py:13
  32.6 3.8 %collective-permute-done.11 = bf16[48,1792]{1,0:T(8,128)(2,1)S(1)} collective-permute-done((bf16[48,1792]{1,0:T(8,128)(2,1)S(1)}, bf16[48,1792]{1,0:T(8,128)(2,1)S(1)}, u32[]{:S(2)}, u32[]{:S(2)}) %collective-permute-start.11) | collective-permute-done | bytes 172064 | tf_op jit(solution)/shard_map/ppermute | solution.py:13
  36.6 2.2 %collective-permute-start.13 = (bf16[24,1792]{1,0:T(8,128)(2,1)S(1)}, bf16[24,1792]{1,0:T(8,128)(2,1)S(1)}, u32[]{:S(2)}, u32[]{:S(2)}) collective-permute-start(bf16[24,1792]{1,0:T(8,128)(2,1)S(1)} %get-tuple-element.66), channel_id=1, source_target_pairs={{0,24},{8,16},{16,8},{24,0},{1,25},{9,17},{17,9},{25,1},{2,26},{10... | collective-permute-start | bytes 258056 | tf_op jit(solution)/shard_map/ppermute | solution.py:13
  38.8 1.0 %collective-permute-start.19 = (bf16[24,1792]{1,0:T(8,128)(2,1)S(1)}, bf16[24,1792]{1,0:T(8,128)(2,1)S(1)}, u32[]{:S(2)}, u32[]{:S(2)}) collective-permute-start(bf16[24,1792]{1,0:T(8,128)(2,1)S(1)} %get-tuple-element.65), channel_id=1, source_target_pairs={{0,16},{8,24},{16,0},{24,8},{1,17},{9,25},{17,1},{25,9},{2,18},{10... | collective-permute-start | bytes 258056 | tf_op jit(solution)/shard_map/ppermute | solution.py:13
  39.9 1.5 %collective-permute-start.16 = (bf16[24,1792]{1,0:T(8,128)(2,1)S(1)}, bf16[24,1792]{1,0:T(8,128)(2,1)S(1)}, u32[]{:S(2)}, u32[]{:S(2)}) collective-permute-start(bf16[24,1792]{1,0:T(8,128)(2,1)S(1)} %get-tuple-element.52), channel_id=1, source_target_pairs={{0,6},{2,4},{4,2},{6,0},{1,7},{3,5},{5,3},{7,1},{8,14},{10,12},{12... | collective-permute-start | bytes 258056 | tf_op jit(solution)/shard_map/ppermute | solution.py:13
  41.4 0.5 %collective-permute-start.17 = (bf16[24,1792]{1,0:T(8,128)(2,1)S(1)}, bf16[24,1792]{1,0:T(8,128)(2,1)S(1)}, u32[]{:S(2)}, u32[]{:S(2)}) collective-permute-start(bf16[24,1792]{1,0:T(8,128)(2,1)S(1)} %get-tuple-element.53), channel_id=1, source_target_pairs={{0,2},{2,0},{4,6},{6,4},{1,3},{3,1},{5,7},{7,5},{8,10},{10,8},{12,... | collective-permute-start | bytes 258056 | tf_op jit(solution)/shard_map/ppermute | solution.py:13
  41.9 1.5 %collective-permute-start.18 = (bf16[24,1792]{1,0:T(8,128)(2,1)S(1)}, bf16[24,1792]{1,0:T(8,128)(2,1)S(1)}, u32[]{:S(2)}, u32[]{:S(2)}) collective-permute-start(bf16[24,1792]{1,0:T(8,128)(2,1)S(1)} %get-tuple-element.54), channel_id=1, source_target_pairs={{0,4},{2,6},{4,0},{6,2},{1,5},{3,7},{5,1},{7,3},{8,12},{10,14},{12... | collective-permute-start | bytes 258056 | tf_op jit(solution)/shard_map/ppermute | solution.py:13
  43.5 1.9 %collective-permute-done.16 = bf16[24,1792]{1,0:T(8,128)(2,1)S(1)} collective-permute-done((bf16[24,1792]{1,0:T(8,128)(2,1)S(1)}, bf16[24,1792]{1,0:T(8,128)(2,1)S(1)}, u32[]{:S(2)}, u32[]{:S(2)}) %collective-permute-start.16) | collective-permute-done | bytes 86048 | tf_op jit(solution)/shard_map/ppermute | solution.py:13
  45.4 0.5 %collective-permute-done.17 = bf16[24,1792]{1,0:T(8,128)(2,1)S(1)} collective-permute-done((bf16[24,1792]{1,0:T(8,128)(2,1)S(1)}, bf16[24,1792]{1,0:T(8,128)(2,1)S(1)}, u32[]{:S(2)}, u32[]{:S(2)}) %collective-permute-start.17) | collective-permute-done | bytes 86048 | tf_op jit(solution)/shard_map/ppermute | solution.py:13
  45.9 0.5 %collective-permute-done.18 = bf16[24,1792]{1,0:T(8,128)(2,1)S(1)} collective-permute-done((bf16[24,1792]{1,0:T(8,128)(2,1)S(1)}, bf16[24,1792]{1,0:T(8,128)(2,1)S(1)}, u32[]{:S(2)}, u32[]{:S(2)}) %collective-permute-start.18) | collective-permute-done | bytes 86048 | tf_op jit(solution)/shard_map/ppermute | solution.py:13
  46.5 0.7 %add_convert_fusion = bf16[24,1792]{1,0:T(8,128)(2,1)} fusion(f32[24,1792]{1,0:T(8,128)S(1)} %add_add_fusion, bf16[24,1792]{1,0:T(8,128)(2,1)S(1)} %collective-permute-done.19), kind=kLoop, calls=%fused_computation | loop fusion | flops 129024 | bytes 344064 | tf_op jit(solution)/shard_map/convert_element_type | solution.py:240
  (29 shorter events, 2.7 us)
Async XLA Ops:
  1.0 8.6 %collective-permute-start = (bf16[24,1920]{1,0:T(8,128)(2,1)S(1)}, bf16[24,1920]{1,0:T(8,128)(2,1)S(1)}, u32[]{:S(2)}, u32[]{:S(2)}) collective-permute-start(bf16[24,1920]{1,0:T(8,128)(2,1)S(1)} %get-tuple-element.33), channel_id=1, source_target_pairs={{0,24},{8,16},{16,8},{24,0},{1,25},{9,17},{17,9},{25,1},{2,26},{10... | collective-permute-start | bytes 276488 | tf_op jit(solution)/shard_map/ppermute | solution.py:13
  6.2 7.8 %collective-permute-start.1 = (bf16[24,1920]{1,0:T(8,128)(2,1)S(1)}, bf16[24,1920]{1,0:T(8,128)(2,1)S(1)}, u32[]{:S(2)}, u32[]{:S(2)}) collective-permute-start(bf16[24,1920]{1,0:T(8,128)(2,1)S(1)} %get-tuple-element.33), channel_id=1, source_target_pairs={{0,16},{8,24},{16,0},{24,8},{1,17},{9,25},{17,1},{25,9},{2,18},{10... | collective-permute-start | bytes 276488 | tf_op jit(solution)/shard_map/ppermute | solution.py:13
  6.2 12.8 %collective-permute-start.3 = (bf16[96,1920]{1,0:T(8,128)(2,1)S(1)}, bf16[96,1920]{1,0:T(8,128)(2,1)S(1)}, u32[]{:S(2)}, u32[]{:S(2)}) collective-permute-start(bf16[96,1920]{1,0:T(8,128)(2,1)S(1)} %get-tuple-element.34.x_ref), channel_id=1, source_target_pairs={{0,8},{8,0},{16,24},{24,16},{1,9},{9,1},{17,25},{25,17},{2,10},{10... | collective-permute-start | bytes 1105928 | tf_op jit(solution)/shard_map/ppermute | solution.py:13
  9.4 8.1 %collective-permute-start.4 = (bf16[96,1024]{1,0:T(8,128)(2,1)S(1)}, bf16[96,1024]{1,0:T(8,128)(2,1)S(1)}, u32[]{:S(2)}, u32[]{:S(2)}) collective-permute-start(bf16[96,1024]{1,0:T(8,128)(2,1)S(1)} %get-tuple-element.35.part_ref), channel_id=1, source_target_pairs={{0,1},{1,0},{2,3},{3,2},{4,5},{5,4},{6,7},{7,6},{8,9},{9,8},{10,11... | collective-permute-start | bytes 589832 | tf_op jit(solution)/shard_map/ppermute | solution.py:13
  14.0 6.6 %collective-permute-start.2 = (bf16[48,1920]{1,0:T(8,128)(2,1)S(1)}, bf16[48,1920]{1,0:T(8,128)(2,1)S(1)}, u32[]{:S(2)}, u32[]{:S(2)}) collective-permute-start(bf16[48,1920]{1,0:T(8,128)(2,1)S(1)} %get-tuple-element.67), channel_id=1, source_target_pairs={{0,2},{2,0},{4,6},{6,4},{1,3},{3,1},{5,7},{7,5},{8,10},{10,8},{12,... | collective-permute-start | bytes 552968 | tf_op jit(solution)/shard_map/ppermute | solution.py:13
  15.6 7.4 %collective-permute-start.5 = (bf16[48,1920]{1,0:T(8,128)(2,1)S(1)}, bf16[48,1920]{1,0:T(8,128)(2,1)S(1)}, u32[]{:S(2)}, u32[]{:S(2)}) collective-permute-start(bf16[48,1920]{1,0:T(8,128)(2,1)S(1)} %get-tuple-element.67), channel_id=1, source_target_pairs={{0,4},{2,6},{4,0},{6,2},{1,5},{3,7},{5,1},{7,3},{8,12},{10,14},{12... | collective-permute-start | bytes 552968 | tf_op jit(solution)/shard_map/ppermute | solution.py:13
  17.1 6.0 %collective-permute-start.7 = (bf16[24,1920]{1,0:T(8,128)(2,1)S(1)}, bf16[24,1920]{1,0:T(8,128)(2,1)S(1)}, u32[]{:S(2)}, u32[]{:S(2)}) collective-permute-start(bf16[24,1920]{1,0:T(8,128)(2,1)S(1)} %collective-permute-done), channel_id=1, source_target_pairs={{0,6},{2,4},{4,2},{6,0},{1,7},{3,5},{5,3},{7,1},{8,14},{10,12},{12... | collective-permute-start | bytes 276488 | tf_op jit(solution)/shard_map/ppermute | solution.py:13
  17.6 6.0 %collective-permute-start.8 = (bf16[24,1920]{1,0:T(8,128)(2,1)S(1)}, bf16[24,1920]{1,0:T(8,128)(2,1)S(1)}, u32[]{:S(2)}, u32[]{:S(2)}) collective-permute-start(bf16[24,1920]{1,0:T(8,128)(2,1)S(1)} %get-tuple-element.44), channel_id=1, source_target_pairs={{0,16},{8,24},{16,0},{24,8},{1,17},{9,25},{17,1},{25,9},{2,18},{10... | collective-permute-start | bytes 276488 | tf_op jit(solution)/shard_map/ppermute | solution.py:13
  19.7 1.5 %collective-permute-start.6 = (bf16[96,1024]{1,0:T(8,128)(2,1)S(1)}, bf16[96,1024]{1,0:T(8,128)(2,1)S(1)}, u32[]{:S(2)}, u32[]{:S(2)}) collective-permute-start(bf16[96,1024]{1,0:T(8,128)(2,1)S(1)} %shard_map.67.part_ref), channel_id=1, source_target_pairs={{0,1},{1,0},{2,3},{3,2},{4,5},{5,4},{6,7},{7,6},{8,9},{9,8},{10,11... | collective-permute-start | bytes 589832 | tf_op jit(solution)/shard_map/ppermute | solution.py:13
  24.5 1.8 %collective-permute-start.9 = (bf16[192,1024]{1,0:T(8,128)(2,1)S(1)}, bf16[192,1024]{1,0:T(8,128)(2,1)S(1)}, u32[]{:S(2)}, u32[]{:S(2)}) collective-permute-start(bf16[192,1024]{1,0:T(8,128)(2,1)S(1)} %shard_map.69.part_ref), channel_id=1, source_target_pairs={{0,1},{1,0},{2,3},{3,2},{4,5},{5,4},{6,7},{7,6},{8,9},{9,8},{10,11... | collective-permute-start | bytes 1179656 | tf_op jit(solution)/shard_map/ppermute | solution.py:13
  24.6 15.2 %collective-permute-start.14 = (bf16[96,1792]{1,0:T(8,128)(2,1)S(1)}, bf16[96,1792]{1,0:T(8,128)(2,1)S(1)}, u32[]{:S(2)}, u32[]{:S(2)}) collective-permute-start(bf16[96,1792]{1,0:T(8,128)(2,1)S(1)} %shard_map.68), channel_id=1, source_target_pairs={{0,8},{8,0},{16,24},{24,16},{1,9},{9,1},{17,25},{25,17},{2,10},{10... | collective-permute-start | bytes 1032200 | tf_op jit(solution)/shard_map/ppermute | solution.py:13
  27.0 5.5 %collective-permute-start.10 = (bf16[24,1792]{1,0:T(8,128)(2,1)S(1)}, bf16[24,1792]{1,0:T(8,128)(2,1)S(1)}, u32[]{:S(2)}, u32[]{:S(2)}) collective-permute-start(bf16[24,1792]{1,0:T(8,128)(2,1)S(1)} %get-tuple-element.62), channel_id=1, source_target_pairs={{0,6},{2,4},{4,2},{6,0},{1,7},{3,5},{5,3},{7,1},{8,14},{10,12},{12... | collective-permute-start | bytes 258056 | tf_op jit(solution)/shard_map/ppermute | solution.py:13
  29.5 10.3 %collective-permute-start.15 = (bf16[24,1792]{1,0:T(8,128)(2,1)S(1)}, bf16[24,1792]{1,0:T(8,128)(2,1)S(1)}, u32[]{:S(2)}, u32[]{:S(2)}) collective-permute-start(bf16[24,1792]{1,0:T(8,128)(2,1)S(1)} %get-tuple-element.50), channel_id=1, source_target_pairs={{0,16},{8,24},{16,0},{24,8},{1,17},{9,25},{17,1},{25,9},{2,18},{10... | collective-permute-start | bytes 258056 | tf_op jit(solution)/shard_map/ppermute | solution.py:13
  30.4 5.9 %collective-permute-start.11 = (bf16[48,1792]{1,0:T(8,128)(2,1)S(1)}, bf16[48,1792]{1,0:T(8,128)(2,1)S(1)}, u32[]{:S(2)}, u32[]{:S(2)}) collective-permute-start(bf16[48,1792]{1,0:T(8,128)(2,1)S(1)} %get-tuple-element.64), channel_id=1, source_target_pairs={{0,2},{2,0},{4,6},{6,4},{1,3},{3,1},{5,7},{7,5},{8,10},{10,8},{12,... | collective-permute-start | bytes 516104 | tf_op jit(solution)/shard_map/ppermute | solution.py:13
  31.0 5.6 %collective-permute-start.12 = (bf16[48,1792]{1,0:T(8,128)(2,1)S(1)}, bf16[48,1792]{1,0:T(8,128)(2,1)S(1)}, u32[]{:S(2)}, u32[]{:S(2)}) collective-permute-start(bf16[48,1792]{1,0:T(8,128)(2,1)S(1)} %get-tuple-element.63), channel_id=1, source_target_pairs={{0,4},{2,6},{4,0},{6,2},{1,5},{3,7},{5,1},{7,3},{8,12},{10,14},{12... | collective-permute-start | bytes 516104 | tf_op jit(solution)/shard_map/ppermute | solution.py:13
  36.6 6.8 %collective-permute-start.13 = (bf16[24,1792]{1,0:T(8,128)(2,1)S(1)}, bf16[24,1792]{1,0:T(8,128)(2,1)S(1)}, u32[]{:S(2)}, u32[]{:S(2)}) collective-permute-start(bf16[24,1792]{1,0:T(8,128)(2,1)S(1)} %get-tuple-element.66), channel_id=1, source_target_pairs={{0,24},{8,16},{16,8},{24,0},{1,25},{9,17},{17,9},{25,1},{2,26},{10... | collective-permute-start | bytes 258056 | tf_op jit(solution)/shard_map/ppermute | solution.py:13
  38.8 7.7 %collective-permute-start.19 = (bf16[24,1792]{1,0:T(8,128)(2,1)S(1)}, bf16[24,1792]{1,0:T(8,128)(2,1)S(1)}, u32[]{:S(2)}, u32[]{:S(2)}) collective-permute-start(bf16[24,1792]{1,0:T(8,128)(2,1)S(1)} %get-tuple-element.65), channel_id=1, source_target_pairs={{0,16},{8,24},{16,0},{24,8},{1,17},{9,25},{17,1},{25,9},{2,18},{10... | collective-permute-start | bytes 258056 | tf_op jit(solution)/shard_map/ppermute | solution.py:13
  39.9 5.4 %collective-permute-start.16 = (bf16[24,1792]{1,0:T(8,128)(2,1)S(1)}, bf16[24,1792]{1,0:T(8,128)(2,1)S(1)}, u32[]{:S(2)}, u32[]{:S(2)}) collective-permute-start(bf16[24,1792]{1,0:T(8,128)(2,1)S(1)} %get-tuple-element.52), channel_id=1, source_target_pairs={{0,6},{2,4},{4,2},{6,0},{1,7},{3,5},{5,3},{7,1},{8,14},{10,12},{12... | collective-permute-start | bytes 258056 | tf_op jit(solution)/shard_map/ppermute | solution.py:13
  41.4 4.5 %collective-permute-start.17 = (bf16[24,1792]{1,0:T(8,128)(2,1)S(1)}, bf16[24,1792]{1,0:T(8,128)(2,1)S(1)}, u32[]{:S(2)}, u32[]{:S(2)}) collective-permute-start(bf16[24,1792]{1,0:T(8,128)(2,1)S(1)} %get-tuple-element.53), channel_id=1, source_target_pairs={{0,2},{2,0},{4,6},{6,4},{1,3},{3,1},{5,7},{7,5},{8,10},{10,8},{12,... | collective-permute-start | bytes 258056 | tf_op jit(solution)/shard_map/ppermute | solution.py:13
  41.9 4.5 %collective-permute-start.18 = (bf16[24,1792]{1,0:T(8,128)(2,1)S(1)}, bf16[24,1792]{1,0:T(8,128)(2,1)S(1)}, u32[]{:S(2)}, u32[]{:S(2)}) collective-permute-start(bf16[24,1792]{1,0:T(8,128)(2,1)S(1)} %get-tuple-element.54), channel_id=1, source_target_pairs={{0,4},{2,6},{4,0},{6,2},{1,5},{3,7},{5,1},{7,3},{8,12},{10,14},{12... | collective-permute-start | bytes 258056 | tf_op jit(solution)/shard_map/ppermute | solution.py:13

commit v8 on v7

--- a/solution.py
+++ b/solution.py
@@ -37,10 +37,9 @@
     return jax.ShapeDtypeStruct(dims, jnp.bfloat16)
 
 
-def prepare(tokens, expert_ids, affinity, rows):
+def prepare(tokens, expert_ids, affinity, rows, expert_count):
     tok_count, width = tokens.shape
     choices = expert_ids.shape[1]
-
     parts = tok_count // rows
 
     def body(tokens_hbm, ids_hbm, affinity_hbm, all_ref, share_ref, opposite_ref, ids_ref, affinity_ref, sems):
@@ -60,19 +59,25 @@
         weight = jnp.zeros((LANES, tok_count), jnp.float32)
         for c in range(choices):
             weight += jnp.where(ids[c : c + 1, :] == lane, share[c : c + 1, :], 0.0)
-        all_ref[:, width:] = weight.T.astype(jnp.bfloat16)
+        weight = weight.T
+        all_ref[:, width:] = weight.astype(jnp.bfloat16)
         copies[0].wait()
         for i in range(parts):
-            other = i ^ (parts - 1)
+            opposite = i ^ (parts - 1)
 
             @pl.when(lax.axis_index("local") == i)
             def _():
-                share_ref[...] = all_ref[i * rows : (i + 1) * rows, :]
-                opposite_ref[...] = all_ref[other * rows : (other + 1) * rows, :]
+                lanes = jnp.zeros((rows, LANES), jnp.float32)
+                for j in range(parts):
+                    mine = weight[(i ^ j) * rows : ((i ^ j) + 1) * rows, :]
+                    lanes += mine if j == 0 else pltpu.roll(mine, j * expert_count, 1)
+                share_ref[:, :width] = all_ref[i * rows : (i + 1) * rows, :width]
+                share_ref[:, width:] = lanes.astype(jnp.bfloat16)
+                opposite_ref[...] = all_ref[opposite * rows : (opposite + 1) * rows, :width]
 
     return pl.pallas_call(
         body,
-        out_shape=(shape(tok_count, width + LANES), *[shape(rows, width + LANES)] * 2),
+        out_shape=(shape(tok_count, width + LANES), shape(rows, width + LANES), shape(rows, width)),
         in_specs=[pl.BlockSpec(memory_space=pltpu.HBM)] * 3,
         out_specs=[pl.BlockSpec(memory_space=pltpu.VMEM)] * 3,
         scratch_shapes=[
@@ -94,14 +99,16 @@
         out_ref[:, i * hid : (i + 1) * hid] = part.astype(jnp.bfloat16)
 
 
-def project(x, w_gate, w_up):
-    count = x.shape[0]
+def project(pieces, w_gate, w_up):
+    counts = [piece.shape[0] for piece in pieces]
     width, hid = w_gate.shape
 
-    def body(x_ref, gate_ref, up_ref, out_ref):
-        project_into(out_ref, x_ref[:, :width], (gate_ref, up_ref))
-
-    return in_vmem(body, shape(count, 2 * hid), 4 * count * width * hid, x, w_gate, w_up)
+    def body(*refs):
+        *piece_refs, gate_ref, up_ref, out_ref = refs
+        rows = jnp.concatenate([ref[:, :width] for ref in piece_refs], axis=0)
+        project_into(out_ref, rows, (gate_ref, up_ref))
+
+    return in_vmem(body, shape(sum(counts), 2 * hid), 4 * sum(counts) * width * hid, *pieces, w_gate, w_up)
 
 
 def load_and_project(x, *weights):
@@ -126,22 +133,33 @@
     )(x, *(in_hbm(w) for w in weights))
 
 
-def finish(x, part, other, w_down, group_size):
-    count = x.shape[0]
+def finish(tables, layout, group_size, part, other, w_down):
     hid, width = w_down.shape
-
-    def body(x_ref, part_ref, other_ref, down_ref, out_ref):
+    counts = [sum(tables[t].shape[0] for t, _ in runs) for runs in layout]
+
+    def body(*refs):
+        table_refs = refs[: len(tables)]
+        part_ref, other_ref, down_ref = refs[len(tables) : len(tables) + 3]
+        out_refs = refs[len(tables) + 3 :]
         both = part_ref[...].astype(jnp.float32) + other_ref[...].astype(jnp.float32)
         gate, up = both[:, :hid], both[:, hid:]
         hidden = (gate / (1.0 + jnp.exp(-gate)) * up).astype(jnp.bfloat16)
         expert = 2 * lax.axis_index("node") + lax.axis_index("local") // group_size
-        lane = lax.broadcasted_iota(jnp.int32, (count, LANES), 1)
-        table = x_ref[:, width:].astype(jnp.float32)
-        scale = jnp.sum(jnp.where(lane == expert, table, 0.0), axis=1, keepdims=True)
+        columns = []
+        for runs in layout:
+            for t, first in runs:
+                table = table_refs[t][:, width:].astype(jnp.float32)
+                lane = lax.broadcasted_iota(jnp.int32, table.shape, 1)
+                columns.append(jnp.sum(jnp.where(lane == expert + first, table, 0.0), axis=1, keepdims=True))
         out = jnp.dot(hidden, down_ref[...], preferred_element_type=jnp.float32)
-        out_ref[...] = (out * scale).astype(jnp.bfloat16)
-
-    return in_vmem(body, shape(count, width), 2 * count * width * hid, x, part, other, w_down)
+        out = (out * jnp.concatenate(columns, axis=0)).astype(jnp.bfloat16)
+        start = 0
+        for count, ref in zip(counts, out_refs):
+            ref[...] = out[start : start + count, :]
+            start += count
+
+    outs = [shape(count, width) for count in counts]
+    return in_vmem(body, outs, 2 * sum(counts) * width * hid, *tables, part, other, w_down)
 
 
 def merge(rows, partners, *values):
@@ -173,24 +191,27 @@
     group_size = local_count // 2
     tok_count, _ = expert_ids.shape
     rows = tok_count // local_count
+    width = tokens.shape[1]
     far = list(range(node_count - 1, 1, -1))
 
     def split(value):
         step = value.shape[0] // local_count
         return [value[j * step : (j + 1) * step] for j in range(local_count)]
 
-    everything, own, opposite = prepare(tokens, expert_ids, affinity, rows)
+    everything, own, opposite = prepare(tokens, expert_ids, affinity, rows, 2 * node_count)
     near = swap(everything, "node", 1)
     arrived = {k: swap(own, "node", k) for k in far}
     part_own, gate, up, down = load_and_project(everything, w_gate[0], w_up[0], w_down[0])
 
     def begin(x):
-        part = project(x, gate, up)
+        part = project([x], gate, up)
         return x, part, swap(part, "cuts", 1)
 
-    def complete(state, *others):
+    def complete(state, *others, tables=None, lanes=(0,)):
         x, part, other = state
-        return finish(x, part, after(other, *others), down, group_size)
+        tables = [x] if tables is None else tables
+        layout = [[(t, first) for first in lanes for t in range(len(tables))]]
+        return finish(tables, layout, group_size, part, after(other, *others), down)[0]
 
     sum_order = list(range(1, local_count))
     gather_order = sorted(sum_order, key=lambda j: (-j.bit_count(), j))
@@ -202,19 +223,20 @@
         return sum(value.astype(jnp.float32) for value in values)
 
     arrived[far[0]] = after(arrived[far[0]], part_own)
-    joined = jnp.concatenate([arrived[k] for k in far], axis=0)
-    fewer = jnp.concatenate([arrived[k] for k in far[:-1]], axis=0)
+    joined = jnp.concatenate([arrived[k][:, :width] for k in far], axis=0)
+    fewer = jnp.concatenate([arrived[k][:, :width] for k in far[:-1]], axis=0)
     others = exchanged([fewer if j == local_count - 1 else joined for j in gather_order], gather_order)
     out_own = complete((everything, part_own, swap(part_own, "cuts", 1)))
     direct = swap(after(opposite, *arrived.values()), "node", far[-1])
-    near_state = begin(after(near, out_own))
+    near_state = begin(near)
     out_near = complete(near_state)
     others[1] = after(others[1], near_state[1])
     others[2] = after(others[2], out_near)
     by_partner = [joined] + [others[gather_order.index(j)] for j in range(1, local_count)] + [direct]
-    state = begin(jnp.concatenate(by_partner, axis=0))
+    state = begin(after(jnp.concatenate(by_partner, axis=0), out_own))
     near_back = swap(out_near, "node", 1)
-    out_far = complete(state, out_near)
+    lanes = [2 * node_count * j for j in range(local_count)]
+    out_far = complete(state, out_near, tables=[arrived[k] for k in far], lanes=lanes)
     blocks = split(out_far)
     direct_back = swap(after(blocks[-1][-rows:], out_near), "node", far[-1])
     blocks[-1] = blocks[-1][:-rows]
@@ -233,11 +255,8 @@
     out_own = after(out_own, *done)
     mine, *blocks = merge(rows, gather_order, out_own, near_back, direct_back)
     later = exchanged(blocks, gather_order)
-    *back, last = back
-    total = summed([*back, mine])
-    total, *later = lax.optimization_barrier((total, *later))
-    total, last = lax.optimization_barrier((total + summed(later), last))
-    return (total + last.astype(jnp.float32)).astype(jnp.bfloat16)
+    total, *later = lax.optimization_barrier((summed(back), *later))
+    return (total + summed([mine, *later])).astype(jnp.bfloat16)
 
 
 def slots_on_device(tokens, expert_ids, affinity, w_gate, w_up, w_down):
@@ -301,7 +320,7 @@
     expert_count = 2 * node_count
     capacity = (5 * tok_count * top_count + 4 * expert_count - 1) // (4 * expert_count)
     powers = all(size & (size - 1) == 0 for size in (node_count, local_count))
-    everywhere = node_count == top_count // 2 and capacity >= tok_count and expert_count <= LANES
+    everywhere = node_count == top_count // 2 and capacity >= tok_count and local_count * expert_count <= LANES
     everywhere = everywhere and node_count > 2 and local_count > 2
     chosen = dense_on_device if everywhere and powers and tok_count % local_count == 0 else slots_on_device
     return chosen(tokens, expert_ids, affinity, w_gate, w_up, w_down)

time: 47.3 us -> 47.3 us (level)
  transfers between devices with their start and end apart: 20 -> 20, of which waited for: 14 -> 13; matrix products, arithmetic and copies ran while one was open for 1% -> 0% of each run, Pallas kernels for 11% -> 11%
where the time goes in v8:
time: 47.3 us; the launch traced here: 47.1 us
  starting transfers between devices  22.2 us (47%)
  waiting for transfers between devices  16.8 us (36%)
  Pallas kernels  7.03 us (15%)
  other arithmetic  0.82 us (2%)
    ppermute x20, starting transfers between devices, swap(): return lax.ppermute(value, axis, [(i, i ^ bits) for i in range(size)])  22.2 us
    ppermute x20, waiting for transfers between devices, swap(): return lax.ppermute(value, axis, [(i, i ^ bits) for i in range(size)])  16.8 us
    pallas_call x6, Pallas kernels, in_vmem(): pl.pallas_call(body, out_shape=out_shapes, in_specs=[pl.BlockSpec(memory_...  3.31 us
    pallas_call x1, Pallas kernels, load_and_project(): pl.pallas_call(body, out_shape=(shape(count, 2 * hid), *(shape(*w.shape)...  2.63 us
    pallas_call x1, Pallas kernels, prepare(): pl.pallas_call(body, out_shape=(shape(tok_count, width + LANES), shape(ro...  1.08 us
  transfers between devices with their start and end apart: 20, of which 13 were waited for; matrix products, arithmetic and copies ran while one was open for 0% of the time, Pallas kernels for 11%

profile of v8, /device:TPU:0, one launch (start us, length us, event | category | flops | bytes accessed | tf_op | source)
XLA Modules:
  0.0 47.1 jit_solution(12625877215893144975)
XLA Ops:
  0.0 1.1 %shard_map.64 = (bf16[96,1920]{1,0:T(8,128)(2,1)S(1)}, bf16[24,1920]{1,0:T(8,128)(2,1)S(1)}, bf16[24,1792]{1,0:T(8,128)(2,1)S(1)}) custom-call(bf16[96,1792]{1,0:T(8,128)(2,1)} %tokens_hbm.1, s32[8,96]{1,0:T(8,128)} %bitcast.8, f32[8,96]{1,0:T(8,128)} %bitcast.9), custom_call_target="tpu_custom_call" | custom-call | flops 1000000 | bytes 1048576 | tf_op jit(solution)/shard_map/pallas_call | solution.py:78
  1.1 5.1 %collective-permute-start = (bf16[24,1920]{1,0:T(8,128)(2,1)S(1)}, bf16[24,1920]{1,0:T(8,128)(2,1)S(1)}, u32[]{:S(2)}, u32[]{:S(2)}) collective-permute-start(bf16[24,1920]{1,0:T(8,128)(2,1)S(1)} %get-tuple-element.31), channel_id=1, source_target_pairs={{0,24},{8,16},{16,8},{24,0},{1,25},{9,17},{17,9},{25,1},{2,26},{10... | collective-permute-start | bytes 276488 | tf_op jit(solution)/shard_map/ppermute | solution.py:13
  6.2 0.6 %collective-permute-start.3 = (bf16[96,1920]{1,0:T(8,128)(2,1)S(1)}, bf16[96,1920]{1,0:T(8,128)(2,1)S(1)}, u32[]{:S(2)}, u32[]{:S(2)}) collective-permute-start(bf16[96,1920]{1,0:T(8,128)(2,1)S(1)} %get-tuple-element.32.x_ref.refs_0_), channel_id=1, source_target_pairs={{0,8},{8,0},{16,24},{24,16},{1,9},{9,1},{17,25},{25,17},{2,10},{10... | collective-permute-start | bytes 1105928 | tf_op jit(solution)/shard_map/ppermute | solution.py:13
  6.8 2.6 %shard_map.65 = (bf16[96,1024]{1,0:T(8,128)(2,1)S(1)}, bf16[1792,512]{1,0:T(8,128)(2,1)S(1)}, bf16[1792,512]{1,0:T(8,128)(2,1)S(1)}, bf16[512,1792]{1,0:T(8,128)(2,1)S(1)}) custom-call(bf16[96,1920]{1,0:T(8,128)(2,1)S(1)} %get-tuple-element.32.x_ref.refs_0_, bf16[1792,512]{1,0:T(8,128)(2,1)} %bitcast.5, bf16[1792,512]{1,0:T(8,128)(2,1)} %bitcast.6, ...), custom_call_target="tpu_custom_call" | custom-call | tf_op jit(solution)/shard_map/pallas_call | solution.py:126
  9.7 4.4 %collective-permute-done.1.refs_1_ = bf16[24,1920]{1,0:T(8,128)(2,1)S(1)} collective-permute-done((bf16[24,1920]{1,0:T(8,128)(2,1)S(1)}, bf16[24,1920]{1,0:T(8,128)(2,1)S(1)}, u32[]{:S(2)}, u32[]{:S(2)}) %collective-permute-start.1) | collective-permute-done | bytes 92192 | tf_op jit(solution)/shard_map/ppermute | solution.py:13
  14.1 1.6 %collective-permute-start.2 = (bf16[48,1792]{1,0:T(8,128)(2,1)S(1)}, bf16[48,1792]{1,0:T(8,128)(2,1)S(1)}, u32[]{:S(2)}, u32[]{:S(2)}) collective-permute-start(bf16[48,1792]{1,0:T(8,128)(2,1)S(1)} %pad_maximum_fusion), channel_id=1, source_target_pairs={{0,2},{2,0},{4,6},{6,4},{1,3},{3,1},{5,7},{7,5},{8,10},{10,8},{12,... | collective-permute-start | bytes 516104 | tf_op jit(solution)/shard_map/ppermute | solution.py:13
  15.6 1.5 %collective-permute-start.4 = (bf16[48,1792]{1,0:T(8,128)(2,1)S(1)}, bf16[48,1792]{1,0:T(8,128)(2,1)S(1)}, u32[]{:S(2)}, u32[]{:S(2)}) collective-permute-start(bf16[48,1792]{1,0:T(8,128)(2,1)S(1)} %pad_maximum_fusion), channel_id=1, source_target_pairs={{0,4},{2,6},{4,0},{6,2},{1,5},{3,7},{5,1},{7,3},{8,12},{10,14},{12... | collective-permute-start | bytes 516104 | tf_op jit(solution)/shard_map/ppermute | solution.py:13
  17.6 0.6 %collective-permute-start.7 = (bf16[24,1792]{1,0:T(8,128)(2,1)S(1)}, bf16[24,1792]{1,0:T(8,128)(2,1)S(1)}, u32[]{:S(2)}, u32[]{:S(2)}) collective-permute-start(bf16[24,1792]{1,0:T(8,128)(2,1)S(1)} %get-tuple-element.41), channel_id=1, source_target_pairs={{0,16},{8,24},{16,0},{24,8},{1,17},{9,25},{17,1},{25,9},{2,18},{10... | collective-permute-start | bytes 258056 | tf_op jit(solution)/shard_map/ppermute | solution.py:13
  18.3 0.5 %shard_map.68.own_ref = bf16[96,1792]{1,0:T(8,128)(2,1)S(1)} custom-call(bf16[96,1920]{1,0:T(8,128)(2,1)S(1)} %get-tuple-element.32.x_ref.refs_0_, bf16[96,1024]{1,0:T(8,128)(2,1)S(1)} %get-tuple-element.33.refs_1_, bf16[96,1024]{1,0:T(8,128)(2,1)S(1)} %collective-permute-done.8.refs_2_, bf16[512,1792]{1,0:T(8,128)(2,1)S(1)} %get-tuple-element.38.refs_3_.refs_4_), custom_call_target="tpu_custom_call" | custom-call | flops 176160768 | bytes 1048576 | tf_op jit(solution)/shard_map/pallas_call | solution.py:22
  19.0 0.7 %shard_map.66.refs_1_ = bf16[96,1024]{1,0:T(8,128)(2,1)S(1)} custom-call(bf16[96,1920]{1,0:T(8,128)(2,1)S(1)} %collective-permute-done.3.refs_0_, bf16[1792,512]{1,0:T(8,128)(2,1)S(1)} %get-tuple-element.35.refs_1_, bf16[1792,512]{1,0:T(8,128)(2,1)S(1)} %get-tuple-element.36.refs_2_), custom_call_target="tpu_custom_call" | custom-call | flops 352321536 | bytes 1048576 | tf_op jit(solution)/shard_map/pallas_call | solution.py:22
  19.8 0.7 %collective-permute-done.2 = bf16[48,1792]{1,0:T(8,128)(2,1)S(1)} collective-permute-done((bf16[48,1792]{1,0:T(8,128)(2,1)S(1)}, bf16[48,1792]{1,0:T(8,128)(2,1)S(1)}, u32[]{:S(2)}, u32[]{:S(2)}) %collective-permute-start.2) | collective-permute-done | bytes 172064 | tf_op jit(solution)/shard_map/ppermute | solution.py:13
  20.5 0.7 %collective-permute-done.5.refs_2_ = bf16[96,1024]{1,0:T(8,128)(2,1)S(1)} collective-permute-done((bf16[96,1024]{1,0:T(8,128)(2,1)S(1)}, bf16[96,1024]{1,0:T(8,128)(2,1)S(1)}, u32[]{:S(2)}, u32[]{:S(2)}) %collective-permute-start.5) | collective-permute-done | bytes 196640 | tf_op jit(solution)/shard_map/ppermute | solution.py:13
  21.2 0.5 %shard_map.67 = bf16[96,1792]{1,0:T(8,128)(2,1)S(1)} custom-call(bf16[96,1920]{1,0:T(8,128)(2,1)S(1)} %collective-permute-done.3.refs_0_, bf16[96,1024]{1,0:T(8,128)(2,1)S(1)} %shard_map.66.refs_1_, bf16[96,1024]{1,0:T(8,128)(2,1)S(1)} %collective-permute-done.5.refs_2_, bf16[512,1792]{1,0:T(8,128)(2,1)S(1)} %get-tuple-element.38.refs_3_.refs_4_), custom_call_target="tpu_custom_call" | custom-call | flops 176160768 | bytes 1048576 | tf_op jit(solution)/shard_map/pallas_call | solution.py:22
  21.7 1.2 %collective-permute-done.4 = bf16[48,1792]{1,0:T(8,128)(2,1)S(1)} collective-permute-done((bf16[48,1792]{1,0:T(8,128)(2,1)S(1)}, bf16[48,1792]{1,0:T(8,128)(2,1)S(1)}, u32[]{:S(2)}, u32[]{:S(2)}) %collective-permute-start.4) | collective-permute-done | bytes 172064 | tf_op jit(solution)/shard_map/ppermute | solution.py:13
  22.9 0.7 %collective-permute-done.7 = bf16[24,1792]{1,0:T(8,128)(2,1)S(1)} collective-permute-done((bf16[24,1792]{1,0:T(8,128)(2,1)S(1)}, bf16[24,1792]{1,0:T(8,128)(2,1)S(1)}, u32[]{:S(2)}, u32[]{:S(2)}) %collective-permute-start.7) | collective-permute-done | bytes 86048 | tf_op jit(solution)/shard_map/ppermute | solution.py:13
  23.6 0.9 %shard_map.69.refs_2_ = bf16[192,1024]{1,0:T(8,128)(2,1)S(1)} custom-call(bf16[192,1792]{1,0:T(8,128)(2,1)S(1)} %constant_dynamic-update-slice_fusion.refs_0_, bf16[1792,512]{1,0:T(8,128)(2,1)S(1)} %get-tuple-element.35.refs_1_, bf16[1792,512]{1,0:T(8,128)(2,1)S(1)} %get-tuple-element.36.refs_2_), custom_call_target="tpu_custom_call" | custom-call | flops 704643072 | bytes 1048576 | tf_op jit(solution)/shard_map/pallas_call | solution.py:22
  24.5 0.8 %collective-permute-start.15 = (bf16[96,1792]{1,0:T(8,128)(2,1)S(1)}, bf16[96,1792]{1,0:T(8,128)(2,1)S(1)}, u32[]{:S(2)}, u32[]{:S(2)}) collective-permute-start(bf16[96,1792]{1,0:T(8,128)(2,1)S(1)} %shard_map.67), channel_id=1, source_target_pairs={{0,8},{8,0},{16,24},{24,16},{1,9},{9,1},{17,25},{25,17},{2,10},{10... | collective-permute-start | bytes 1032200 | tf_op jit(solution)/shard_map/ppermute | solution.py:13
  25.3 0.9 %collective-permute-done.9.refs_3_ = bf16[192,1024]{1,0:T(8,128)(2,1)S(1)} collective-permute-done((bf16[192,1024]{1,0:T(8,128)(2,1)S(1)}, bf16[192,1024]{1,0:T(8,128)(2,1)S(1)}, u32[]{:S(2)}, u32[]{:S(2)}) %collective-permute-start.9) | collective-permute-done | bytes 393248 | tf_op jit(solution)/shard_map/ppermute | solution.py:13
  26.2 0.7 %shard_map.70 = bf16[192,1792]{1,0:T(8,128)(2,1)S(1)} custom-call(bf16[24,1920]{1,0:T(8,128)(2,1)S(1)} %collective-permute-done.refs_0_, bf16[24,1920]{1,0:T(8,128)(2,1)S(1)} %collective-permute-done.1.refs_1_, bf16[192,1024]{1,0:T(8,128)(2,1)S(1)} %shard_map.69.refs_2_, bf16[192,1024]{1,0:T(8,128)(2,1)S(1)} %collective-permute-done.9.refs_3_, ...), custom_call_target="tpu_custom_call" | custom-call | flops 352321536 | bytes 1048576 | tf_op jit(solution)/shard_map/pallas_call | solution.py:22
  26.9 2.5 %collective-permute-start.10 = (bf16[24,1792]{1,0:T(8,128)(2,1)S(1)}, bf16[24,1792]{1,0:T(8,128)(2,1)S(1)}, u32[]{:S(2)}, u32[]{:S(2)}) collective-permute-start(bf16[24,1792]{1,0:T(8,128)(2,1)S(1)} %get-tuple-element.58), channel_id=1, source_target_pairs={{0,6},{2,4},{4,2},{6,0},{1,7},{3,5},{5,3},{7,1},{8,14},{10,12},{12... | collective-permute-start | bytes 258056 | tf_op jit(solution)/shard_map/ppermute | solution.py:13
  29.5 1.0 %collective-permute-start.16 = (bf16[24,1792]{1,0:T(8,128)(2,1)S(1)}, bf16[24,1792]{1,0:T(8,128)(2,1)S(1)}, u32[]{:S(2)}, u32[]{:S(2)}) collective-permute-start(bf16[24,1792]{1,0:T(8,128)(2,1)S(1)} %get-tuple-element.48), channel_id=1, source_target_pairs={{0,16},{8,24},{16,0},{24,8},{1,17},{9,25},{17,1},{25,9},{2,18},{10... | collective-permute-start | bytes 258056 | tf_op jit(solution)/shard_map/ppermute | solution.py:13
  30.5 0.5 %collective-permute-start.11 = (bf16[48,1792]{1,0:T(8,128)(2,1)S(1)}, bf16[48,1792]{1,0:T(8,128)(2,1)S(1)}, u32[]{:S(2)}, u32[]{:S(2)}) collective-permute-start(bf16[48,1792]{1,0:T(8,128)(2,1)S(1)} %get-tuple-element.60), channel_id=1, source_target_pairs={{0,2},{2,0},{4,6},{6,4},{1,3},{3,1},{5,7},{7,5},{8,10},{10,8},{12,... | collective-permute-start | bytes 516104 | tf_op jit(solution)/shard_map/ppermute | solution.py:13
  31.0 0.5 %collective-permute-start.12 = (bf16[48,1792]{1,0:T(8,128)(2,1)S(1)}, bf16[48,1792]{1,0:T(8,128)(2,1)S(1)}, u32[]{:S(2)}, u32[]{:S(2)}) collective-permute-start(bf16[48,1792]{1,0:T(8,128)(2,1)S(1)} %get-tuple-element.59), channel_id=1, source_target_pairs={{0,4},{2,6},{4,0},{6,2},{1,5},{3,7},{5,1},{7,3},{8,12},{10,14},{12... | collective-permute-start | bytes 516104 | tf_op jit(solution)/shard_map/ppermute | solution.py:13
  31.5 1.0 %collective-permute-done.10 = bf16[24,1792]{1,0:T(8,128)(2,1)S(1)} collective-permute-done((bf16[24,1792]{1,0:T(8,128)(2,1)S(1)}, bf16[24,1792]{1,0:T(8,128)(2,1)S(1)}, u32[]{:S(2)}, u32[]{:S(2)}) %collective-permute-start.10) | collective-permute-done | bytes 86048 | tf_op jit(solution)/shard_map/ppermute | solution.py:13
  32.5 3.8 %collective-permute-done.11 = bf16[48,1792]{1,0:T(8,128)(2,1)S(1)} collective-permute-done((bf16[48,1792]{1,0:T(8,128)(2,1)S(1)}, bf16[48,1792]{1,0:T(8,128)(2,1)S(1)}, u32[]{:S(2)}, u32[]{:S(2)}) %collective-permute-start.11) | collective-permute-done | bytes 172064 | tf_op jit(solution)/shard_map/ppermute | solution.py:13
  36.7 2.2 %collective-permute-start.13 = (bf16[24,1792]{1,0:T(8,128)(2,1)S(1)}, bf16[24,1792]{1,0:T(8,128)(2,1)S(1)}, u32[]{:S(2)}, u32[]{:S(2)}) collective-permute-start(bf16[24,1792]{1,0:T(8,128)(2,1)S(1)} %get-tuple-element.61), channel_id=1, source_target_pairs={{0,24},{8,16},{16,8},{24,0},{1,25},{9,17},{17,9},{25,1},{2,26},{10... | collective-permute-start | bytes 258056 | tf_op jit(solution)/shard_map/ppermute | solution.py:13
  38.8 1.0 %collective-permute-start.14 = (bf16[24,1792]{1,0:T(8,128)(2,1)S(1)}, bf16[24,1792]{1,0:T(8,128)(2,1)S(1)}, u32[]{:S(2)}, u32[]{:S(2)}) collective-permute-start(bf16[24,1792]{1,0:T(8,128)(2,1)S(1)} %get-tuple-element.62), channel_id=1, source_target_pairs={{0,16},{8,24},{16,0},{24,8},{1,17},{9,25},{17,1},{25,9},{2,18},{10... | collective-permute-start | bytes 258056 | tf_op jit(solution)/shard_map/ppermute | solution.py:13
  39.9 1.5 %collective-permute-start.17 = (bf16[24,1792]{1,0:T(8,128)(2,1)S(1)}, bf16[24,1792]{1,0:T(8,128)(2,1)S(1)}, u32[]{:S(2)}, u32[]{:S(2)}) collective-permute-start(bf16[24,1792]{1,0:T(8,128)(2,1)S(1)} %get-tuple-element.49), channel_id=1, source_target_pairs={{0,6},{2,4},{4,2},{6,0},{1,7},{3,5},{5,3},{7,1},{8,14},{10,12},{12... | collective-permute-start | bytes 258056 | tf_op jit(solution)/shard_map/ppermute | solution.py:13
  41.4 0.5 %collective-permute-start.18 = (bf16[24,1792]{1,0:T(8,128)(2,1)S(1)}, bf16[24,1792]{1,0:T(8,128)(2,1)S(1)}, u32[]{:S(2)}, u32[]{:S(2)}) collective-permute-start(bf16[24,1792]{1,0:T(8,128)(2,1)S(1)} %get-tuple-element.50), channel_id=1, source_target_pairs={{0,2},{2,0},{4,6},{6,4},{1,3},{3,1},{5,7},{7,5},{8,10},{10,8},{12,... | collective-permute-start | bytes 258056 | tf_op jit(solution)/shard_map/ppermute | solution.py:13
  41.9 1.5 %collective-permute-start.19 = (bf16[24,1792]{1,0:T(8,128)(2,1)S(1)}, bf16[24,1792]{1,0:T(8,128)(2,1)S(1)}, u32[]{:S(2)}, u32[]{:S(2)}) collective-permute-start(bf16[24,1792]{1,0:T(8,128)(2,1)S(1)} %get-tuple-element.51), channel_id=1, source_target_pairs={{0,4},{2,6},{4,0},{6,2},{1,5},{3,7},{5,1},{7,3},{8,12},{10,14},{12... | collective-permute-start | bytes 258056 | tf_op jit(solution)/shard_map/ppermute | solution.py:13
  43.5 2.7 %collective-permute-done.14 = bf16[24,1792]{1,0:T(8,128)(2,1)S(1)} collective-permute-done((bf16[24,1792]{1,0:T(8,128)(2,1)S(1)}, bf16[24,1792]{1,0:T(8,128)(2,1)S(1)}, u32[]{:S(2)}, u32[]{:S(2)}) %collective-permute-start.14) | collective-permute-done | bytes 86048 | tf_op jit(solution)/shard_map/ppermute | solution.py:13
  46.4 0.7 %add_convert_fusion = bf16[24,1792]{1,0:T(8,128)(2,1)} fusion(f32[24,1792]{1,0:T(8,128)S(1)} %convert_add_fusion, bf16[24,1792]{1,0:T(8,128)(2,1)S(1)} %collective-permute-done.19, bf16[24,1792]{1,0:T(8,128)(2,1)S(1)} %collective-permute-done.18, bf16[24,1792]{1,0:T(8,128)(2,1)S(1)} %collective-permute-done.17, bf16[24,1792]{1,0:T(8,128)(2,1)S(1)} %get-tuple-element.53), kind=kLoop, calls=%fused_computation.1 | loop fusion | flops 387072 | bytes 602112 | tf_op jit(solution)/shard_map/convert_element_type | solution.py:259
  (29 shorter events, 1.8 us)
Async XLA Ops:
  1.1 8.6 %collective-permute-start = (bf16[24,1920]{1,0:T(8,128)(2,1)S(1)}, bf16[24,1920]{1,0:T(8,128)(2,1)S(1)}, u32[]{:S(2)}, u32[]{:S(2)}) collective-permute-start(bf16[24,1920]{1,0:T(8,128)(2,1)S(1)} %get-tuple-element.31), channel_id=1, source_target_pairs={{0,24},{8,16},{16,8},{24,0},{1,25},{9,17},{17,9},{25,1},{2,26},{10... | collective-permute-start | bytes 276488 | tf_op jit(solution)/shard_map/ppermute | solution.py:13
  6.2 7.8 %collective-permute-start.1 = (bf16[24,1920]{1,0:T(8,128)(2,1)S(1)}, bf16[24,1920]{1,0:T(8,128)(2,1)S(1)}, u32[]{:S(2)}, u32[]{:S(2)}) collective-permute-start(bf16[24,1920]{1,0:T(8,128)(2,1)S(1)} %get-tuple-element.31), channel_id=1, source_target_pairs={{0,16},{8,24},{16,0},{24,8},{1,17},{9,25},{17,1},{25,9},{2,18},{10... | collective-permute-start | bytes 276488 | tf_op jit(solution)/shard_map/ppermute | solution.py:13
  6.2 12.8 %collective-permute-start.3 = (bf16[96,1920]{1,0:T(8,128)(2,1)S(1)}, bf16[96,1920]{1,0:T(8,128)(2,1)S(1)}, u32[]{:S(2)}, u32[]{:S(2)}) collective-permute-start(bf16[96,1920]{1,0:T(8,128)(2,1)S(1)} %get-tuple-element.32.x_ref.refs_0_), channel_id=1, source_target_pairs={{0,8},{8,0},{16,24},{24,16},{1,9},{9,1},{17,25},{25,17},{2,10},{10... | collective-permute-start | bytes 1105928 | tf_op jit(solution)/shard_map/ppermute | solution.py:13
  9.5 8.2 %collective-permute-start.8 = (bf16[96,1024]{1,0:T(8,128)(2,1)S(1)}, bf16[96,1024]{1,0:T(8,128)(2,1)S(1)}, u32[]{:S(2)}, u32[]{:S(2)}) collective-permute-start(bf16[96,1024]{1,0:T(8,128)(2,1)S(1)} %get-tuple-element.33.refs_1_), channel_id=1, source_target_pairs={{0,1},{1,0},{2,3},{3,2},{4,5},{5,4},{6,7},{7,6},{8,9},{9,8},{10,11... | collective-permute-start | bytes 589832 | tf_op jit(solution)/shard_map/ppermute | solution.py:13
  14.1 6.4 %collective-permute-start.2 = (bf16[48,1792]{1,0:T(8,128)(2,1)S(1)}, bf16[48,1792]{1,0:T(8,128)(2,1)S(1)}, u32[]{:S(2)}, u32[]{:S(2)}) collective-permute-start(bf16[48,1792]{1,0:T(8,128)(2,1)S(1)} %pad_maximum_fusion), channel_id=1, source_target_pairs={{0,2},{2,0},{4,6},{6,4},{1,3},{3,1},{5,7},{7,5},{8,10},{10,8},{12,... | collective-permute-start | bytes 516104 | tf_op jit(solution)/shard_map/ppermute | solution.py:13
  15.6 7.2 %collective-permute-start.4 = (bf16[48,1792]{1,0:T(8,128)(2,1)S(1)}, bf16[48,1792]{1,0:T(8,128)(2,1)S(1)}, u32[]{:S(2)}, u32[]{:S(2)}) collective-permute-start(bf16[48,1792]{1,0:T(8,128)(2,1)S(1)} %pad_maximum_fusion), channel_id=1, source_target_pairs={{0,4},{2,6},{4,0},{6,2},{1,5},{3,7},{5,1},{7,3},{8,12},{10,14},{12... | collective-permute-start | bytes 516104 | tf_op jit(solution)/shard_map/ppermute | solution.py:13
  17.2 5.7 %collective-permute-start.6 = (bf16[24,1792]{1,0:T(8,128)(2,1)S(1)}, bf16[24,1792]{1,0:T(8,128)(2,1)S(1)}, u32[]{:S(2)}, u32[]{:S(2)}) collective-permute-start(bf16[24,1792]{1,0:T(8,128)(2,1)S(1)} %get-tuple-element.63), channel_id=1, source_target_pairs={{0,6},{2,4},{4,2},{6,0},{1,7},{3,5},{5,3},{7,1},{8,14},{10,12},{12... | collective-permute-start | bytes 258056 | tf_op jit(solution)/shard_map/ppermute | solution.py:13
  17.6 5.9 %collective-permute-start.7 = (bf16[24,1792]{1,0:T(8,128)(2,1)S(1)}, bf16[24,1792]{1,0:T(8,128)(2,1)S(1)}, u32[]{:S(2)}, u32[]{:S(2)}) collective-permute-start(bf16[24,1792]{1,0:T(8,128)(2,1)S(1)} %get-tuple-element.41), channel_id=1, source_target_pairs={{0,16},{8,24},{16,0},{24,8},{1,17},{9,25},{17,1},{25,9},{2,18},{10... | collective-permute-start | bytes 258056 | tf_op jit(solution)/shard_map/ppermute | solution.py:13
  19.7 1.5 %collective-permute-start.5 = (bf16[96,1024]{1,0:T(8,128)(2,1)S(1)}, bf16[96,1024]{1,0:T(8,128)(2,1)S(1)}, u32[]{:S(2)}, u32[]{:S(2)}) collective-permute-start(bf16[96,1024]{1,0:T(8,128)(2,1)S(1)} %shard_map.66.refs_1_), channel_id=1, source_target_pairs={{0,1},{1,0},{2,3},{3,2},{4,5},{5,4},{6,7},{7,6},{8,9},{9,8},{10,11... | collective-permute-start | bytes 589832 | tf_op jit(solution)/shard_map/ppermute | solution.py:13
  24.5 1.8 %collective-permute-start.9 = (bf16[192,1024]{1,0:T(8,128)(2,1)S(1)}, bf16[192,1024]{1,0:T(8,128)(2,1)S(1)}, u32[]{:S(2)}, u32[]{:S(2)}) collective-permute-start(bf16[192,1024]{1,0:T(8,128)(2,1)S(1)} %shard_map.69.refs_2_), channel_id=1, source_target_pairs={{0,1},{1,0},{2,3},{3,2},{4,5},{5,4},{6,7},{7,6},{8,9},{9,8},{10,11... | collective-permute-start | bytes 1179656 | tf_op jit(solution)/shard_map/ppermute | solution.py:13
  24.5 15.3 %collective-permute-start.15 = (bf16[96,1792]{1,0:T(8,128)(2,1)S(1)}, bf16[96,1792]{1,0:T(8,128)(2,1)S(1)}, u32[]{:S(2)}, u32[]{:S(2)}) collective-permute-start(bf16[96,1792]{1,0:T(8,128)(2,1)S(1)} %shard_map.67), channel_id=1, source_target_pairs={{0,8},{8,0},{16,24},{24,16},{1,9},{9,1},{17,25},{25,17},{2,10},{10... | collective-permute-start | bytes 1032200 | tf_op jit(solution)/shard_map/ppermute | solution.py:13
  26.9 5.5 %collective-permute-start.10 = (bf16[24,1792]{1,0:T(8,128)(2,1)S(1)}, bf16[24,1792]{1,0:T(8,128)(2,1)S(1)}, u32[]{:S(2)}, u32[]{:S(2)}) collective-permute-start(bf16[24,1792]{1,0:T(8,128)(2,1)S(1)} %get-tuple-element.58), channel_id=1, source_target_pairs={{0,6},{2,4},{4,2},{6,0},{1,7},{3,5},{5,3},{7,1},{8,14},{10,12},{12... | collective-permute-start | bytes 258056 | tf_op jit(solution)/shard_map/ppermute | solution.py:13
  29.5 10.3 %collective-permute-start.16 = (bf16[24,1792]{1,0:T(8,128)(2,1)S(1)}, bf16[24,1792]{1,0:T(8,128)(2,1)S(1)}, u32[]{:S(2)}, u32[]{:S(2)}) collective-permute-start(bf16[24,1792]{1,0:T(8,128)(2,1)S(1)} %get-tuple-element.48), channel_id=1, source_target_pairs={{0,16},{8,24},{16,0},{24,8},{1,17},{9,25},{17,1},{25,9},{2,18},{10... | collective-permute-start | bytes 258056 | tf_op jit(solution)/shard_map/ppermute | solution.py:13
  30.5 5.9 %collective-permute-start.11 = (bf16[48,1792]{1,0:T(8,128)(2,1)S(1)}, bf16[48,1792]{1,0:T(8,128)(2,1)S(1)}, u32[]{:S(2)}, u32[]{:S(2)}) collective-permute-start(bf16[48,1792]{1,0:T(8,128)(2,1)S(1)} %get-tuple-element.60), channel_id=1, source_target_pairs={{0,2},{2,0},{4,6},{6,4},{1,3},{3,1},{5,7},{7,5},{8,10},{10,8},{12,... | collective-permute-start | bytes 516104 | tf_op jit(solution)/shard_map/ppermute | solution.py:13
  31.0 5.6 %collective-permute-start.12 = (bf16[48,1792]{1,0:T(8,128)(2,1)S(1)}, bf16[48,1792]{1,0:T(8,128)(2,1)S(1)}, u32[]{:S(2)}, u32[]{:S(2)}) collective-permute-start(bf16[48,1792]{1,0:T(8,128)(2,1)S(1)} %get-tuple-element.59), channel_id=1, source_target_pairs={{0,4},{2,6},{4,0},{6,2},{1,5},{3,7},{5,1},{7,3},{8,12},{10,14},{12... | collective-permute-start | bytes 516104 | tf_op jit(solution)/shard_map/ppermute | solution.py:13
  36.7 6.8 %collective-permute-start.13 = (bf16[24,1792]{1,0:T(8,128)(2,1)S(1)}, bf16[24,1792]{1,0:T(8,128)(2,1)S(1)}, u32[]{:S(2)}, u32[]{:S(2)}) collective-permute-start(bf16[24,1792]{1,0:T(8,128)(2,1)S(1)} %get-tuple-element.61), channel_id=1, source_target_pairs={{0,24},{8,16},{16,8},{24,0},{1,25},{9,17},{17,9},{25,1},{2,26},{10... | collective-permute-start | bytes 258056 | tf_op jit(solution)/shard_map/ppermute | solution.py:13
  38.8 7.3 %collective-permute-start.14 = (bf16[24,1792]{1,0:T(8,128)(2,1)S(1)}, bf16[24,1792]{1,0:T(8,128)(2,1)S(1)}, u32[]{:S(2)}, u32[]{:S(2)}) collective-permute-start(bf16[24,1792]{1,0:T(8,128)(2,1)S(1)} %get-tuple-element.62), channel_id=1, source_target_pairs={{0,16},{8,24},{16,0},{24,8},{1,17},{9,25},{17,1},{25,9},{2,18},{10... | collective-permute-start | bytes 258056 | tf_op jit(solution)/shard_map/ppermute | solution.py:13
  39.9 6.3 %collective-permute-start.17 = (bf16[24,1792]{1,0:T(8,128)(2,1)S(1)}, bf16[24,1792]{1,0:T(8,128)(2,1)S(1)}, u32[]{:S(2)}, u32[]{:S(2)}) collective-permute-start(bf16[24,1792]{1,0:T(8,128)(2,1)S(1)} %get-tuple-element.49), channel_id=1, source_target_pairs={{0,6},{2,4},{4,2},{6,0},{1,7},{3,5},{5,3},{7,1},{8,14},{10,12},{12... | collective-permute-start | bytes 258056 | tf_op jit(solution)/shard_map/ppermute | solution.py:13
  41.4 4.8 %collective-permute-start.18 = (bf16[24,1792]{1,0:T(8,128)(2,1)S(1)}, bf16[24,1792]{1,0:T(8,128)(2,1)S(1)}, u32[]{:S(2)}, u32[]{:S(2)}) collective-permute-start(bf16[24,1792]{1,0:T(8,128)(2,1)S(1)} %get-tuple-element.50), channel_id=1, source_target_pairs={{0,2},{2,0},{4,6},{6,4},{1,3},{3,1},{5,7},{7,5},{8,10},{10,8},{12,... | collective-permute-start | bytes 258056 | tf_op jit(solution)/shard_map/ppermute | solution.py:13
  41.9 4.5 %collective-permute-start.19 = (bf16[24,1792]{1,0:T(8,128)(2,1)S(1)}, bf16[24,1792]{1,0:T(8,128)(2,1)S(1)}, u32[]{:S(2)}, u32[]{:S(2)}) collective-permute-start(bf16[24,1792]{1,0:T(8,128)(2,1)S(1)} %get-tuple-element.51), channel_id=1, source_target_pairs={{0,4},{2,6},{4,0},{6,2},{1,5},{3,7},{5,1},{7,3},{8,12},{10,14},{12... | collective-permute-start | bytes 258056 | tf_op jit(solution)/shard_map/ppermute | solution.py:13

commit v9 on v7

--- a/solution.py
+++ b/solution.py
@@ -207,12 +207,12 @@
     others = exchanged([fewer if j == local_count - 1 else joined for j in gather_order], gather_order)
     out_own = complete((everything, part_own, swap(part_own, "cuts", 1)))
     direct = swap(after(opposite, *arrived.values()), "node", far[-1])
-    near_state = begin(after(near, out_own))
+    near_state = begin(near)
     out_near = complete(near_state)
     others[1] = after(others[1], near_state[1])
     others[2] = after(others[2], out_near)
     by_partner = [joined] + [others[gather_order.index(j)] for j in range(1, local_count)] + [direct]
-    state = begin(jnp.concatenate(by_partner, axis=0))
+    state = begin(after(jnp.concatenate(by_partner, axis=0), out_own))
     near_back = swap(out_near, "node", 1)
     out_far = complete(state, out_near)
     blocks = split(out_far)
@@ -233,11 +233,8 @@
     out_own = after(out_own, *done)
     mine, *blocks = merge(rows, gather_order, out_own, near_back, direct_back)
     later = exchanged(blocks, gather_order)
-    *back, last = back
-    total = summed([*back, mine])
-    total, *later = lax.optimization_barrier((total, *later))
-    total, last = lax.optimization_barrier((total + summed(later), last))
-    return (total + last.astype(jnp.float32)).astype(jnp.bfloat16)
+    total, *later = lax.optimization_barrier((summed(back), *later))
+    return (total + summed([mine, *later])).astype(jnp.bfloat16)
 
 
 def slots_on_device(tokens, expert_ids, affinity, w_gate, w_up, w_down):

time: 47.3 us -> 47.3 us (level)
  transfers between devices with their start and end apart: 20 -> 20, of which waited for: 14 -> 13; matrix products, arithmetic and copies ran while one was open for 1% -> 0% of each run, Pallas kernels for 11% -> 11%
where the time goes in v9:
time: 47.3 us; the launch traced here: 47.1 us
  starting transfers between devices  22.1 us (47%)
  waiting for transfers between devices  17 us (36%)
  Pallas kernels  6.95 us (15%)
  other arithmetic  0.8 us (2%)
    ppermute x20, starting transfers between devices, swap(): return lax.ppermute(value, axis, [(i, i ^ bits) for i in range(size)])  22.1 us
    ppermute x20, waiting for transfers between devices, swap(): return lax.ppermute(value, axis, [(i, i ^ bits) for i in range(size)])  17 us
    pallas_call x6, Pallas kernels, in_vmem(): pl.pallas_call(body, out_shape=out_shapes, in_specs=[pl.BlockSpec(memory_...  3.29 us
    pallas_call x1, Pallas kernels, load_and_project(): pl.pallas_call(body, out_shape=(shape(count, 2 * hid), *(shape(*w.shape)...  2.63 us
    pallas_call x1, Pallas kernels, prepare(): pl.pallas_call(body, out_shape=(shape(tok_count, width + LANES), *[shape(...  1.03 us
  transfers between devices with their start and end apart: 20, of which 13 were waited for; matrix products, arithmetic and copies ran while one was open for 0% of the time, Pallas kernels for 11%

profile of v9, /device:TPU:0, one launch (start us, length us, event | category | flops | bytes accessed | tf_op | source)
XLA Modules:
  0.0 47.1 jit_solution(17185341635931857501)
XLA Ops:
  0.0 1.0 %shard_map.64 = (bf16[96,1920]{1,0:T(8,128)(2,1)S(1)}, bf16[24,1920]{1,0:T(8,128)(2,1)S(1)}, bf16[24,1920]{1,0:T(8,128)(2,1)S(1)}) custom-call(bf16[96,1792]{1,0:T(8,128)(2,1)} %tokens_hbm.1, s32[8,96]{1,0:T(8,128)} %bitcast.8, f32[8,96]{1,0:T(8,128)} %bitcast.9), custom_call_target="tpu_custom_call" | custom-call | flops 1000000 | bytes 1048576 | tf_op jit(solution)/shard_map/pallas_call | solution.py:73
  1.0 5.1 %collective-permute-start = (bf16[24,1920]{1,0:T(8,128)(2,1)S(1)}, bf16[24,1920]{1,0:T(8,128)(2,1)S(1)}, u32[]{:S(2)}, u32[]{:S(2)}) collective-permute-start(bf16[24,1920]{1,0:T(8,128)(2,1)S(1)} %get-tuple-element.31), channel_id=1, source_target_pairs={{0,24},{8,16},{16,8},{24,0},{1,25},{9,17},{17,9},{25,1},{2,26},{10... | collective-permute-start | bytes 276488 | tf_op jit(solution)/shard_map/ppermute | solution.py:13
  6.2 0.6 %collective-permute-start.3 = (bf16[96,1920]{1,0:T(8,128)(2,1)S(1)}, bf16[96,1920]{1,0:T(8,128)(2,1)S(1)}, u32[]{:S(2)}, u32[]{:S(2)}) collective-permute-start(bf16[96,1920]{1,0:T(8,128)(2,1)S(1)} %get-tuple-element.32.x_ref), channel_id=1, source_target_pairs={{0,8},{8,0},{16,24},{24,16},{1,9},{9,1},{17,25},{25,17},{2,10},{10... | collective-permute-start | bytes 1105928 | tf_op jit(solution)/shard_map/ppermute | solution.py:13
  6.8 2.6 %shard_map.65 = (bf16[96,1024]{1,0:T(8,128)(2,1)S(1)}, bf16[1792,512]{1,0:T(8,128)(2,1)S(1)}, bf16[1792,512]{1,0:T(8,128)(2,1)S(1)}, bf16[512,1792]{1,0:T(8,128)(2,1)S(1)}) custom-call(bf16[96,1920]{1,0:T(8,128)(2,1)S(1)} %get-tuple-element.32.x_ref, bf16[1792,512]{1,0:T(8,128)(2,1)} %bitcast.5, bf16[1792,512]{1,0:T(8,128)(2,1)} %bitcast.6, ...), custom_call_target="tpu_custom_call" | custom-call | tf_op jit(solution)/shard_map/pallas_call | solution.py:119
  9.6 4.4 %collective-permute-done.1 = bf16[24,1920]{1,0:T(8,128)(2,1)S(1)} collective-permute-done((bf16[24,1920]{1,0:T(8,128)(2,1)S(1)}, bf16[24,1920]{1,0:T(8,128)(2,1)S(1)}, u32[]{:S(2)}, u32[]{:S(2)}) %collective-permute-start.1) | collective-permute-done | bytes 92192 | tf_op jit(solution)/shard_map/ppermute | solution.py:13
  14.0 1.6 %collective-permute-start.2 = (bf16[48,1920]{1,0:T(8,128)(2,1)S(1)}, bf16[48,1920]{1,0:T(8,128)(2,1)S(1)}, u32[]{:S(2)}, u32[]{:S(2)}) collective-permute-start(bf16[48,1920]{1,0:T(8,128)(2,1)S(1)} %get-tuple-element.63), channel_id=1, source_target_pairs={{0,2},{2,0},{4,6},{6,4},{1,3},{3,1},{5,7},{7,5},{8,10},{10,8},{12,... | collective-permute-start | bytes 552968 | tf_op jit(solution)/shard_map/ppermute | solution.py:13
  15.6 1.5 %collective-permute-start.4 = (bf16[48,1920]{1,0:T(8,128)(2,1)S(1)}, bf16[48,1920]{1,0:T(8,128)(2,1)S(1)}, u32[]{:S(2)}, u32[]{:S(2)}) collective-permute-start(bf16[48,1920]{1,0:T(8,128)(2,1)S(1)} %get-tuple-element.63), channel_id=1, source_target_pairs={{0,4},{2,6},{4,0},{6,2},{1,5},{3,7},{5,1},{7,3},{8,12},{10,14},{12... | collective-permute-start | bytes 552968 | tf_op jit(solution)/shard_map/ppermute | solution.py:13
  17.1 0.5 %collective-permute-start.6 = (bf16[24,1920]{1,0:T(8,128)(2,1)S(1)}, bf16[24,1920]{1,0:T(8,128)(2,1)S(1)}, u32[]{:S(2)}, u32[]{:S(2)}) collective-permute-start(bf16[24,1920]{1,0:T(8,128)(2,1)S(1)} %collective-permute-done), channel_id=1, source_target_pairs={{0,6},{2,4},{4,2},{6,0},{1,7},{3,5},{5,3},{7,1},{8,14},{10,12},{12... | collective-permute-start | bytes 276488 | tf_op jit(solution)/shard_map/ppermute | solution.py:13
  17.6 0.6 %collective-permute-start.7 = (bf16[24,1920]{1,0:T(8,128)(2,1)S(1)}, bf16[24,1920]{1,0:T(8,128)(2,1)S(1)}, u32[]{:S(2)}, u32[]{:S(2)}) collective-permute-start(bf16[24,1920]{1,0:T(8,128)(2,1)S(1)} %get-tuple-element.41), channel_id=1, source_target_pairs={{0,16},{8,24},{16,0},{24,8},{1,17},{9,25},{17,1},{25,9},{2,18},{10... | collective-permute-start | bytes 276488 | tf_op jit(solution)/shard_map/ppermute | solution.py:13
  18.2 0.5 %shard_map.68.own_ref = bf16[96,1792]{1,0:T(8,128)(2,1)S(1)} custom-call(bf16[96,1920]{1,0:T(8,128)(2,1)S(1)} %get-tuple-element.32.x_ref, bf16[96,1024]{1,0:T(8,128)(2,1)S(1)} %get-tuple-element.33.part_ref, bf16[96,1024]{1,0:T(8,128)(2,1)S(1)} %collective-permute-done.8.other_ref, bf16[512,1792]{1,0:T(8,128)(2,1)S(1)} %get-tuple-element.38.down_ref), custom_call_target="tpu_custom_call" | custom-call | flops 176160768 | bytes 1048576 | tf_op jit(solution)/shard_map/pallas_call | solution.py:22
  19.0 0.7 %shard_map.66.part_ref = bf16[96,1024]{1,0:T(8,128)(2,1)S(1)} custom-call(bf16[96,1920]{1,0:T(8,128)(2,1)S(1)} %collective-permute-done.3.x_ref, bf16[1792,512]{1,0:T(8,128)(2,1)S(1)} %get-tuple-element.35.gate_ref, bf16[1792,512]{1,0:T(8,128)(2,1)S(1)} %get-tuple-element.36.up_ref), custom_call_target="tpu_custom_call" | custom-call | flops 352321536 | bytes 1048576 | tf_op jit(solution)/shard_map/pallas_call | solution.py:22
  19.8 0.9 %collective-permute-done.2 = bf16[48,1920]{1,0:T(8,128)(2,1)S(1)} collective-permute-done((bf16[48,1920]{1,0:T(8,128)(2,1)S(1)}, bf16[48,1920]{1,0:T(8,128)(2,1)S(1)}, u32[]{:S(2)}, u32[]{:S(2)}) %collective-permute-start.2) | collective-permute-done | bytes 184352 | tf_op jit(solution)/shard_map/ppermute | solution.py:13
  20.7 0.5 %collective-permute-done.5.other_ref = bf16[96,1024]{1,0:T(8,128)(2,1)S(1)} collective-permute-done((bf16[96,1024]{1,0:T(8,128)(2,1)S(1)}, bf16[96,1024]{1,0:T(8,128)(2,1)S(1)}, u32[]{:S(2)}, u32[]{:S(2)}) %collective-permute-start.5) | collective-permute-done | bytes 196640 | tf_op jit(solution)/shard_map/ppermute | solution.py:13
  21.7 1.3 %collective-permute-done.4 = bf16[48,1920]{1,0:T(8,128)(2,1)S(1)} collective-permute-done((bf16[48,1920]{1,0:T(8,128)(2,1)S(1)}, bf16[48,1920]{1,0:T(8,128)(2,1)S(1)}, u32[]{:S(2)}, u32[]{:S(2)}) %collective-permute-start.4) | collective-permute-done | bytes 184352 | tf_op jit(solution)/shard_map/ppermute | solution.py:13
  23.1 0.6 %collective-permute-done.7 = bf16[24,1920]{1,0:T(8,128)(2,1)S(1)} collective-permute-done((bf16[24,1920]{1,0:T(8,128)(2,1)S(1)}, bf16[24,1920]{1,0:T(8,128)(2,1)S(1)}, u32[]{:S(2)}, u32[]{:S(2)}) %collective-permute-start.7) | collective-permute-done | bytes 92192 | tf_op jit(solution)/shard_map/ppermute | solution.py:13
  23.6 0.9 %shard_map.69.part_ref = bf16[192,1024]{1,0:T(8,128)(2,1)S(1)} custom-call(bf16[192,1920]{1,0:T(8,128)(2,1)S(1)} %constant_dynamic-update-slice_fusion.2.x_ref, bf16[1792,512]{1,0:T(8,128)(2,1)S(1)} %get-tuple-element.35.gate_ref, bf16[1792,512]{1,0:T(8,128)(2,1)S(1)} %get-tuple-element.36.up_ref), custom_call_target="tpu_custom_call" | custom-call | flops 704643072 | bytes 1048576 | tf_op jit(solution)/shard_map/pallas_call | solution.py:22
  24.6 0.8 %collective-permute-start.15 = (bf16[96,1792]{1,0:T(8,128)(2,1)S(1)}, bf16[96,1792]{1,0:T(8,128)(2,1)S(1)}, u32[]{:S(2)}, u32[]{:S(2)}) collective-permute-start(bf16[96,1792]{1,0:T(8,128)(2,1)S(1)} %shard_map.67), channel_id=1, source_target_pairs={{0,8},{8,0},{16,24},{24,16},{1,9},{9,1},{17,25},{25,17},{2,10},{10... | collective-permute-start | bytes 1032200 | tf_op jit(solution)/shard_map/ppermute | solution.py:13
  25.4 0.9 %collective-permute-done.9.other_ref = bf16[192,1024]{1,0:T(8,128)(2,1)S(1)} collective-permute-done((bf16[192,1024]{1,0:T(8,128)(2,1)S(1)}, bf16[192,1024]{1,0:T(8,128)(2,1)S(1)}, u32[]{:S(2)}, u32[]{:S(2)}) %collective-permute-start.9) | collective-permute-done | bytes 393248 | tf_op jit(solution)/shard_map/ppermute | solution.py:13
  26.3 0.6 %shard_map.70 = bf16[192,1792]{1,0:T(8,128)(2,1)S(1)} custom-call(bf16[192,1920]{1,0:T(8,128)(2,1)S(1)} %constant_dynamic-update-slice_fusion.2.x_ref, bf16[192,1024]{1,0:T(8,128)(2,1)S(1)} %shard_map.69.part_ref, bf16[192,1024]{1,0:T(8,128)(2,1)S(1)} %collective-permute-done.9.other_ref, bf16[512,1792]{1,0:T(8,128)(2,1)S(1)} %get-tuple-element.38.down_ref), custom_call_target="tpu_custom_call" | custom-call | flops 352321536 | bytes 1048576 | tf_op jit(solution)/shard_map/pallas_call | solution.py:22
  27.0 2.5 %collective-permute-start.10 = (bf16[24,1792]{1,0:T(8,128)(2,1)S(1)}, bf16[24,1792]{1,0:T(8,128)(2,1)S(1)}, u32[]{:S(2)}, u32[]{:S(2)}) collective-permute-start(bf16[24,1792]{1,0:T(8,128)(2,1)S(1)} %get-tuple-element.58), channel_id=1, source_target_pairs={{0,6},{2,4},{4,2},{6,0},{1,7},{3,5},{5,3},{7,1},{8,14},{10,12},{12... | collective-permute-start | bytes 258056 | tf_op jit(solution)/shard_map/ppermute | solution.py:13
  29.5 0.9 %collective-permute-start.16 = (bf16[24,1792]{1,0:T(8,128)(2,1)S(1)}, bf16[24,1792]{1,0:T(8,128)(2,1)S(1)}, u32[]{:S(2)}, u32[]{:S(2)}) collective-permute-start(bf16[24,1792]{1,0:T(8,128)(2,1)S(1)} %get-tuple-element.48), channel_id=1, source_target_pairs={{0,16},{8,24},{16,0},{24,8},{1,17},{9,25},{17,1},{25,9},{2,18},{10... | collective-permute-start | bytes 258056 | tf_op jit(solution)/shard_map/ppermute | solution.py:13
  30.4 0.5 %collective-permute-start.11 = (bf16[48,1792]{1,0:T(8,128)(2,1)S(1)}, bf16[48,1792]{1,0:T(8,128)(2,1)S(1)}, u32[]{:S(2)}, u32[]{:S(2)}) collective-permute-start(bf16[48,1792]{1,0:T(8,128)(2,1)S(1)} %get-tuple-element.60), channel_id=1, source_target_pairs={{0,2},{2,0},{4,6},{6,4},{1,3},{3,1},{5,7},{7,5},{8,10},{10,8},{12,... | collective-permute-start | bytes 516104 | tf_op jit(solution)/shard_map/ppermute | solution.py:13
  31.0 0.5 %collective-permute-start.12 = (bf16[48,1792]{1,0:T(8,128)(2,1)S(1)}, bf16[48,1792]{1,0:T(8,128)(2,1)S(1)}, u32[]{:S(2)}, u32[]{:S(2)}) collective-permute-start(bf16[48,1792]{1,0:T(8,128)(2,1)S(1)} %get-tuple-element.59), channel_id=1, source_target_pairs={{0,4},{2,6},{4,0},{6,2},{1,5},{3,7},{5,1},{7,3},{8,12},{10,14},{12... | collective-permute-start | bytes 516104 | tf_op jit(solution)/shard_map/ppermute | solution.py:13
  31.5 1.0 %collective-permute-done.10 = bf16[24,1792]{1,0:T(8,128)(2,1)S(1)} collective-permute-done((bf16[24,1792]{1,0:T(8,128)(2,1)S(1)}, bf16[24,1792]{1,0:T(8,128)(2,1)S(1)}, u32[]{:S(2)}, u32[]{:S(2)}) %collective-permute-start.10) | collective-permute-done | bytes 86048 | tf_op jit(solution)/shard_map/ppermute | solution.py:13
  32.6 3.8 %collective-permute-done.11 = bf16[48,1792]{1,0:T(8,128)(2,1)S(1)} collective-permute-done((bf16[48,1792]{1,0:T(8,128)(2,1)S(1)}, bf16[48,1792]{1,0:T(8,128)(2,1)S(1)}, u32[]{:S(2)}, u32[]{:S(2)}) %collective-permute-start.11) | collective-permute-done | bytes 172064 | tf_op jit(solution)/shard_map/ppermute | solution.py:13
  36.6 2.2 %collective-permute-start.13 = (bf16[24,1792]{1,0:T(8,128)(2,1)S(1)}, bf16[24,1792]{1,0:T(8,128)(2,1)S(1)}, u32[]{:S(2)}, u32[]{:S(2)}) collective-permute-start(bf16[24,1792]{1,0:T(8,128)(2,1)S(1)} %get-tuple-element.61), channel_id=1, source_target_pairs={{0,24},{8,16},{16,8},{24,0},{1,25},{9,17},{17,9},{25,1},{2,26},{10... | collective-permute-start | bytes 258056 | tf_op jit(solution)/shard_map/ppermute | solution.py:13
  38.8 1.0 %collective-permute-start.14 = (bf16[24,1792]{1,0:T(8,128)(2,1)S(1)}, bf16[24,1792]{1,0:T(8,128)(2,1)S(1)}, u32[]{:S(2)}, u32[]{:S(2)}) collective-permute-start(bf16[24,1792]{1,0:T(8,128)(2,1)S(1)} %get-tuple-element.62), channel_id=1, source_target_pairs={{0,16},{8,24},{16,0},{24,8},{1,17},{9,25},{17,1},{25,9},{2,18},{10... | collective-permute-start | bytes 258056 | tf_op jit(solution)/shard_map/ppermute | solution.py:13
  39.9 1.5 %collective-permute-start.17 = (bf16[24,1792]{1,0:T(8,128)(2,1)S(1)}, bf16[24,1792]{1,0:T(8,128)(2,1)S(1)}, u32[]{:S(2)}, u32[]{:S(2)}) collective-permute-start(bf16[24,1792]{1,0:T(8,128)(2,1)S(1)} %get-tuple-element.49), channel_id=1, source_target_pairs={{0,6},{2,4},{4,2},{6,0},{1,7},{3,5},{5,3},{7,1},{8,14},{10,12},{12... | collective-permute-start | bytes 258056 | tf_op jit(solution)/shard_map/ppermute | solution.py:13
  41.4 0.5 %collective-permute-start.18 = (bf16[24,1792]{1,0:T(8,128)(2,1)S(1)}, bf16[24,1792]{1,0:T(8,128)(2,1)S(1)}, u32[]{:S(2)}, u32[]{:S(2)}) collective-permute-start(bf16[24,1792]{1,0:T(8,128)(2,1)S(1)} %get-tuple-element.50), channel_id=1, source_target_pairs={{0,2},{2,0},{4,6},{6,4},{1,3},{3,1},{5,7},{7,5},{8,10},{10,8},{12,... | collective-permute-start | bytes 258056 | tf_op jit(solution)/shard_map/ppermute | solution.py:13
  41.9 1.5 %collective-permute-start.19 = (bf16[24,1792]{1,0:T(8,128)(2,1)S(1)}, bf16[24,1792]{1,0:T(8,128)(2,1)S(1)}, u32[]{:S(2)}, u32[]{:S(2)}) collective-permute-start(bf16[24,1792]{1,0:T(8,128)(2,1)S(1)} %get-tuple-element.51), channel_id=1, source_target_pairs={{0,4},{2,6},{4,0},{6,2},{1,5},{3,7},{5,1},{7,3},{8,12},{10,14},{12... | collective-permute-start | bytes 258056 | tf_op jit(solution)/shard_map/ppermute | solution.py:13
  43.5 2.7 %collective-permute-done.14 = bf16[24,1792]{1,0:T(8,128)(2,1)S(1)} collective-permute-done((bf16[24,1792]{1,0:T(8,128)(2,1)S(1)}, bf16[24,1792]{1,0:T(8,128)(2,1)S(1)}, u32[]{:S(2)}, u32[]{:S(2)}) %collective-permute-start.14) | collective-permute-done | bytes 86048 | tf_op jit(solution)/shard_map/ppermute | solution.py:13
  46.4 0.7 %add_convert_fusion = bf16[24,1792]{1,0:T(8,128)(2,1)} fusion(f32[24,1792]{1,0:T(8,128)S(1)} %convert_add_fusion, bf16[24,1792]{1,0:T(8,128)(2,1)S(1)} %collective-permute-done.19, bf16[24,1792]{1,0:T(8,128)(2,1)S(1)} %collective-permute-done.18, bf16[24,1792]{1,0:T(8,128)(2,1)S(1)} %collective-permute-done.17, bf16[24,1792]{1,0:T(8,128)(2,1)S(1)} %get-tuple-element.53), kind=kLoop, calls=%fused_computation | loop fusion | flops 387072 | bytes 602112 | tf_op jit(solution)/shard_map/convert_element_type | solution.py:237
  (28 shorter events, 1.9 us)
Async XLA Ops:
  1.0 8.6 %collective-permute-start = (bf16[24,1920]{1,0:T(8,128)(2,1)S(1)}, bf16[24,1920]{1,0:T(8,128)(2,1)S(1)}, u32[]{:S(2)}, u32[]{:S(2)}) collective-permute-start(bf16[24,1920]{1,0:T(8,128)(2,1)S(1)} %get-tuple-element.31), channel_id=1, source_target_pairs={{0,24},{8,16},{16,8},{24,0},{1,25},{9,17},{17,9},{25,1},{2,26},{10... | collective-permute-start | bytes 276488 | tf_op jit(solution)/shard_map/ppermute | solution.py:13
  6.2 7.8 %collective-permute-start.1 = (bf16[24,1920]{1,0:T(8,128)(2,1)S(1)}, bf16[24,1920]{1,0:T(8,128)(2,1)S(1)}, u32[]{:S(2)}, u32[]{:S(2)}) collective-permute-start(bf16[24,1920]{1,0:T(8,128)(2,1)S(1)} %get-tuple-element.31), channel_id=1, source_target_pairs={{0,16},{8,24},{16,0},{24,8},{1,17},{9,25},{17,1},{25,9},{2,18},{10... | collective-permute-start | bytes 276488 | tf_op jit(solution)/shard_map/ppermute | solution.py:13
  6.2 12.8 %collective-permute-start.3 = (bf16[96,1920]{1,0:T(8,128)(2,1)S(1)}, bf16[96,1920]{1,0:T(8,128)(2,1)S(1)}, u32[]{:S(2)}, u32[]{:S(2)}) collective-permute-start(bf16[96,1920]{1,0:T(8,128)(2,1)S(1)} %get-tuple-element.32.x_ref), channel_id=1, source_target_pairs={{0,8},{8,0},{16,24},{24,16},{1,9},{9,1},{17,25},{25,17},{2,10},{10... | collective-permute-start | bytes 1105928 | tf_op jit(solution)/shard_map/ppermute | solution.py:13
  9.4 8.1 %collective-permute-start.8 = (bf16[96,1024]{1,0:T(8,128)(2,1)S(1)}, bf16[96,1024]{1,0:T(8,128)(2,1)S(1)}, u32[]{:S(2)}, u32[]{:S(2)}) collective-permute-start(bf16[96,1024]{1,0:T(8,128)(2,1)S(1)} %get-tuple-element.33.part_ref), channel_id=1, source_target_pairs={{0,1},{1,0},{2,3},{3,2},{4,5},{5,4},{6,7},{7,6},{8,9},{9,8},{10,11... | collective-permute-start | bytes 589832 | tf_op jit(solution)/shard_map/ppermute | solution.py:13
  14.0 6.6 %collective-permute-start.2 = (bf16[48,1920]{1,0:T(8,128)(2,1)S(1)}, bf16[48,1920]{1,0:T(8,128)(2,1)S(1)}, u32[]{:S(2)}, u32[]{:S(2)}) collective-permute-start(bf16[48,1920]{1,0:T(8,128)(2,1)S(1)} %get-tuple-element.63), channel_id=1, source_target_pairs={{0,2},{2,0},{4,6},{6,4},{1,3},{3,1},{5,7},{7,5},{8,10},{10,8},{12,... | collective-permute-start | bytes 552968 | tf_op jit(solution)/shard_map/ppermute | solution.py:13
  15.6 7.4 %collective-permute-start.4 = (bf16[48,1920]{1,0:T(8,128)(2,1)S(1)}, bf16[48,1920]{1,0:T(8,128)(2,1)S(1)}, u32[]{:S(2)}, u32[]{:S(2)}) collective-permute-start(bf16[48,1920]{1,0:T(8,128)(2,1)S(1)} %get-tuple-element.63), channel_id=1, source_target_pairs={{0,4},{2,6},{4,0},{6,2},{1,5},{3,7},{5,1},{7,3},{8,12},{10,14},{12... | collective-permute-start | bytes 552968 | tf_op jit(solution)/shard_map/ppermute | solution.py:13
  17.1 6.0 %collective-permute-start.6 = (bf16[24,1920]{1,0:T(8,128)(2,1)S(1)}, bf16[24,1920]{1,0:T(8,128)(2,1)S(1)}, u32[]{:S(2)}, u32[]{:S(2)}) collective-permute-start(bf16[24,1920]{1,0:T(8,128)(2,1)S(1)} %collective-permute-done), channel_id=1, source_target_pairs={{0,6},{2,4},{4,2},{6,0},{1,7},{3,5},{5,3},{7,1},{8,14},{10,12},{12... | collective-permute-start | bytes 276488 | tf_op jit(solution)/shard_map/ppermute | solution.py:13
  17.6 6.0 %collective-permute-start.7 = (bf16[24,1920]{1,0:T(8,128)(2,1)S(1)}, bf16[24,1920]{1,0:T(8,128)(2,1)S(1)}, u32[]{:S(2)}, u32[]{:S(2)}) collective-permute-start(bf16[24,1920]{1,0:T(8,128)(2,1)S(1)} %get-tuple-element.41), channel_id=1, source_target_pairs={{0,16},{8,24},{16,0},{24,8},{1,17},{9,25},{17,1},{25,9},{2,18},{10... | collective-permute-start | bytes 276488 | tf_op jit(solution)/shard_map/ppermute | solution.py:13
  19.7 1.5 %collective-permute-start.5 = (bf16[96,1024]{1,0:T(8,128)(2,1)S(1)}, bf16[96,1024]{1,0:T(8,128)(2,1)S(1)}, u32[]{:S(2)}, u32[]{:S(2)}) collective-permute-start(bf16[96,1024]{1,0:T(8,128)(2,1)S(1)} %shard_map.66.part_ref), channel_id=1, source_target_pairs={{0,1},{1,0},{2,3},{3,2},{4,5},{5,4},{6,7},{7,6},{8,9},{9,8},{10,11... | collective-permute-start | bytes 589832 | tf_op jit(solution)/shard_map/ppermute | solution.py:13
  24.5 1.8 %collective-permute-start.9 = (bf16[192,1024]{1,0:T(8,128)(2,1)S(1)}, bf16[192,1024]{1,0:T(8,128)(2,1)S(1)}, u32[]{:S(2)}, u32[]{:S(2)}) collective-permute-start(bf16[192,1024]{1,0:T(8,128)(2,1)S(1)} %shard_map.69.part_ref), channel_id=1, source_target_pairs={{0,1},{1,0},{2,3},{3,2},{4,5},{5,4},{6,7},{7,6},{8,9},{9,8},{10,11... | collective-permute-start | bytes 1179656 | tf_op jit(solution)/shard_map/ppermute | solution.py:13
  24.6 15.2 %collective-permute-start.15 = (bf16[96,1792]{1,0:T(8,128)(2,1)S(1)}, bf16[96,1792]{1,0:T(8,128)(2,1)S(1)}, u32[]{:S(2)}, u32[]{:S(2)}) collective-permute-start(bf16[96,1792]{1,0:T(8,128)(2,1)S(1)} %shard_map.67), channel_id=1, source_target_pairs={{0,8},{8,0},{16,24},{24,16},{1,9},{9,1},{17,25},{25,17},{2,10},{10... | collective-permute-start | bytes 1032200 | tf_op jit(solution)/shard_map/ppermute | solution.py:13
  27.0 5.5 %collective-permute-start.10 = (bf16[24,1792]{1,0:T(8,128)(2,1)S(1)}, bf16[24,1792]{1,0:T(8,128)(2,1)S(1)}, u32[]{:S(2)}, u32[]{:S(2)}) collective-permute-start(bf16[24,1792]{1,0:T(8,128)(2,1)S(1)} %get-tuple-element.58), channel_id=1, source_target_pairs={{0,6},{2,4},{4,2},{6,0},{1,7},{3,5},{5,3},{7,1},{8,14},{10,12},{12... | collective-permute-start | bytes 258056 | tf_op jit(solution)/shard_map/ppermute | solution.py:13
  29.5 10.3 %collective-permute-start.16 = (bf16[24,1792]{1,0:T(8,128)(2,1)S(1)}, bf16[24,1792]{1,0:T(8,128)(2,1)S(1)}, u32[]{:S(2)}, u32[]{:S(2)}) collective-permute-start(bf16[24,1792]{1,0:T(8,128)(2,1)S(1)} %get-tuple-element.48), channel_id=1, source_target_pairs={{0,16},{8,24},{16,0},{24,8},{1,17},{9,25},{17,1},{25,9},{2,18},{10... | collective-permute-start | bytes 258056 | tf_op jit(solution)/shard_map/ppermute | solution.py:13
  30.4 5.9 %collective-permute-start.11 = (bf16[48,1792]{1,0:T(8,128)(2,1)S(1)}, bf16[48,1792]{1,0:T(8,128)(2,1)S(1)}, u32[]{:S(2)}, u32[]{:S(2)}) collective-permute-start(bf16[48,1792]{1,0:T(8,128)(2,1)S(1)} %get-tuple-element.60), channel_id=1, source_target_pairs={{0,2},{2,0},{4,6},{6,4},{1,3},{3,1},{5,7},{7,5},{8,10},{10,8},{12,... | collective-permute-start | bytes 516104 | tf_op jit(solution)/shard_map/ppermute | solution.py:13
  31.0 5.6 %collective-permute-start.12 = (bf16[48,1792]{1,0:T(8,128)(2,1)S(1)}, bf16[48,1792]{1,0:T(8,128)(2,1)S(1)}, u32[]{:S(2)}, u32[]{:S(2)}) collective-permute-start(bf16[48,1792]{1,0:T(8,128)(2,1)S(1)} %get-tuple-element.59), channel_id=1, source_target_pairs={{0,4},{2,6},{4,0},{6,2},{1,5},{3,7},{5,1},{7,3},{8,12},{10,14},{12... | collective-permute-start | bytes 516104 | tf_op jit(solution)/shard_map/ppermute | solution.py:13
  36.6 6.8 %collective-permute-start.13 = (bf16[24,1792]{1,0:T(8,128)(2,1)S(1)}, bf16[24,1792]{1,0:T(8,128)(2,1)S(1)}, u32[]{:S(2)}, u32[]{:S(2)}) collective-permute-start(bf16[24,1792]{1,0:T(8,128)(2,1)S(1)} %get-tuple-element.61), channel_id=1, source_target_pairs={{0,24},{8,16},{16,8},{24,0},{1,25},{9,17},{17,9},{25,1},{2,26},{10... | collective-permute-start | bytes 258056 | tf_op jit(solution)/shard_map/ppermute | solution.py:13
  38.8 7.3 %collective-permute-start.14 = (bf16[24,1792]{1,0:T(8,128)(2,1)S(1)}, bf16[24,1792]{1,0:T(8,128)(2,1)S(1)}, u32[]{:S(2)}, u32[]{:S(2)}) collective-permute-start(bf16[24,1792]{1,0:T(8,128)(2,1)S(1)} %get-tuple-element.62), channel_id=1, source_target_pairs={{0,16},{8,24},{16,0},{24,8},{1,17},{9,25},{17,1},{25,9},{2,18},{10... | collective-permute-start | bytes 258056 | tf_op jit(solution)/shard_map/ppermute | solution.py:13
  39.9 6.3 %collective-permute-start.17 = (bf16[24,1792]{1,0:T(8,128)(2,1)S(1)}, bf16[24,1792]{1,0:T(8,128)(2,1)S(1)}, u32[]{:S(2)}, u32[]{:S(2)}) collective-permute-start(bf16[24,1792]{1,0:T(8,128)(2,1)S(1)} %get-tuple-element.49), channel_id=1, source_target_pairs={{0,6},{2,4},{4,2},{6,0},{1,7},{3,5},{5,3},{7,1},{8,14},{10,12},{12... | collective-permute-start | bytes 258056 | tf_op jit(solution)/shard_map/ppermute | solution.py:13
  41.4 4.8 %collective-permute-start.18 = (bf16[24,1792]{1,0:T(8,128)(2,1)S(1)}, bf16[24,1792]{1,0:T(8,128)(2,1)S(1)}, u32[]{:S(2)}, u32[]{:S(2)}) collective-permute-start(bf16[24,1792]{1,0:T(8,128)(2,1)S(1)} %get-tuple-element.50), channel_id=1, source_target_pairs={{0,2},{2,0},{4,6},{6,4},{1,3},{3,1},{5,7},{7,5},{8,10},{10,8},{12,... | collective-permute-start | bytes 258056 | tf_op jit(solution)/shard_map/ppermute | solution.py:13
  41.9 4.5 %collective-permute-start.19 = (bf16[24,1792]{1,0:T(8,128)(2,1)S(1)}, bf16[24,1792]{1,0:T(8,128)(2,1)S(1)}, u32[]{:S(2)}, u32[]{:S(2)}) collective-permute-start(bf16[24,1792]{1,0:T(8,128)(2,1)S(1)} %get-tuple-element.51), channel_id=1, source_target_pairs={{0,4},{2,6},{4,0},{6,2},{1,5},{3,7},{5,1},{7,3},{8,12},{10,14},{12... | collective-permute-start | bytes 258056 | tf_op jit(solution)/shard_map/ppermute | solution.py:13
